TPU v7x, 32 devices: a whole 2x2x4 slice. The times are simulated.
32 devices in a mesh: req: 16 (over z, y, x), tp: 2 (over core).
Axes of the slice: x: 2, y: 2, z: 4, core: 2. Of those that a mesh axis runs over, the one named last changes fastest.
Arguments:
- hidden_in: bfloat16 [4, 64, 3072], P(None, 'req', 'tp'), may hold values from -6 to 6
- norm_gain: float32 [3072], replicated, may hold values from 0.1 to 1.9
- w_query: bfloat16 [3072, 2048], P(None, 'tp'), may hold values from -1 to 1
- w_key: bfloat16 [3072, 1024], P(None, 'tp'), may hold values from -1 to 1
- w_value: bfloat16 [3072, 1024], P(None, 'tp'), may hold values from -0.109375 to 0.109375
- w_out: bfloat16 [2048, 3072], P('tp'), may hold values from -0.125 to 0.125
- prompt_keys: bfloat16 [16, 512, 1024], P('req', None, 'tp'), may hold values from -100 to 100
- prompt_values: bfloat16 [16, 512, 1024], P('req', None, 'tp'), may hold values from -8 to 8
- gen_keys: bfloat16 [64, 64, 1024], P('req', None, 'tp'), may hold values from -9 to 9
- gen_values: bfloat16 [64, 64, 1024], P('req', None, 'tp'), may hold values from -8 to 8
- lengths: int32 [8], replicated, may hold values from 768 to 1024, as said below
- parents: int32 [4, 64], replicated, may hold values from 0 to 7
Outputs:
- attended: bfloat16 [4, 64, 3072], P(None, 'req', 'tp')
Inputs may be any that keep to these rules, and one draw needn't show every extreme that they name: `lengths`: one request has a prompt of exactly 1024 tokens.
All inputs are finite; a program needn't handle non-finite values.
Results may differ from a plain program's by a relative error of at most 0.028.
Values may be sent and summed in bfloat16 or wider, within the bound.
No kernel may reach another device: no remote copies, remote signals or barrier semaphores. Data moves between devices by JAX's collectives and lax.ppermute only.
A program may use at most 64 MiB of HBM per device.

v0:
```python
import functools
import math

import jax
import jax.numpy as jnp
from jax import lax
from jax.experimental import pallas as pl
from jax.experimental.pallas import tpu as pltpu
from jax.sharding import PartitionSpec as P

HD = 128
BEAMS = 8

norm_eps = 1e-05
masked_score = -1e30
rope_base = 500000.0


def quotient(x, size):
    return x >> (size.bit_length() - 1) if size & (size - 1) == 0 else x // size


def remainder(x, size):
    return x & (size - 1) if size & (size - 1) == 0 else x % size


def permute_by(value, axis, distance):
    pairs = [(source, source ^ distance) for source in range(lax.axis_size(axis))]
    return lax.ppermute(value, axis, pairs)


def across(value, beam_distance, tp_distance):
    req, tp = lax.axis_size("req"), lax.axis_size("tp")
    pairs = [
        (r * tp + t, (r ^ beam_distance) * tp + (t ^ tp_distance))
        for r in range(req)
        for t in range(tp)
    ]
    return lax.ppermute(value, ("req", "tp"), pairs)


def lay_out(pieces, gain, x_s, xn_ref, first):
    steps, own, part = pieces[0].shape
    rows = steps * own
    me_tp = lax.axis_index("tp")
    total = jnp.zeros((rows, HD), jnp.float32)
    for t, piece in enumerate(pieces):
        column = pl.multiple_of((me_tp ^ t) * part, HD)
        for s in range(steps):
            x_s[t, pl.ds(s * own, own), :] = piece[s].astype(jnp.float32)
        mine = x_s[t]
        xn_ref[pl.ds(first, rows), pl.ds(column, part)] = (
            mine * gain[:, pl.ds(column, part)]
        ).astype(jnp.bfloat16)
        mine = mine * mine
        for c in range(part // HD):
            total = total + mine[:, c * HD : (c + 1) * HD]
    mean = jnp.sum(total, axis=-1, keepdims=True) / (part * len(pieces))
    return lax.rsqrt(mean + norm_eps)


def rotate(x, cosine, sine):
    return (x * cosine + pltpu.roll(x, HD // 2, 1) * sine).astype(jnp.bfloat16)


def load_kernel(
    sizes,
    lengths,
    parents,
    gain,
    hidden,
    wq,
    wk,
    wv,
    pk,
    pv,
    gk,
    gv,
    *refs,
):
    steps, own, tp, kv, group, history = sizes
    pieces = refs[: tp - 1]
    (
        gain_ref,
        xn_ref,
        scale_ref,
        wq_ref,
        keys_ref,
        values_ref,
        cosine_ref,
        sine_ref,
        bias_ref,
        lengths_s,
        parents_s,
        hidden_s,
        x_s,
        wk_s,
        wv_s,
        sems,
    ) = refs[tp - 1 :]
    rows = steps * own
    blocks = pk.shape[0]
    half_len = blocks * history
    device = lax.axis_index("req")
    request = device // 2
    parity = device % 2

    small = [
        (gain, gain_ref),
        (hidden, hidden_s),
        (lengths, lengths_s),
        (parents, parents_s),
    ]
    large = []
    for source, target, parts in ((wk, wk_s, 2), (wv, wv_s, 2)):
        size = source.shape[0] // parts
        for n in range(parts):
            place = pl.ds(n * size, size)
            large.append((source.at[place], target.at[place]))
    for prompt, gen, target in ((pk, gk, keys_ref), (pv, gv, values_ref)):
        large.append((prompt, target.at[pl.ds(0, blocks)]))
        large.append((gen, target.at[pl.ds(blocks, own)]))
    size = wq.shape[0] // 4
    for n in range(4):
        place = pl.ds(n * size, size)
        large.append((wq.at[place, pl.ds(0, wq_ref.shape[1])], wq_ref.at[place]))
    copies = [
        pltpu.make_async_copy(source, target, sems.at[n])
        for n, (source, target) in enumerate(small + large)
    ]
    for copy in copies:
        copy.start()
    large = copies[len(small) :]
    for copy in copies[: len(small)]:
        copy.wait()

    scale = lay_out((hidden_s, *pieces), gain_ref, x_s, xn_ref, 0)
    scale_ref[...] = jnp.broadcast_to(scale, scale_ref.shape)

    length = lengths_s[request]
    row = lax.broadcasted_iota(jnp.int32, (rows, HD), 0)
    lane = lax.broadcasted_iota(jnp.int32, (rows, HD), 1)
    half_dim = HD // 2
    inverse = jnp.exp(
        remainder(lane, half_dim).astype(jnp.float32) * (-math.log(rope_base) / half_dim)
    )
    angle = (length + history + quotient(row, own)).astype(jnp.float32) * inverse
    sine = jnp.sin(angle)
    sine = jnp.where(lane < half_dim, -sine, sine)
    cosine = jnp.cos(angle)
    cosine_ref[...] = cosine
    sine_ref[...] = sine

    count = group * 2 * rows

    def parent_of(s, beam):
        out = jnp.zeros_like(beam)
        for j in range(BEAMS):
            out = jnp.where(beam == j, parents_s[s, request * BEAMS + j], out)
        return out

    row = remainder(lax.broadcasted_iota(jnp.int32, (count, HD), 0), 2 * rows)
    row_step = quotient(remainder(row, rows), own)
    row_parity = jnp.where(row < rows, parity, 1 - parity)
    beam = row_parity * own + remainder(row, own)
    ancestors = [None] * steps
    at = beam
    for s in reversed(range(steps)):
        if s < steps - 1:
            at = jnp.where(row_step > s, parent_of(s + 1, at), beam)
        ancestors[s] = jnp.where(row_step >= s, at, -1)
    origin = parent_of(0, at)
    lane = lax.broadcasted_iota(jnp.int32, (count, HD), 1)

    for c in range(half_len // HD):
        place = parity * half_len + c * HD + lane
        bias_ref[:, pl.ds(c * HD, HD)] = jnp.where(place < length, 0.0, masked_score)
    for c in range(own * history // HD):
        key_beam = parity * own + quotient(c * HD + lane, history)
        bias_ref[:, pl.ds(half_len + c * HD, HD)] = jnp.where(
            key_beam == origin, 0.0, masked_score
        )
    new_bias = jnp.full((count, HD), masked_score, jnp.float32)
    for s in range(steps):
        hit = (quotient(lane, own) == s) & (
            ancestors[s] == parity * own + remainder(lane, own)
        )
        new_bias = jnp.where(hit, 0.0, new_bias)
    bias_ref[:, pl.ds(half_len + own * history, HD)] = new_bias

    cosine = cosine * scale
    sine = sine * scale
    new = pl.ds(blocks + own, keys_ref.shape[0] - blocks - own)
    for first, w_s, target, finish in (
        (0, wk_s, keys_ref, lambda x: rotate(x, cosine, sine)),
        (2, wv_s, values_ref, lambda x: (x * scale).astype(jnp.bfloat16)),
    ):
        target[new] = jnp.zeros((HD // history, history, kv * HD), jnp.bfloat16)
        for copy in large[first : first + 2]:
            copy.wait()
        fresh = jnp.dot(xn_ref[...], w_s[...], preferred_element_type=jnp.float32)
        for g in range(kv):
            target[blocks + own, pl.ds(0, rows), pl.ds(g * HD, HD)] = finish(
                fresh[:, g * HD : (g + 1) * HD]
            )
    for copy in large[4:]:
        copy.wait()


def attend_kernel(
    sizes,
    gain_ref,
    xn_ref,
    scale_ref,
    wq_ref,
    keys_ref,
    values_ref,
    cosine_ref,
    sine_ref,
    bias_ref,
    wq,
    *refs,
):
    steps, own, tp, kv, group = sizes
    pieces = refs[:tp]
    kept_ref, kept_lse_ref, sent_ref, x_s, xn_s, wq_s, sems = refs[tp:]
    rows = steps * own
    heads = kv * group
    keys_count = keys_ref.shape[0] * keys_ref.shape[1]
    near = wq_ref.shape[1]
    copies = []
    if near < wq.shape[1]:
        size = group * HD
        for n in range((wq.shape[1] - near) // size):
            copies.append(
                pltpu.make_async_copy(
                    wq.at[:, pl.ds(near + n * size, size)], wq_s.at[n], sems.at[n]
                )
            )
    for copy in copies:
        copy.start()

    xn_s[pl.ds(0, rows), :] = xn_ref[...]
    scale = lay_out(pieces, gain_ref, x_s, xn_s, rows)
    scale = jnp.concatenate([scale_ref[...], jnp.broadcast_to(scale, (rows, HD))], axis=0)
    scale = scale * HD**-0.5
    cosine = jnp.concatenate([cosine_ref[...]] * 2, axis=0) * scale
    sine = jnp.concatenate([sine_ref[...]] * 2, axis=0) * scale

    def score(g):
        lower = g * group * HD
        if lower < near:
            w = wq_ref[:, pl.ds(lower, group * HD)]
        else:
            n = (lower - near) // (group * HD)
            copies[n].wait()
            w = wq_s[n]
        q = jnp.dot(xn_s[...], w, preferred_element_type=jnp.float32)
        q = jnp.concatenate(
            [rotate(q[:, j * HD : (j + 1) * HD], cosine, sine) for j in range(group)], axis=0
        )
        keys = keys_ref[:, :, pl.ds(g * HD, HD)].reshape(keys_count, HD)
        return (
            lax.dot_general(q, keys, (((1,), (1,)), ((), ())), preferred_element_type=jnp.float32)
            + bias_ref[...]
        )

    ones = jnp.ones((keys_count, HD), jnp.bfloat16)

    def mix(g, scores):
        most = scores[:, :HD]
        for c in range(1, keys_count // HD):
            most = jnp.maximum(most, scores[:, c * HD : (c + 1) * HD])
        top = jnp.max(most, axis=-1, keepdims=True)
        values = values_ref[:, :, pl.ds(g * HD, HD)].reshape(keys_count, HD)
        mixed = jnp.dot(
            jnp.exp(scores - top).astype(jnp.bfloat16),
            jnp.concatenate([values, ones], axis=1),
            preferred_element_type=jnp.float32,
        )
        return mixed, top

    results, scores = [], None
    for g in range(kv):
        after = score(g)
        if g > 0:
            results.append(mix(g - 1, scores))
        scores = after
    results.append(mix(kv - 1, scores))

    lane = lax.broadcasted_iota(jnp.int32, (rows, HD), 1)
    kept_lse = jnp.zeros((rows, HD), jnp.float32)
    sent_lse = jnp.zeros((rows, HD), jnp.float32)
    for g, (mixed, top) in enumerate(results):
        total = mixed[:, HD:]
        mixed = mixed[:, :HD] / total
        lse = top + jnp.log(total)
        for j in range(group):
            h = g * group + j
            lower = j * 2 * rows
            kept_ref[:, pl.ds(h * HD, HD)] = mixed[lower : lower + rows]
            sent_ref[:, pl.ds(h * HD, HD)] = mixed[lower + rows : lower + 2 * rows].astype(
                jnp.bfloat16
            )
            kept_lse = jnp.where(lane == h, lse[lower : lower + rows], kept_lse)
            sent_lse = jnp.where(
                remainder(lane, heads) == h, lse[lower + rows : lower + 2 * rows], sent_lse
            )
    kept_lse_ref[...] = kept_lse
    terms = jnp.zeros((rows, HD), jnp.float32)
    rest = sent_lse
    for n in range(3):
        term = rest.astype(jnp.bfloat16).astype(jnp.float32)
        terms = jnp.where(quotient(lane, heads) == n, term, terms)
        rest = rest - term
    sent_ref[:, pl.ds(heads * HD, HD)] = terms.astype(jnp.bfloat16)


def fetch_kernel(kept_lse_ref, w_out, kept_lse_out, w_out_ref, sems):
    copies = []
    tp = w_out_ref.shape[0]
    part = w_out_ref.shape[-1]
    me_tp = lax.axis_index("tp")
    for d in range(tp):
        place = pl.ds(pl.multiple_of((me_tp ^ d) * part, HD), part)
        copies.append(pltpu.make_async_copy(w_out.at[:, place], w_out_ref.at[d], sems.at[d]))
    for copy in copies:
        copy.start()
    kept_lse_out[...] = kept_lse_ref[...]
    for copy in copies:
        copy.wait()


def project_kernel(sizes, kept_ref, kept_lse_ref, got_ref, w_out_ref, *refs):
    steps, own, tp, heads, chunk = sizes
    outs = refs[:tp]
    (ctx_s,) = refs[tp:]
    part = outs[0].shape[-1]
    base = heads * HD
    lse_mine = kept_lse_ref[...]
    terms = got_ref[:, pl.ds(base, HD)].astype(jnp.float32)
    lse_got = terms + pltpu.roll(terms, HD - heads, 1) + pltpu.roll(terms, HD - 2 * heads, 1)
    top = jnp.maximum(lse_mine, lse_got)
    mine = jnp.exp(lse_mine - top)
    got = jnp.exp(lse_got - top)
    share = mine / (mine + got)
    for h in range(heads):
        cols = pl.ds(h * HD, HD)
        w = share[:, h : h + 1]
        ctx_s[:, cols] = (
            kept_ref[:, cols] * w + got_ref[:, cols].astype(jnp.float32) * (1.0 - w)
        ).astype(jnp.bfloat16)
    for d in list(range(1, tp)) + [0]:
        for lower in range(0, part, chunk):
            cols = pl.ds(lower, chunk)
            out = jnp.dot(ctx_s[...], w_out_ref[d, :, cols], preferred_element_type=jnp.float32)
            for s in range(steps):
                outs[d][s, :, cols] = out[s * own : (s + 1) * own].astype(outs[d].dtype)


def body(
    hidden_in,
    norm_gain,
    w_query,
    w_key,
    w_value,
    w_out,
    prompt_keys,
    prompt_values,
    gen_keys,
    gen_values,
    lengths,
    parents,
):
    steps, own, part = hidden_in.shape
    tp = lax.axis_size("tp")
    rows = steps * own
    width = w_query.shape[0]
    kv = w_key.shape[1] // HD
    group = w_query.shape[1] // w_key.shape[1]
    heads = kv * group
    history = gen_keys.shape[1]

    near_pieces = [across(hidden_in, 0, t) for t in range(1, tp)]
    far_pieces = [across(hidden_in, 1, t) for t in range(tp)]

    def in_hbm(x):
        return pltpu.with_memory_space_constraint(x, pltpu.HBM)

    vmem = pl.BlockSpec(memory_space=pltpu.VMEM)
    hbm = pl.BlockSpec(memory_space=pltpu.HBM)
    params = pltpu.CompilerParams(vmem_limit_bytes=16 * 2**20)
    f32, bf16 = jnp.float32, jnp.bfloat16
    blocks = prompt_keys.shape[1] // history
    cache = (blocks + own + HD // history, history, kv * HD)
    near = max(kv // 2, 1) * group * HD
    loaded = pl.pallas_call(
        functools.partial(load_kernel, (steps, own, tp, kv, group, history)),
        out_shape=(
            jax.ShapeDtypeStruct((1, width), f32),
            jax.ShapeDtypeStruct((rows, width), bf16),
            jax.ShapeDtypeStruct((rows, HD), f32),
            jax.ShapeDtypeStruct((width, near), bf16),
            jax.ShapeDtypeStruct(cache, bf16),
            jax.ShapeDtypeStruct(cache, bf16),
            jax.ShapeDtypeStruct((rows, HD), f32),
            jax.ShapeDtypeStruct((rows, HD), f32),
            jax.ShapeDtypeStruct((group * 2 * rows, cache[0] * history), f32),
        ),
        in_specs=[hbm] * 11 + [vmem] * (tp - 1),
        out_specs=(vmem,) * 9,
        scratch_shapes=[
            pltpu.SMEM(lengths.shape, jnp.int32),
            pltpu.SMEM(parents.shape, jnp.int32),
            pltpu.VMEM(hidden_in.shape, bf16),
            pltpu.VMEM((tp, rows, part), f32),
            pltpu.VMEM(w_key.shape, bf16),
            pltpu.VMEM(w_value.shape, bf16),
            pltpu.SemaphoreType.DMA((16,)),
        ],
        compiler_params=params,
        name="load",
    )(
        *(
            in_hbm(x)
            for x in (
                lengths,
                parents,
                norm_gain[None, :],
                hidden_in,
                w_query,
                w_key,
                w_value,
                prompt_keys.reshape(blocks, history, kv * HD),
                prompt_values.reshape(blocks, history, kv * HD),
                gen_keys,
                gen_values,
            )
        ),
        *near_pieces,
    )

    kept, kept_lse, sent = pl.pallas_call(
        functools.partial(attend_kernel, (steps, own, tp, kv, group)),
        out_shape=(
            jax.ShapeDtypeStruct((rows, heads * HD), f32),
            jax.ShapeDtypeStruct((rows, HD), f32),
            jax.ShapeDtypeStruct((rows, heads * HD + HD), bf16),
        ),
        in_specs=[vmem] * 9 + [hbm] + [vmem] * tp,
        out_specs=(vmem,) * 3,
        scratch_shapes=[
            pltpu.VMEM((tp, rows, part), f32),
            pltpu.VMEM((2 * rows, width), bf16),
            pltpu.VMEM((kv, width, group * HD), bf16),
            pltpu.SemaphoreType.DMA((kv,)),
        ],
        compiler_params=params,
        name="attend",
    )(*loaded, in_hbm(w_query), *far_pieces)

    got = permute_by(sent, "req", 1)
    kept_lse, w_out_near = pl.pallas_call(
        fetch_kernel,
        out_shape=(
            jax.ShapeDtypeStruct((rows, HD), f32),
            jax.ShapeDtypeStruct((tp, heads * HD, part), bf16),
        ),
        in_specs=[vmem, hbm],
        out_specs=(vmem, vmem),
        scratch_shapes=[pltpu.SemaphoreType.DMA((tp,))],
        compiler_params=params,
        name="fetch",
    )(kept_lse, in_hbm(w_out))

    out_types = [f32] + [bf16] * (tp - 1)
    sums = pl.pallas_call(
        functools.partial(project_kernel, (steps, own, tp, heads, math.gcd(part, 512))),
        out_shape=tuple(jax.ShapeDtypeStruct((steps, own, part), kind) for kind in out_types),
        in_specs=[vmem] * 4,
        out_specs=(vmem,) * tp,
        scratch_shapes=[pltpu.VMEM((rows, heads * HD), bf16)],
        compiler_params=params,
        name="project",
    )(kept, kept_lse, got, w_out_near)
    total = sums[0]
    for t in range(1, tp):
        total = total + across(sums[t], 0, t).astype(f32)
    return total.astype(bf16)


def solution(mesh):
    in_specs = (
        P(None, "req", "tp"),
        P(),
        P(None, "tp"),
        P(None, "tp"),
        P(None, "tp"),
        P("tp", None),
        P("req", None, "tp"),
        P("req", None, "tp"),
        P("req", None, "tp"),
        P("req", None, "tp"),
        P(),
        P(),
    )
    out_specs = P(None, "req", "tp")
    return jax.shard_map(body, mesh=mesh, in_specs=in_specs, out_specs=out_specs, check_vma=False)
```

profile of v0, /device:TPU:0, one launch (start us, length us, event | category | flops | bytes accessed | tf_op | source)
XLA Modules:
  0.0 19.4 jit_solution(12438053638811720304)
XLA Ops:
  0.0 0.5 %collective-permute-start = (bf16[4,4,1536]{2,1,0:T(4,128)(2,1)}, bf16[4,4,1536]{2,1,0:T(4,128)(2,1)S(1)}, u32[]{:S(2)}, u32[]{:S(2)}) collective-permute-start(bf16[4,4,1536]{2,1,0:T(4,128)(2,1)} %hidden.1), channel_id=1, source_target_pairs={{0,1},{1,0},{2,3},{3,2},{4,5},{5,4},{6,7},{7,6},{8,9},{9,8},{10,11... | collective-permute-start | bytes 147464 | tf_op jit(solution)/shard_map/ppermute | solution.py:39
  0.5 2.6 %collective-permute-start.2 = (bf16[4,4,1536]{2,1,0:T(4,128)(2,1)}, bf16[4,4,1536]{2,1,0:T(4,128)(2,1)S(1)}, u32[]{:S(2)}, u32[]{:S(2)}) collective-permute-start(bf16[4,4,1536]{2,1,0:T(4,128)(2,1)} %hidden.1), channel_id=1, source_target_pairs={{0,3},{1,2},{2,1},{3,0},{4,7},{5,6},{6,5},{7,4},{8,11},{9,10},{10,... | collective-permute-start | bytes 147464 | tf_op jit(solution)/shard_map/ppermute | solution.py:39
  3.1 0.0 collective-permute-start.1
  3.1 0.0 collective-permute-done.refs_0_
  3.1 4.3 %load.1 = (f32[1,3072]{1,0:T(1,128)S(1)}, bf16[16,3072]{1,0:T(8,128)(2,1)S(1)}, f32[16,128]{1,0:T(8,128)S(1)}, bf16[3072,512]{1,0:T(8,128)(2,1)S(1)}, bf16[14,64...) custom-call(s32[8]{0:T(128)} %lengths.1, ...), custom_call_target="tpu_custom_call" | custom-call | tf_op jit(solution)/shard_map/load/pallas_call | solution.py:397
  7.4 0.0 collective-permute-done.2.refs_1_
  7.4 0.0 collective-permute-done.1.refs_0_
  7.4 4.0 %attend.1 = (f32[16,1024]{1,0:T(8,128)S(1)}, f32[16,128]{1,0:T(8,128)S(1)}, bf16[16,1152]{1,0:T(8,128)(2,1)S(1)}) custom-call(f32[1,3072]{1,0:T(1,128)S(1)} %get-tuple-element.21.gain_ref, bf16[16,3072]{1,0:T(8,128)(2,1)S(1)} %get-tuple-element.22.xn_ref, f32[16,128]{1,0:T(8,128)S(1)} %get-tuple-element.23.scale_ref, ...), custom_call_target="tpu_custom_call" | custom-call | tf_op jit(solution)/shard_map/attend/pallas_call | solution.py:443
  11.5 2.1 %collective-permute-start.3 = (bf16[16,1152]{1,0:T(8,128)(2,1)S(1)}, bf16[16,1152]{1,0:T(8,128)(2,1)S(1)}, u32[]{:S(2)}, u32[]{:S(2)}) collective-permute-start(bf16[16,1152]{1,0:T(8,128)(2,1)S(1)} %get-tuple-element.33), channel_id=1, source_target_pairs={{0,2},{2,0},{4,6},{6,4},{8,10},{10,8},{12,14},{14,12},{16,18},{18,... | collective-permute-start | bytes 110600 | tf_op jit(solution)/shard_map/ppermute | solution.py:29
  13.6 2.9 %fetch.1 = (f32[16,128]{1,0:T(8,128)S(1)}, bf16[2,1024,1536]{2,1,0:T(8,128)(2,1)S(1)}) custom-call(f32[16,128]{1,0:T(8,128)S(1)} %get-tuple-element.31.kept_lse_ref, bf16[1024,3072]{1,0:T(8,128)(2,1)} %w_out.1), custom_call_target="tpu_custom_call" | custom-call | tf_op jit(solution)/shard_map/fetch/pallas_call | solution.py:463
  16.4 0.0 collective-permute-done.3.got_ref
  16.4 1.1 %project.1 = (f32[4,4,1536]{2,1,0:T(4,128)S(1)}, bf16[4,4,1536]{2,1,0:T(4,128)(2,1)S(1)}) custom-call(f32[16,1024]{1,0:T(8,128)S(1)} %get-tuple-element.30.kept_ref, f32[16,128]{1,0:T(8,128)S(1)} %get-tuple-element.32.kept_lse_ref, bf16[16,1152]{1,0:T(8,128)(2,1)S(1)} %collective-permute-done.3.got_ref, bf16[2,1024,1536]{2,1,0:T(8,128)(2,1)S(1)} %get-tuple-element.34.w_out_ref), custom_call_target="tpu_custom_call" | custom-call | tf_op jit(solution)/shard_map/project/pallas_call | solution.py:477
  17.5 0.0 collective-permute-start.4
  17.5 1.2 %collective-permute-done.4 = bf16[4,4,1536]{2,1,0:T(4,128)(2,1)S(1)} collective-permute-done((bf16[4,4,1536]{2,1,0:T(4,128)(2,1)S(1)}, bf16[4,4,1536]{2,1,0:T(4,128)(2,1)S(1)}, u32[]{:S(2)}, u32[]{:S(2)}) %collective-permute-start.4) | collective-permute-done | bytes 49184 | tf_op jit(solution)/shard_map/ppermute | solution.py:39
  18.8 0.7 %add_convert_fusion = bf16[4,4,1536]{2,1,0:T(4,128)(2,1)} fusion(f32[4,4,1536]{2,1,0:T(4,128)S(1)} %get-tuple-element.35, bf16[4,4,1536]{2,1,0:T(4,128)(2,1)S(1)} %collective-permute-done.4), kind=kLoop, calls=%fused_computation | loop fusion | flops 73728 | bytes 196608 | tf_op jit(solution)/shard_map/convert_element_type | solution.py:489
Async XLA Ops:
  0.0 3.1 %collective-permute-start = (bf16[4,4,1536]{2,1,0:T(4,128)(2,1)}, bf16[4,4,1536]{2,1,0:T(4,128)(2,1)S(1)}, u32[]{:S(2)}, u32[]{:S(2)}) collective-permute-start(bf16[4,4,1536]{2,1,0:T(4,128)(2,1)} %hidden.1), channel_id=1, source_target_pairs={{0,1},{1,0},{2,3},{3,2},{4,5},{5,4},{6,7},{7,6},{8,9},{9,8},{10,11... | collective-permute-start | bytes 147464 | tf_op jit(solution)/shard_map/ppermute | solution.py:39
  0.5 7.0 %collective-permute-start.2 = (bf16[4,4,1536]{2,1,0:T(4,128)(2,1)}, bf16[4,4,1536]{2,1,0:T(4,128)(2,1)S(1)}, u32[]{:S(2)}, u32[]{:S(2)}) collective-permute-start(bf16[4,4,1536]{2,1,0:T(4,128)(2,1)} %hidden.1), channel_id=1, source_target_pairs={{0,3},{1,2},{2,1},{3,0},{4,7},{5,6},{6,5},{7,4},{8,11},{9,10},{10,... | collective-permute-start | bytes 147464 | tf_op jit(solution)/shard_map/ppermute | solution.py:39
  3.1 4.4 %collective-permute-start.1 = (bf16[4,4,1536]{2,1,0:T(4,128)(2,1)}, bf16[4,4,1536]{2,1,0:T(4,128)(2,1)S(1)}, u32[]{:S(2)}, u32[]{:S(2)}) collective-permute-start(bf16[4,4,1536]{2,1,0:T(4,128)(2,1)} %hidden.1), channel_id=1, source_target_pairs={{0,2},{1,3},{2,0},{3,1},{4,6},{5,7},{6,4},{7,5},{8,10},{9,11},{10,... | collective-permute-start | bytes 147464 | tf_op jit(solution)/shard_map/ppermute | solution.py:39
  11.5 5.0 %collective-permute-start.3 = (bf16[16,1152]{1,0:T(8,128)(2,1)S(1)}, bf16[16,1152]{1,0:T(8,128)(2,1)S(1)}, u32[]{:S(2)}, u32[]{:S(2)}) collective-permute-start(bf16[16,1152]{1,0:T(8,128)(2,1)S(1)} %get-tuple-element.33), channel_id=1, source_target_pairs={{0,2},{2,0},{4,6},{6,4},{8,10},{10,8},{12,14},{14,12},{16,18},{18,... | collective-permute-start | bytes 110600 | tf_op jit(solution)/shard_map/ppermute | solution.py:29
  17.5 1.2 %collective-permute-start.4 = (bf16[4,4,1536]{2,1,0:T(4,128)(2,1)S(1)}, bf16[4,4,1536]{2,1,0:T(4,128)(2,1)S(1)}, u32[]{:S(2)}, u32[]{:S(2)}) collective-permute-start(bf16[4,4,1536]{2,1,0:T(4,128)(2,1)S(1)} %get-tuple-element.36), channel_id=1, source_target_pairs={{0,1},{1,0},{2,3},{3,2},{4,5},{5,4},{6,7},{7,6},{8,9},{9,8},{10,11... | collective-permute-start | bytes 147464 | tf_op jit(solution)/shard_map/ppermute | solution.py:39
where the time goes:
time: 19.6 us; the launch traced here: 19.4 us
  Pallas kernels  12.3 us (63%)
  starting transfers between devices  5.14 us (26%)
  waiting for transfers between devices  1.25 us (6%)
  other arithmetic  0.65 us (3%)
    pallas_call x1, Pallas kernels, body(): pl.pallas_call(functools.partial(load_kernel, (steps, own, tp, kv, group,...  4.35 us
    pallas_call x1, Pallas kernels, body(): pl.pallas_call(functools.partial(attend_kernel, (steps, own, tp, kv, grou...  4.04 us
    ppermute x4, starting transfers between devices, across(): return lax.ppermute(value, ('req', 'tp'), pairs)  3.06 us
    pallas_call x1, Pallas kernels, body(): pl.pallas_call(fetch_kernel, out_shape=(jax.ShapeDtypeStruct((rows, HD),...  2.86 us
    ppermute x1, starting transfers between devices, permute_by(): return lax.ppermute(value, axis, pairs)  2.08 us
    ppermute x4, waiting for transfers between devices, across(): return lax.ppermute(value, ('req', 'tp'), pairs)  1.24 us
    pallas_call x1, Pallas kernels, body(): pl.pallas_call(functools.partial(project_kernel, (steps, own, tp, heads,...  1.08 us
    convert_element_type x1, other arithmetic, body(): return total.astype(bf16)  0.65 us
  transfers between devices with their start and end apart: 5, of which 1 were waited for; matrix products, arithmetic and copies ran while one was open for 0% of the time, Pallas kernels for 37%

commit v1 on v0

--- a/solution.py
+++ b/solution.py
@@ -78,7 +78,7 @@
     gv,
     *refs,
 ):
-    steps, own, tp, kv, group, history = sizes
+    steps, own, tp, kv, group, history, packed = sizes
     pieces = refs[: tp - 1]
     (
         gain_ref,
@@ -96,6 +96,7 @@
         x_s,
         wk_s,
         wv_s,
+        values_s,
         sems,
     ) = refs[tp - 1 :]
     rows = steps * own
@@ -111,15 +112,14 @@
         (lengths, lengths_s),
         (parents, parents_s),
     ]
-    large = []
+    old = blocks + own
+    large = [(pv, values_s.at[pl.ds(0, blocks)]), (gv, values_s.at[pl.ds(blocks, own)])]
     for source, target, parts in ((wk, wk_s, 2), (wv, wv_s, 2)):
         size = source.shape[0] // parts
         for n in range(parts):
             place = pl.ds(n * size, size)
             large.append((source.at[place], target.at[place]))
-    for prompt, gen, target in ((pk, gk, keys_ref), (pv, gv, values_ref)):
-        large.append((prompt, target.at[pl.ds(0, blocks)]))
-        large.append((gen, target.at[pl.ds(blocks, own)]))
+    large += [(pk, keys_ref.at[pl.ds(0, blocks)]), (gk, keys_ref.at[pl.ds(blocks, own)])]
     size = wq.shape[0] // 4
     for n in range(4):
         place = pl.ds(n * size, size)
@@ -138,20 +138,27 @@
     scale_ref[...] = jnp.broadcast_to(scale, scale_ref.shape)
 
     length = lengths_s[request]
+    half_dim = HD // 2
+    fall = -math.log(rope_base) / half_dim
+
+    def angles(step, place):
+        return (length + history + step).astype(jnp.float32) * jnp.exp(
+            place.astype(jnp.float32) * fall
+        )
+
     row = lax.broadcasted_iota(jnp.int32, (rows, HD), 0)
     lane = lax.broadcasted_iota(jnp.int32, (rows, HD), 1)
-    half_dim = HD // 2
-    inverse = jnp.exp(
-        remainder(lane, half_dim).astype(jnp.float32) * (-math.log(rope_base) / half_dim)
-    )
-    angle = (length + history + quotient(row, own)).astype(jnp.float32) * inverse
-    sine = jnp.sin(angle)
-    sine = jnp.where(lane < half_dim, -sine, sine)
-    cosine = jnp.cos(angle)
-    cosine_ref[...] = cosine
-    sine_ref[...] = sine
-
-    count = group * 2 * rows
+    angle = angles(quotient(row, own), remainder(lane, half_dim))
+    key_cosine = jnp.cos(angle) * scale
+    key_sine = jnp.sin(angle) * scale
+    key_sine = jnp.where(lane < half_dim, -key_sine, key_sine)
+
+    lanes = packed * group * 2 * rows
+    place = lax.broadcasted_iota(jnp.int32, (half_dim, lanes), 0)
+    lane = lax.broadcasted_iota(jnp.int32, (half_dim, lanes), 1)
+    angle = angles(quotient(remainder(lane, rows), own), place)
+    cosine_ref[...] = jnp.cos(angle)
+    sine_ref[...] = jnp.sin(angle)
 
     def parent_of(s, beam):
         out = jnp.zeros_like(beam)
@@ -159,7 +166,7 @@
             out = jnp.where(beam == j, parents_s[s, request * BEAMS + j], out)
         return out
 
-    row = remainder(lax.broadcasted_iota(jnp.int32, (count, HD), 0), 2 * rows)
+    row = remainder(lax.broadcasted_iota(jnp.int32, (8, lanes), 1), 2 * rows)
     row_step = quotient(remainder(row, rows), own)
     row_parity = jnp.where(row < rows, parity, 1 - parity)
     beam = row_parity * own + remainder(row, own)
@@ -170,40 +177,45 @@
             at = jnp.where(row_step > s, parent_of(s + 1, at), beam)
         ancestors[s] = jnp.where(row_step >= s, at, -1)
     origin = parent_of(0, at)
-    lane = lax.broadcasted_iota(jnp.int32, (count, HD), 1)
-
-    for c in range(half_len // HD):
-        place = parity * half_len + c * HD + lane
-        bias_ref[:, pl.ds(c * HD, HD)] = jnp.where(place < length, 0.0, masked_score)
-    for c in range(own * history // HD):
-        key_beam = parity * own + quotient(c * HD + lane, history)
-        bias_ref[:, pl.ds(half_len + c * HD, HD)] = jnp.where(
-            key_beam == origin, 0.0, masked_score
+
+    place = parity * half_len + lax.broadcasted_iota(jnp.int32, (half_len, lanes), 0)
+    bias_ref[pl.ds(0, half_len), :] = jnp.where(place < length, 0.0, masked_score)
+    for n in range(own):
+        seen = jnp.where(origin == parity * own + n, 0.0, masked_score)
+        for c in range(0, history, 8):
+            bias_ref[pl.ds(half_len + n * history + c, 8), :] = seen
+    sublane = lax.broadcasted_iota(jnp.int32, (8, lanes), 0)
+    for c in range(0, HD, 8):
+        seen = jnp.full((8, lanes), masked_score, jnp.float32)
+        for s in range(c // own, min((c + 8) // own, steps)):
+            hit = (quotient(c + sublane, own) == s) & (
+                ancestors[s] == parity * own + remainder(c + sublane, own)
+            )
+            seen = jnp.where(hit, 0.0, seen)
+        bias_ref[pl.ds(old * history + c, 8), :] = seen
+
+    for copy in large[:2]:
+        copy.wait()
+    values_ref[:, pl.ds(0, old * history)] = values_s[...].reshape(old * history, kv * HD).T
+    keys_ref[pl.ds(old, HD // history)] = jnp.zeros(
+        (HD // history, history, kv * HD), jnp.bfloat16
+    )
+    for copy in large[2:4]:
+        copy.wait()
+    fresh = jnp.dot(xn_ref[...], wk_s[...], preferred_element_type=jnp.float32)
+    for g in range(kv):
+        cols = pl.ds(g * HD, HD)
+        keys_ref[old, pl.ds(0, rows), cols] = rotate(
+            fresh[:, g * HD : (g + 1) * HD], key_cosine, key_sine
         )
-    new_bias = jnp.full((count, HD), masked_score, jnp.float32)
-    for s in range(steps):
-        hit = (quotient(lane, own) == s) & (
-            ancestors[s] == parity * own + remainder(lane, own)
-        )
-        new_bias = jnp.where(hit, 0.0, new_bias)
-    bias_ref[:, pl.ds(half_len + own * history, HD)] = new_bias
-
-    cosine = cosine * scale
-    sine = sine * scale
-    new = pl.ds(blocks + own, keys_ref.shape[0] - blocks - own)
-    for first, w_s, target, finish in (
-        (0, wk_s, keys_ref, lambda x: rotate(x, cosine, sine)),
-        (2, wv_s, values_ref, lambda x: (x * scale).astype(jnp.bfloat16)),
-    ):
-        target[new] = jnp.zeros((HD // history, history, kv * HD), jnp.bfloat16)
-        for copy in large[first : first + 2]:
-            copy.wait()
-        fresh = jnp.dot(xn_ref[...], w_s[...], preferred_element_type=jnp.float32)
-        for g in range(kv):
-            target[blocks + own, pl.ds(0, rows), pl.ds(g * HD, HD)] = finish(
-                fresh[:, g * HD : (g + 1) * HD]
-            )
-    for copy in large[4:]:
+    for copy in large[4:6]:
+        copy.wait()
+    fresh = jnp.dot(xn_ref[...], wv_s[...], preferred_element_type=jnp.float32) * scale
+    fresh = jnp.concatenate(
+        [fresh, jnp.zeros((HD - rows, kv * HD), jnp.float32)], axis=0
+    ).astype(jnp.bfloat16)
+    values_ref[:, pl.ds(old * history, HD)] = fresh.T
+    for copy in large[6:]:
         copy.wait()
 
 
@@ -221,22 +233,20 @@
     wq,
     *refs,
 ):
-    steps, own, tp, kv, group = sizes
+    steps, own, tp, kv, group, packed = sizes
     pieces = refs[:tp]
     kept_ref, kept_lse_ref, sent_ref, x_s, xn_s, wq_s, sems = refs[tp:]
     rows = steps * own
-    heads = kv * group
+    packs = kv // packed
     keys_count = keys_ref.shape[0] * keys_ref.shape[1]
     near = wq_ref.shape[1]
-    copies = []
-    if near < wq.shape[1]:
-        size = group * HD
-        for n in range((wq.shape[1] - near) // size):
-            copies.append(
-                pltpu.make_async_copy(
-                    wq.at[:, pl.ds(near + n * size, size)], wq_s.at[n], sems.at[n]
-                )
-            )
+    size = packed * group * HD
+    copies = [
+        pltpu.make_async_copy(
+            wq.at[:, pl.ds(near + n * size, size)], wq_s.at[n], sems.at[n]
+        )
+        for n in range((wq.shape[1] - near) // size)
+    ]
     for copy in copies:
         copy.start()
 
@@ -244,76 +254,80 @@
     scale = lay_out(pieces, gain_ref, x_s, xn_s, rows)
     scale = jnp.concatenate([scale_ref[...], jnp.broadcast_to(scale, (rows, HD))], axis=0)
     scale = scale * HD**-0.5
-    cosine = jnp.concatenate([cosine_ref[...]] * 2, axis=0) * scale
-    sine = jnp.concatenate([sine_ref[...]] * 2, axis=0) * scale
-
-    def score(g):
-        lower = g * group * HD
-        if lower < near:
-            w = wq_ref[:, pl.ds(lower, group * HD)]
+    lanes = size // HD * 2 * rows
+    lane = lax.broadcasted_iota(jnp.int32, (HD, lanes), 1)
+    owner = quotient(lane, group * 2 * rows)
+
+    def score(p):
+        if p * size < near:
+            w = wq_ref[:, pl.ds(p * size, size)]
         else:
-            n = (lower - near) // (group * HD)
+            n = p - near // size
             copies[n].wait()
             w = wq_s[n]
         q = jnp.dot(xn_s[...], w, preferred_element_type=jnp.float32)
         q = jnp.concatenate(
-            [rotate(q[:, j * HD : (j + 1) * HD], cosine, sine) for j in range(group)], axis=0
+            [q[:, j * HD : (j + 1) * HD] * scale for j in range(packed * group)], axis=0
+        ).T
+        cosine, sine = cosine_ref[...], sine_ref[...]
+        first, second = q[: HD // 2], q[HD // 2 :]
+        q = jnp.concatenate(
+            [first * cosine - second * sine, second * cosine + first * sine], axis=0
         )
-        keys = keys_ref[:, :, pl.ds(g * HD, HD)].reshape(keys_count, HD)
+        q = jnp.concatenate([jnp.where(owner == i, q, 0.0) for i in range(packed)], axis=0)
+        keys = keys_ref[:, :, pl.ds(p * packed * HD, packed * HD)]
         return (
-            lax.dot_general(q, keys, (((1,), (1,)), ((), ())), preferred_element_type=jnp.float32)
+            jnp.dot(
+                keys.reshape(keys_count, packed * HD),
+                q.astype(jnp.bfloat16),
+                preferred_element_type=jnp.float32,
+            )
             + bias_ref[...]
         )
 
-    ones = jnp.ones((keys_count, HD), jnp.bfloat16)
-
-    def mix(g, scores):
-        most = scores[:, :HD]
-        for c in range(1, keys_count // HD):
-            most = jnp.maximum(most, scores[:, c * HD : (c + 1) * HD])
-        top = jnp.max(most, axis=-1, keepdims=True)
-        values = values_ref[:, :, pl.ds(g * HD, HD)].reshape(keys_count, HD)
+    def mix(p, scores):
+        top = jnp.max(scores, axis=0, keepdims=True)
+        powers = jnp.exp(scores - top)
+        total = jnp.sum(powers, axis=0, keepdims=True)
         mixed = jnp.dot(
-            jnp.exp(scores - top).astype(jnp.bfloat16),
-            jnp.concatenate([values, ones], axis=1),
+            values_ref[pl.ds(p * packed * HD, packed * HD), :],
+            powers.astype(jnp.bfloat16),
             preferred_element_type=jnp.float32,
         )
-        return mixed, top
+        out = mixed[:HD]
+        for i in range(1, packed):
+            out = jnp.where(owner == i, mixed[i * HD : (i + 1) * HD], out)
+        out = (out * (1.0 / total)).T
+        for j in range(packed * group):
+            cols = pl.ds((p * packed * group + j) * HD, HD)
+            lower = j * 2 * rows
+            kept_ref[:, cols] = out[lower : lower + rows]
+            sent_ref[:, cols] = out[lower + rows : lower + 2 * rows].astype(jnp.bfloat16)
+        lse = top + jnp.log(total)
+        if lanes < HD:
+            lse = jnp.concatenate([lse, jnp.zeros((1, HD - lanes), jnp.float32)], axis=1)
+        return lse
 
     results, scores = [], None
-    for g in range(kv):
-        after = score(g)
-        if g > 0:
-            results.append(mix(g - 1, scores))
+    for p in range(packs):
+        after = score(p)
+        if p > 0:
+            results.append(mix(p - 1, scores))
         scores = after
-    results.append(mix(kv - 1, scores))
-
-    lane = lax.broadcasted_iota(jnp.int32, (rows, HD), 1)
+    results.append(mix(packs - 1, scores))
+
+    sublane = lax.broadcasted_iota(jnp.int32, (rows, HD), 0)
     kept_lse = jnp.zeros((rows, HD), jnp.float32)
-    sent_lse = jnp.zeros((rows, HD), jnp.float32)
-    for g, (mixed, top) in enumerate(results):
-        total = mixed[:, HD:]
-        mixed = mixed[:, :HD] / total
-        lse = top + jnp.log(total)
-        for j in range(group):
-            h = g * group + j
-            lower = j * 2 * rows
-            kept_ref[:, pl.ds(h * HD, HD)] = mixed[lower : lower + rows]
-            sent_ref[:, pl.ds(h * HD, HD)] = mixed[lower + rows : lower + 2 * rows].astype(
-                jnp.bfloat16
-            )
-            kept_lse = jnp.where(lane == h, lse[lower : lower + rows], kept_lse)
-            sent_lse = jnp.where(
-                remainder(lane, heads) == h, lse[lower + rows : lower + 2 * rows], sent_lse
-            )
+    terms = jnp.zeros((rows, HD), jnp.float32)
+    for p, lse in enumerate(results):
+        kept_lse = jnp.where(sublane == p, lse, kept_lse)
+        rest = lse
+        for n in range(3):
+            term = rest.astype(jnp.bfloat16).astype(jnp.float32)
+            terms = jnp.where(sublane == n * packs + p, term, terms)
+            rest = rest - term
     kept_lse_ref[...] = kept_lse
-    terms = jnp.zeros((rows, HD), jnp.float32)
-    rest = sent_lse
-    for n in range(3):
-        term = rest.astype(jnp.bfloat16).astype(jnp.float32)
-        terms = jnp.where(quotient(lane, heads) == n, term, terms)
-        rest = rest - term
-    sent_ref[:, pl.ds(heads * HD, HD)] = terms.astype(jnp.bfloat16)
+    sent_ref[:, pl.ds(kv * group * HD, HD)] = terms.astype(jnp.bfloat16)
 
 
 def fetch_kernel(kept_lse_ref, w_out, kept_lse_out, w_out_ref, sems):
@@ -332,21 +346,24 @@
 
 
 def project_kernel(sizes, kept_ref, kept_lse_ref, got_ref, w_out_ref, *refs):
-    steps, own, tp, heads, chunk = sizes
+    steps, own, tp, heads, packs, chunk = sizes
     outs = refs[:tp]
     (ctx_s,) = refs[tp:]
+    rows = steps * own
     part = outs[0].shape[-1]
     base = heads * HD
-    lse_mine = kept_lse_ref[...]
     terms = got_ref[:, pl.ds(base, HD)].astype(jnp.float32)
-    lse_got = terms + pltpu.roll(terms, HD - heads, 1) + pltpu.roll(terms, HD - 2 * heads, 1)
+    lse_got = sum(terms[n * packs : (n + 1) * packs] for n in range(3))
+    lse_got = pltpu.roll(jnp.concatenate([lse_got] * (8 // packs), axis=0), HD - rows, 1)
+    lse_mine = kept_lse_ref[pl.ds(0, 8), :]
     top = jnp.maximum(lse_mine, lse_got)
     mine = jnp.exp(lse_mine - top)
     got = jnp.exp(lse_got - top)
-    share = mine / (mine + got)
+    share = (mine / (mine + got)).T
     for h in range(heads):
         cols = pl.ds(h * HD, HD)
-        w = share[:, h : h + 1]
+        p, j = divmod(h, heads // packs)
+        w = share[j * 2 * rows : j * 2 * rows + rows, p : p + 1]
         ctx_s[:, cols] = (
             kept_ref[:, cols] * w + got_ref[:, cols].astype(jnp.float32) * (1.0 - w)
         ).astype(jnp.bfloat16)
@@ -393,19 +410,22 @@
     f32, bf16 = jnp.float32, jnp.bfloat16
     blocks = prompt_keys.shape[1] // history
     cache = (blocks + own + HD // history, history, kv * HD)
-    near = max(kv // 2, 1) * group * HD
+    packed = 2 - kv % 2
+    packs = kv // packed
+    near = max(packs // 2, 1) * packed * group * HD
+    lanes = packed * group * 2 * rows
     loaded = pl.pallas_call(
-        functools.partial(load_kernel, (steps, own, tp, kv, group, history)),
+        functools.partial(load_kernel, (steps, own, tp, kv, group, history, packed)),
         out_shape=(
             jax.ShapeDtypeStruct((1, width), f32),
             jax.ShapeDtypeStruct((rows, width), bf16),
             jax.ShapeDtypeStruct((rows, HD), f32),
             jax.ShapeDtypeStruct((width, near), bf16),
             jax.ShapeDtypeStruct(cache, bf16),
-            jax.ShapeDtypeStruct(cache, bf16),
-            jax.ShapeDtypeStruct((rows, HD), f32),
-            jax.ShapeDtypeStruct((rows, HD), f32),
-            jax.ShapeDtypeStruct((group * 2 * rows, cache[0] * history), f32),
+            jax.ShapeDtypeStruct((kv * HD, cache[0] * history), bf16),
+            jax.ShapeDtypeStruct((HD // 2, lanes), f32),
+            jax.ShapeDtypeStruct((HD // 2, lanes), f32),
+            jax.ShapeDtypeStruct((cache[0] * history, lanes), f32),
         ),
         in_specs=[hbm] * 11 + [vmem] * (tp - 1),
         out_specs=(vmem,) * 9,
@@ -416,6 +436,7 @@
             pltpu.VMEM((tp, rows, part), f32),
             pltpu.VMEM(w_key.shape, bf16),
             pltpu.VMEM(w_value.shape, bf16),
+            pltpu.VMEM((blocks + own, history, kv * HD), bf16),
             pltpu.SemaphoreType.DMA((16,)),
         ],
         compiler_params=params,
@@ -441,7 +462,7 @@
     )
 
     kept, kept_lse, sent = pl.pallas_call(
-        functools.partial(attend_kernel, (steps, own, tp, kv, group)),
+        functools.partial(attend_kernel, (steps, own, tp, kv, group, packed)),
         out_shape=(
             jax.ShapeDtypeStruct((rows, heads * HD), f32),
             jax.ShapeDtypeStruct((rows, HD), f32),
@@ -452,7 +473,7 @@
         scratch_shapes=[
             pltpu.VMEM((tp, rows, part), f32),
             pltpu.VMEM((2 * rows, width), bf16),
-            pltpu.VMEM((kv, width, group * HD), bf16),
+            pltpu.VMEM((packs, width, packed * group * HD), bf16),
             pltpu.SemaphoreType.DMA((kv,)),
         ],
         compiler_params=params,
@@ -475,7 +496,7 @@
 
     out_types = [f32] + [bf16] * (tp - 1)
     sums = pl.pallas_call(
-        functools.partial(project_kernel, (steps, own, tp, heads, math.gcd(part, 512))),
+        functools.partial(project_kernel, (steps, own, tp, heads, packs, math.gcd(part, 512))),
         out_shape=tuple(jax.ShapeDtypeStruct((steps, own, part), kind) for kind in out_types),
         in_specs=[vmem] * 4,
         out_specs=(vmem,) * tp,

time: 19.6 us -> 19.2 us (0.980)
  Pallas kernels: 12.3 us -> 11.9 us
    pallas_call x1, Pallas kernels: 4.04 us -> 3.55 us  [body(): pl.pallas_call(functools.partial(attend_kernel, (steps, own, tp, kv, grou...]
  transfers between devices with their start and end apart: 5 -> 5, of which waited for: 1 -> 1; matrix products, arithmetic and copies ran while one was open for 0% -> 0% of each run, Pallas kernels for 37% -> 38%
where the time goes in v1:
time: 19.2 us; the launch traced here: 19 us
  Pallas kernels  11.9 us (62%)
  starting transfers between devices  5.15 us (27%)
  waiting for transfers between devices  1.25 us (7%)
  other arithmetic  0.65 us (3%)
    pallas_call x1, Pallas kernels, body(): pl.pallas_call(functools.partial(load_kernel, (steps, own, tp, kv, group,...  4.35 us
    pallas_call x1, Pallas kernels, body(): pl.pallas_call(functools.partial(attend_kernel, (steps, own, tp, kv, grou...  3.55 us
    ppermute x4, starting transfers between devices, across(): return lax.ppermute(value, ('req', 'tp'), pairs)  3.06 us
    pallas_call x1, Pallas kernels, body(): pl.pallas_call(fetch_kernel, out_shape=(jax.ShapeDtypeStruct((rows, HD),...  2.86 us
    ppermute x1, starting transfers between devices, permute_by(): return lax.ppermute(value, axis, pairs)  2.09 us
    ppermute x4, waiting for transfers between devices, across(): return lax.ppermute(value, ('req', 'tp'), pairs)  1.24 us
    pallas_call x1, Pallas kernels, body(): pl.pallas_call(functools.partial(project_kernel, (steps, own, tp, heads,...  1.15 us
    convert_element_type x1, other arithmetic, body(): return total.astype(bf16)  0.65 us
  transfers between devices with their start and end apart: 5, of which 1 were waited for; matrix products, arithmetic and copies ran while one was open for 0% of the time, Pallas kernels for 38%

profile of v1, /device:TPU:0, one launch (start us, length us, event | category | flops | bytes accessed | tf_op | source)
XLA Modules:
  0.0 19.0 jit_solution(10952017424043244707)
XLA Ops:
  0.0 0.5 %collective-permute-start = (bf16[4,4,1536]{2,1,0:T(4,128)(2,1)}, bf16[4,4,1536]{2,1,0:T(4,128)(2,1)S(1)}, u32[]{:S(2)}, u32[]{:S(2)}) collective-permute-start(bf16[4,4,1536]{2,1,0:T(4,128)(2,1)} %hidden.1), channel_id=1, source_target_pairs={{0,1},{1,0},{2,3},{3,2},{4,5},{5,4},{6,7},{7,6},{8,9},{9,8},{10,11... | collective-permute-start | bytes 147464 | tf_op jit(solution)/shard_map/ppermute | solution.py:39
  0.5 2.6 %collective-permute-start.2 = (bf16[4,4,1536]{2,1,0:T(4,128)(2,1)}, bf16[4,4,1536]{2,1,0:T(4,128)(2,1)S(1)}, u32[]{:S(2)}, u32[]{:S(2)}) collective-permute-start(bf16[4,4,1536]{2,1,0:T(4,128)(2,1)} %hidden.1), channel_id=1, source_target_pairs={{0,3},{1,2},{2,1},{3,0},{4,7},{5,6},{6,5},{7,4},{8,11},{9,10},{10,... | collective-permute-start | bytes 147464 | tf_op jit(solution)/shard_map/ppermute | solution.py:39
  3.1 0.0 collective-permute-start.1
  3.1 0.0 collective-permute-done.refs_0_
  3.1 4.3 %load.1 = (f32[1,3072]{1,0:T(1,128)S(1)}, bf16[16,3072]{1,0:T(8,128)(2,1)S(1)}, f32[16,128]{1,0:T(8,128)S(1)}, bf16[3072,512]{1,0:T(8,128)(2,1)S(1)}, bf16[14,64...) custom-call(s32[8]{0:T(128)} %lengths.1, ...), custom_call_target="tpu_custom_call" | custom-call | tf_op jit(solution)/shard_map/load/pallas_call | solution.py:417
  7.4 0.0 collective-permute-done.2.refs_1_
  7.4 0.0 collective-permute-done.1.refs_0_
  7.4 3.6 %attend.1 = (f32[16,1024]{1,0:T(8,128)S(1)}, f32[16,128]{1,0:T(8,128)S(1)}, bf16[16,1152]{1,0:T(8,128)(2,1)S(1)}) custom-call(f32[1,3072]{1,0:T(1,128)S(1)} %get-tuple-element.21.gain_ref, bf16[16,3072]{1,0:T(8,128)(2,1)S(1)} %get-tuple-element.22.xn_ref, f32[16,128]{1,0:T(8,128)S(1)} %get-tuple-element.23.scale_ref, ...), custom_call_target="tpu_custom_call" | custom-call | tf_op jit(solution)/shard_map/attend/pallas_call | solution.py:464
  11.0 2.1 %collective-permute-start.3 = (bf16[16,1152]{1,0:T(8,128)(2,1)S(1)}, bf16[16,1152]{1,0:T(8,128)(2,1)S(1)}, u32[]{:S(2)}, u32[]{:S(2)}) collective-permute-start(bf16[16,1152]{1,0:T(8,128)(2,1)S(1)} %get-tuple-element.33), channel_id=1, source_target_pairs={{0,2},{2,0},{4,6},{6,4},{8,10},{10,8},{12,14},{14,12},{16,18},{18,... | collective-permute-start | bytes 110600 | tf_op jit(solution)/shard_map/ppermute | solution.py:29
  13.1 2.9 %fetch.1 = (f32[16,128]{1,0:T(8,128)S(1)}, bf16[2,1024,1536]{2,1,0:T(8,128)(2,1)S(1)}) custom-call(f32[16,128]{1,0:T(8,128)S(1)} %get-tuple-element.31.kept_lse_ref, bf16[1024,3072]{1,0:T(8,128)(2,1)} %w_out.1), custom_call_target="tpu_custom_call" | custom-call | tf_op jit(solution)/shard_map/fetch/pallas_call | solution.py:484
  16.0 0.0 collective-permute-done.3.got_ref
  16.0 1.2 %project.1 = (f32[4,4,1536]{2,1,0:T(4,128)S(1)}, bf16[4,4,1536]{2,1,0:T(4,128)(2,1)S(1)}) custom-call(f32[16,1024]{1,0:T(8,128)S(1)} %get-tuple-element.30.kept_ref, f32[16,128]{1,0:T(8,128)S(1)} %get-tuple-element.32.kept_lse_ref, bf16[16,1152]{1,0:T(8,128)(2,1)S(1)} %collective-permute-done.3.got_ref, bf16[2,1024,1536]{2,1,0:T(8,128)(2,1)S(1)} %get-tuple-element.34.w_out_ref), custom_call_target="tpu_custom_call" | custom-call | tf_op jit(solution)/shard_map/project/pallas_call | solution.py:498
  17.1 0.0 collective-permute-start.4
  17.1 1.2 %collective-permute-done.4 = bf16[4,4,1536]{2,1,0:T(4,128)(2,1)S(1)} collective-permute-done((bf16[4,4,1536]{2,1,0:T(4,128)(2,1)S(1)}, bf16[4,4,1536]{2,1,0:T(4,128)(2,1)S(1)}, u32[]{:S(2)}, u32[]{:S(2)}) %collective-permute-start.4) | collective-permute-done | bytes 49184 | tf_op jit(solution)/shard_map/ppermute | solution.py:39
  18.4 0.7 %add_convert_fusion = bf16[4,4,1536]{2,1,0:T(4,128)(2,1)} fusion(f32[4,4,1536]{2,1,0:T(4,128)S(1)} %get-tuple-element.35, bf16[4,4,1536]{2,1,0:T(4,128)(2,1)S(1)} %collective-permute-done.4), kind=kLoop, calls=%fused_computation | loop fusion | flops 73728 | bytes 196608 | tf_op jit(solution)/shard_map/convert_element_type | solution.py:510
Async XLA Ops:
  0.0 3.1 %collective-permute-start = (bf16[4,4,1536]{2,1,0:T(4,128)(2,1)}, bf16[4,4,1536]{2,1,0:T(4,128)(2,1)S(1)}, u32[]{:S(2)}, u32[]{:S(2)}) collective-permute-start(bf16[4,4,1536]{2,1,0:T(4,128)(2,1)} %hidden.1), channel_id=1, source_target_pairs={{0,1},{1,0},{2,3},{3,2},{4,5},{5,4},{6,7},{7,6},{8,9},{9,8},{10,11... | collective-permute-start | bytes 147464 | tf_op jit(solution)/shard_map/ppermute | solution.py:39
  0.5 7.0 %collective-permute-start.2 = (bf16[4,4,1536]{2,1,0:T(4,128)(2,1)}, bf16[4,4,1536]{2,1,0:T(4,128)(2,1)S(1)}, u32[]{:S(2)}, u32[]{:S(2)}) collective-permute-start(bf16[4,4,1536]{2,1,0:T(4,128)(2,1)} %hidden.1), channel_id=1, source_target_pairs={{0,3},{1,2},{2,1},{3,0},{4,7},{5,6},{6,5},{7,4},{8,11},{9,10},{10,... | collective-permute-start | bytes 147464 | tf_op jit(solution)/shard_map/ppermute | solution.py:39
  3.1 4.4 %collective-permute-start.1 = (bf16[4,4,1536]{2,1,0:T(4,128)(2,1)}, bf16[4,4,1536]{2,1,0:T(4,128)(2,1)S(1)}, u32[]{:S(2)}, u32[]{:S(2)}) collective-permute-start(bf16[4,4,1536]{2,1,0:T(4,128)(2,1)} %hidden.1), channel_id=1, source_target_pairs={{0,2},{1,3},{2,0},{3,1},{4,6},{5,7},{6,4},{7,5},{8,10},{9,11},{10,... | collective-permute-start | bytes 147464 | tf_op jit(solution)/shard_map/ppermute | solution.py:39
  11.0 5.0 %collective-permute-start.3 = (bf16[16,1152]{1,0:T(8,128)(2,1)S(1)}, bf16[16,1152]{1,0:T(8,128)(2,1)S(1)}, u32[]{:S(2)}, u32[]{:S(2)}) collective-permute-start(bf16[16,1152]{1,0:T(8,128)(2,1)S(1)} %get-tuple-element.33), channel_id=1, source_target_pairs={{0,2},{2,0},{4,6},{6,4},{8,10},{10,8},{12,14},{14,12},{16,18},{18,... | collective-permute-start | bytes 110600 | tf_op jit(solution)/shard_map/ppermute | solution.py:29
  17.1 1.2 %collective-permute-start.4 = (bf16[4,4,1536]{2,1,0:T(4,128)(2,1)S(1)}, bf16[4,4,1536]{2,1,0:T(4,128)(2,1)S(1)}, u32[]{:S(2)}, u32[]{:S(2)}) collective-permute-start(bf16[4,4,1536]{2,1,0:T(4,128)(2,1)S(1)} %get-tuple-element.36), channel_id=1, source_target_pairs={{0,1},{1,0},{2,3},{3,2},{4,5},{5,4},{6,7},{7,6},{8,9},{9,8},{10,11... | collective-permute-start | bytes 147464 | tf_op jit(solution)/shard_map/ppermute | solution.py:39

commit v2 on v1

--- a/solution.py
+++ b/solution.py
@@ -185,7 +185,7 @@
         for c in range(0, history, 8):
             bias_ref[pl.ds(half_len + n * history + c, 8), :] = seen
     sublane = lax.broadcasted_iota(jnp.int32, (8, lanes), 0)
-    for c in range(0, HD, 8):
+    for c in range(0, rows, 8):
         seen = jnp.full((8, lanes), masked_score, jnp.float32)
         for s in range(c // own, min((c + 8) // own, steps)):
             hit = (quotient(c + sublane, own) == s) & (
@@ -238,7 +238,8 @@
     kept_ref, kept_lse_ref, sent_ref, x_s, xn_s, wq_s, sems = refs[tp:]
     rows = steps * own
     packs = kv // packed
-    keys_count = keys_ref.shape[0] * keys_ref.shape[1]
+    keys_count = bias_ref.shape[0]
+    keys_space = values_ref.shape[1]
     near = wq_ref.shape[1]
     size = packed * group * HD
     copies = [
@@ -257,6 +258,7 @@
     lanes = size // HD * 2 * rows
     lane = lax.broadcasted_iota(jnp.int32, (HD, lanes), 1)
     owner = quotient(lane, group * 2 * rows)
+    pad = jnp.zeros((keys_space - keys_count, lanes), jnp.bfloat16)
 
     def score(p):
         if p * size < near:
@@ -278,7 +280,7 @@
         keys = keys_ref[:, :, pl.ds(p * packed * HD, packed * HD)]
         return (
             jnp.dot(
-                keys.reshape(keys_count, packed * HD),
+                keys.reshape(keys_space, packed * HD)[:keys_count],
                 q.astype(jnp.bfloat16),
                 preferred_element_type=jnp.float32,
             )
@@ -291,7 +293,7 @@
         total = jnp.sum(powers, axis=0, keepdims=True)
         mixed = jnp.dot(
             values_ref[pl.ds(p * packed * HD, packed * HD), :],
-            powers.astype(jnp.bfloat16),
+            jnp.concatenate([powers.astype(jnp.bfloat16), pad], axis=0),
             preferred_element_type=jnp.float32,
         )
         out = mixed[:HD]
@@ -308,13 +310,7 @@
             lse = jnp.concatenate([lse, jnp.zeros((1, HD - lanes), jnp.float32)], axis=1)
         return lse
 
-    results, scores = [], None
-    for p in range(packs):
-        after = score(p)
-        if p > 0:
-            results.append(mix(p - 1, scores))
-        scores = after
-    results.append(mix(packs - 1, scores))
+    results = [mix(p, score(p)) for p in range(packs)]
 
     sublane = lax.broadcasted_iota(jnp.int32, (rows, HD), 0)
     kept_lse = jnp.zeros((rows, HD), jnp.float32)
@@ -345,12 +341,23 @@
         copy.wait()
 
 
+def multiply_out(sizes, ctx, w_out_ref, d, out_ref):
+    steps, own, chunk = sizes
+    for lower in range(0, out_ref.shape[-1], chunk):
+        cols = pl.ds(lower, chunk)
+        out = jnp.dot(ctx, w_out_ref[d, :, cols], preferred_element_type=jnp.float32)
+        for s in range(steps):
+            out_ref[s, :, cols] = out[s * own : (s + 1) * own].astype(out_ref.dtype)
+
+
+def project_own_kernel(sizes, ctx_ref, w_out_ref, out_ref):
+    multiply_out(sizes, ctx_ref[...], w_out_ref, 0, out_ref)
+
+
 def project_kernel(sizes, kept_ref, kept_lse_ref, got_ref, w_out_ref, *refs):
     steps, own, tp, heads, packs, chunk = sizes
-    outs = refs[:tp]
-    (ctx_s,) = refs[tp:]
+    ctx_ref, outs = refs[0], refs[1:]
     rows = steps * own
-    part = outs[0].shape[-1]
     base = heads * HD
     terms = got_ref[:, pl.ds(base, HD)].astype(jnp.float32)
     lse_got = sum(terms[n * packs : (n + 1) * packs] for n in range(3))
@@ -364,15 +371,11 @@
         cols = pl.ds(h * HD, HD)
         p, j = divmod(h, heads // packs)
         w = share[j * 2 * rows : j * 2 * rows + rows, p : p + 1]
-        ctx_s[:, cols] = (
+        ctx_ref[:, cols] = (
             kept_ref[:, cols] * w + got_ref[:, cols].astype(jnp.float32) * (1.0 - w)
         ).astype(jnp.bfloat16)
-    for d in list(range(1, tp)) + [0]:
-        for lower in range(0, part, chunk):
-            cols = pl.ds(lower, chunk)
-            out = jnp.dot(ctx_s[...], w_out_ref[d, :, cols], preferred_element_type=jnp.float32)
-            for s in range(steps):
-                outs[d][s, :, cols] = out[s * own : (s + 1) * own].astype(outs[d].dtype)
+    for d in range(1, tp):
+        multiply_out((steps, own, chunk), ctx_ref[...], w_out_ref, d, outs[d - 1])
 
 
 def body(
@@ -425,7 +428,7 @@
             jax.ShapeDtypeStruct((kv * HD, cache[0] * history), bf16),
             jax.ShapeDtypeStruct((HD // 2, lanes), f32),
             jax.ShapeDtypeStruct((HD // 2, lanes), f32),
-            jax.ShapeDtypeStruct((cache[0] * history, lanes), f32),
+            jax.ShapeDtypeStruct(((blocks + own) * history + rows, lanes), f32),
         ),
         in_specs=[hbm] * 11 + [vmem] * (tp - 1),
         out_specs=(vmem,) * 9,
@@ -494,19 +497,29 @@
         name="fetch",
     )(kept_lse, in_hbm(w_out))
 
-    out_types = [f32] + [bf16] * (tp - 1)
-    sums = pl.pallas_call(
-        functools.partial(project_kernel, (steps, own, tp, heads, packs, math.gcd(part, 512))),
-        out_shape=tuple(jax.ShapeDtypeStruct((steps, own, part), kind) for kind in out_types),
+    chunk = math.gcd(part, 512)
+    ctx, *sums = pl.pallas_call(
+        functools.partial(project_kernel, (steps, own, tp, heads, packs, chunk)),
+        out_shape=(
+            jax.ShapeDtypeStruct((rows, heads * HD), bf16),
+            *[jax.ShapeDtypeStruct((steps, own, part), bf16)] * (tp - 1),
+        ),
         in_specs=[vmem] * 4,
         out_specs=(vmem,) * tp,
-        scratch_shapes=[pltpu.VMEM((rows, heads * HD), bf16)],
         compiler_params=params,
         name="project",
     )(kept, kept_lse, got, w_out_near)
-    total = sums[0]
-    for t in range(1, tp):
-        total = total + across(sums[t], 0, t).astype(f32)
+    sums = [across(x, 0, t + 1) for t, x in enumerate(sums)]
+    total = pl.pallas_call(
+        functools.partial(project_own_kernel, (steps, own, chunk)),
+        out_shape=jax.ShapeDtypeStruct((steps, own, part), f32),
+        in_specs=[vmem] * 2,
+        out_specs=vmem,
+        compiler_params=params,
+        name="project_own",
+    )(ctx, w_out_near)
+    for x in sums:
+        total = total + x.astype(f32)
     return total.astype(bf16)
 
 

time: 19.2 us -> 18.8 us (0.979)
  waiting for transfers between devices: 1.25 us -> 0.72 us
    ppermute x4, waiting for transfers between devices: 1.24 us -> 0.72 us  [across(): return lax.ppermute(value, ('req', 'tp'), pairs)]
    pallas_call x0 -> x1, Pallas kernels: none -> 0.53 us  [body(): pl.pallas_call(functools.partial(project_own_kernel, (steps, own, chunk))...]
    pallas_call x1, Pallas kernels: 1.15 us -> 0.75 us  [body(): pl.pallas_call(functools.partial(project_kernel, (steps, own, tp, heads,...]
  transfers between devices with their start and end apart: 5 -> 5, of which waited for: 1 -> 1; matrix products, arithmetic and copies ran while one was open for 0% -> 0% of each run, Pallas kernels for 38% -> 42%
where the time goes in v2:
time: 18.8 us; the launch traced here: 18.6 us
  Pallas kernels  12 us (64%)
  starting transfers between devices  5.15 us (27%)
  waiting for transfers between devices  0.72 us (4%)
  other arithmetic  0.65 us (3%)
    pallas_call x1, Pallas kernels, body(): pl.pallas_call(functools.partial(load_kernel, (steps, own, tp, kv, group,...  4.35 us
    pallas_call x1, Pallas kernels, body(): pl.pallas_call(functools.partial(attend_kernel, (steps, own, tp, kv, grou...  3.56 us
    ppermute x4, starting transfers between devices, across(): return lax.ppermute(value, ('req', 'tp'), pairs)  3.06 us
    pallas_call x1, Pallas kernels, body(): pl.pallas_call(fetch_kernel, out_shape=(jax.ShapeDtypeStruct((rows, HD),...  2.86 us
    ppermute x1, starting transfers between devices, permute_by(): return lax.ppermute(value, axis, pairs)  2.09 us
    pallas_call x1, Pallas kernels, body(): pl.pallas_call(functools.partial(project_kernel, (steps, own, tp, heads,...  0.75 us
    ppermute x4, waiting for transfers between devices, across(): return lax.ppermute(value, ('req', 'tp'), pairs)  0.72 us
    convert_element_type x1, other arithmetic, body(): return total.astype(bf16)  0.65 us
  transfers between devices with their start and end apart: 5, of which 1 were waited for; matrix products, arithmetic and copies ran while one was open for 0% of the time, Pallas kernels for 42%

profile of v2, /device:TPU:0, one launch (start us, length us, event | category | flops | bytes accessed | tf_op | source)
XLA Modules:
  0.0 18.6 jit_solution(10109311601205417410)
XLA Ops:
  0.0 0.5 %collective-permute-start = (bf16[4,4,1536]{2,1,0:T(4,128)(2,1)}, bf16[4,4,1536]{2,1,0:T(4,128)(2,1)S(1)}, u32[]{:S(2)}, u32[]{:S(2)}) collective-permute-start(bf16[4,4,1536]{2,1,0:T(4,128)(2,1)} %hidden.1), channel_id=1, source_target_pairs={{0,1},{1,0},{2,3},{3,2},{4,5},{5,4},{6,7},{7,6},{8,9},{9,8},{10,11... | collective-permute-start | bytes 147464 | tf_op jit(solution)/shard_map/ppermute | solution.py:39
  0.5 2.6 %collective-permute-start.2 = (bf16[4,4,1536]{2,1,0:T(4,128)(2,1)}, bf16[4,4,1536]{2,1,0:T(4,128)(2,1)S(1)}, u32[]{:S(2)}, u32[]{:S(2)}) collective-permute-start(bf16[4,4,1536]{2,1,0:T(4,128)(2,1)} %hidden.1), channel_id=1, source_target_pairs={{0,3},{1,2},{2,1},{3,0},{4,7},{5,6},{6,5},{7,4},{8,11},{9,10},{10,... | collective-permute-start | bytes 147464 | tf_op jit(solution)/shard_map/ppermute | solution.py:39
  3.1 0.0 collective-permute-start.1
  3.1 0.0 collective-permute-done.refs_0_
  3.1 4.3 %load.1 = (f32[1,3072]{1,0:T(1,128)S(1)}, bf16[16,3072]{1,0:T(8,128)(2,1)S(1)}, f32[16,128]{1,0:T(8,128)S(1)}, bf16[3072,512]{1,0:T(8,128)(2,1)S(1)}, bf16[14,64...) custom-call(s32[8]{0:T(128)} %lengths.1, ...), custom_call_target="tpu_custom_call" | custom-call | tf_op jit(solution)/shard_map/load/pallas_call | solution.py:420
  7.4 0.0 collective-permute-done.2.refs_1_
  7.4 0.0 collective-permute-done.1.refs_0_
  7.4 3.6 %attend.1 = (f32[16,1024]{1,0:T(8,128)S(1)}, f32[16,128]{1,0:T(8,128)S(1)}, bf16[16,1152]{1,0:T(8,128)(2,1)S(1)}) custom-call(f32[1,3072]{1,0:T(1,128)S(1)} %get-tuple-element.21.gain_ref, bf16[16,3072]{1,0:T(8,128)(2,1)S(1)} %get-tuple-element.22.xn_ref, f32[16,128]{1,0:T(8,128)S(1)} %get-tuple-element.23.scale_ref, ...), custom_call_target="tpu_custom_call" | custom-call | tf_op jit(solution)/shard_map/attend/pallas_call | solution.py:467
  11.0 2.1 %collective-permute-start.3 = (bf16[16,1152]{1,0:T(8,128)(2,1)S(1)}, bf16[16,1152]{1,0:T(8,128)(2,1)S(1)}, u32[]{:S(2)}, u32[]{:S(2)}) collective-permute-start(bf16[16,1152]{1,0:T(8,128)(2,1)S(1)} %get-tuple-element.33), channel_id=1, source_target_pairs={{0,2},{2,0},{4,6},{6,4},{8,10},{10,8},{12,14},{14,12},{16,18},{18,... | collective-permute-start | bytes 110600 | tf_op jit(solution)/shard_map/ppermute | solution.py:29
  13.1 2.9 %fetch.1 = (f32[16,128]{1,0:T(8,128)S(1)}, bf16[2,1024,1536]{2,1,0:T(8,128)(2,1)S(1)}) custom-call(f32[16,128]{1,0:T(8,128)S(1)} %get-tuple-element.31.kept_lse_ref, bf16[1024,3072]{1,0:T(8,128)(2,1)} %w_out.1), custom_call_target="tpu_custom_call" | custom-call | tf_op jit(solution)/shard_map/fetch/pallas_call | solution.py:487
  16.0 0.0 collective-permute-done.3.got_ref
  16.0 0.7 %project.1 = (bf16[16,1024]{1,0:T(8,128)(2,1)S(1)}, bf16[4,4,1536]{2,1,0:T(4,128)(2,1)S(1)}) custom-call(f32[16,1024]{1,0:T(8,128)S(1)} %get-tuple-element.30.kept_ref, f32[16,128]{1,0:T(8,128)S(1)} %get-tuple-element.32.kept_lse_ref, bf16[16,1152]{1,0:T(8,128)(2,1)S(1)} %collective-permute-done.3.got_ref, bf16[2,1024,1536]{2,1,0:T(8,128)(2,1)S(1)} %get-tuple-element.34.w_out_ref), custom_call_target="tpu_custom_call" | custom-call | tf_op jit(solution)/shard_map/project/pallas_call | solution.py:501
  16.7 0.0 collective-permute-start.4
  16.7 0.5 %project_own.1 = f32[4,4,1536]{2,1,0:T(4,128)S(1)} custom-call(bf16[16,1024]{1,0:T(8,128)(2,1)S(1)} %get-tuple-element.35.ctx_ref, bf16[2,1024,1536]{2,1,0:T(8,128)(2,1)S(1)} %get-tuple-element.34.w_out_ref), custom_call_target="tpu_custom_call" | custom-call | tf_op jit(solution)/shard_map/project_own/pallas_call | solution.py:513
  17.3 0.7 %collective-permute-done.4 = bf16[4,4,1536]{2,1,0:T(4,128)(2,1)S(1)} collective-permute-done((bf16[4,4,1536]{2,1,0:T(4,128)(2,1)S(1)}, bf16[4,4,1536]{2,1,0:T(4,128)(2,1)S(1)}, u32[]{:S(2)}, u32[]{:S(2)}) %collective-permute-start.4) | collective-permute-done | bytes 49184 | tf_op jit(solution)/shard_map/ppermute | solution.py:39
  18.0 0.6 %add_convert_fusion = bf16[4,4,1536]{2,1,0:T(4,128)(2,1)} fusion(f32[4,4,1536]{2,1,0:T(4,128)S(1)} %project_own.1, bf16[4,4,1536]{2,1,0:T(4,128)(2,1)S(1)} %collective-permute-done.4), kind=kLoop, calls=%fused_computation | loop fusion | flops 73728 | bytes 196608 | tf_op jit(solution)/shard_map/convert_element_type | solution.py:523
Async XLA Ops:
  0.0 3.1 %collective-permute-start = (bf16[4,4,1536]{2,1,0:T(4,128)(2,1)}, bf16[4,4,1536]{2,1,0:T(4,128)(2,1)S(1)}, u32[]{:S(2)}, u32[]{:S(2)}) collective-permute-start(bf16[4,4,1536]{2,1,0:T(4,128)(2,1)} %hidden.1), channel_id=1, source_target_pairs={{0,1},{1,0},{2,3},{3,2},{4,5},{5,4},{6,7},{7,6},{8,9},{9,8},{10,11... | collective-permute-start | bytes 147464 | tf_op jit(solution)/shard_map/ppermute | solution.py:39
  0.5 7.0 %collective-permute-start.2 = (bf16[4,4,1536]{2,1,0:T(4,128)(2,1)}, bf16[4,4,1536]{2,1,0:T(4,128)(2,1)S(1)}, u32[]{:S(2)}, u32[]{:S(2)}) collective-permute-start(bf16[4,4,1536]{2,1,0:T(4,128)(2,1)} %hidden.1), channel_id=1, source_target_pairs={{0,3},{1,2},{2,1},{3,0},{4,7},{5,6},{6,5},{7,4},{8,11},{9,10},{10,... | collective-permute-start | bytes 147464 | tf_op jit(solution)/shard_map/ppermute | solution.py:39
  3.1 4.4 %collective-permute-start.1 = (bf16[4,4,1536]{2,1,0:T(4,128)(2,1)}, bf16[4,4,1536]{2,1,0:T(4,128)(2,1)S(1)}, u32[]{:S(2)}, u32[]{:S(2)}) collective-permute-start(bf16[4,4,1536]{2,1,0:T(4,128)(2,1)} %hidden.1), channel_id=1, source_target_pairs={{0,2},{1,3},{2,0},{3,1},{4,6},{5,7},{6,4},{7,5},{8,10},{9,11},{10,... | collective-permute-start | bytes 147464 | tf_op jit(solution)/shard_map/ppermute | solution.py:39
  11.0 5.0 %collective-permute-start.3 = (bf16[16,1152]{1,0:T(8,128)(2,1)S(1)}, bf16[16,1152]{1,0:T(8,128)(2,1)S(1)}, u32[]{:S(2)}, u32[]{:S(2)}) collective-permute-start(bf16[16,1152]{1,0:T(8,128)(2,1)S(1)} %get-tuple-element.33), channel_id=1, source_target_pairs={{0,2},{2,0},{4,6},{6,4},{8,10},{10,8},{12,14},{14,12},{16,18},{18,... | collective-permute-start | bytes 110600 | tf_op jit(solution)/shard_map/ppermute | solution.py:29
  16.7 1.2 %collective-permute-start.4 = (bf16[4,4,1536]{2,1,0:T(4,128)(2,1)S(1)}, bf16[4,4,1536]{2,1,0:T(4,128)(2,1)S(1)}, u32[]{:S(2)}, u32[]{:S(2)}) collective-permute-start(bf16[4,4,1536]{2,1,0:T(4,128)(2,1)S(1)} %get-tuple-element.36), channel_id=1, source_target_pairs={{0,1},{1,0},{2,3},{3,2},{4,5},{5,4},{6,7},{7,6},{8,9},{9,8},{10,11... | collective-permute-start | bytes 147464 | tf_op jit(solution)/shard_map/ppermute | solution.py:39

commit v3 on v2

--- a/solution.py
+++ b/solution.py
@@ -69,7 +69,6 @@
     parents,
     gain,
     hidden,
-    wq,
     wk,
     wv,
     pk,
@@ -84,7 +83,6 @@
         gain_ref,
         xn_ref,
         scale_ref,
-        wq_ref,
         keys_ref,
         values_ref,
         cosine_ref,
@@ -120,10 +118,6 @@
             place = pl.ds(n * size, size)
             large.append((source.at[place], target.at[place]))
     large += [(pk, keys_ref.at[pl.ds(0, blocks)]), (gk, keys_ref.at[pl.ds(blocks, own)])]
-    size = wq.shape[0] // 4
-    for n in range(4):
-        place = pl.ds(n * size, size)
-        large.append((wq.at[place, pl.ds(0, wq_ref.shape[1])], wq_ref.at[place]))
     copies = [
         pltpu.make_async_copy(source, target, sems.at[n])
         for n, (source, target) in enumerate(small + large)
@@ -224,32 +218,22 @@
     gain_ref,
     xn_ref,
     scale_ref,
-    wq_ref,
     keys_ref,
     values_ref,
     cosine_ref,
     sine_ref,
     bias_ref,
-    wq,
+    wq_ref,
     *refs,
 ):
     steps, own, tp, kv, group, packed = sizes
     pieces = refs[:tp]
-    kept_ref, kept_lse_ref, sent_ref, x_s, xn_s, wq_s, sems = refs[tp:]
+    kept_ref, kept_lse_ref, sent_ref, x_s, xn_s = refs[tp:]
     rows = steps * own
     packs = kv // packed
     keys_count = bias_ref.shape[0]
     keys_space = values_ref.shape[1]
-    near = wq_ref.shape[1]
     size = packed * group * HD
-    copies = [
-        pltpu.make_async_copy(
-            wq.at[:, pl.ds(near + n * size, size)], wq_s.at[n], sems.at[n]
-        )
-        for n in range((wq.shape[1] - near) // size)
-    ]
-    for copy in copies:
-        copy.start()
 
     xn_s[pl.ds(0, rows), :] = xn_ref[...]
     scale = lay_out(pieces, gain_ref, x_s, xn_s, rows)
@@ -260,25 +244,28 @@
     owner = quotient(lane, group * 2 * rows)
     pad = jnp.zeros((keys_space - keys_count, lanes), jnp.bfloat16)
 
-    def score(p):
-        if p * size < near:
-            w = wq_ref[:, pl.ds(p * size, size)]
-        else:
-            n = p - near // size
-            copies[n].wait()
-            w = wq_s[n]
-        q = jnp.dot(xn_s[...], w, preferred_element_type=jnp.float32)
-        q = jnp.concatenate(
-            [q[:, j * HD : (j + 1) * HD] * scale for j in range(packed * group)], axis=0
-        ).T
-        cosine, sine = cosine_ref[...], sine_ref[...]
+    every = range(packs)
+    queries = []
+    for p in every:
+        q = jnp.dot(
+            xn_s[...], wq_ref[:, pl.ds(p * size, size)], preferred_element_type=jnp.float32
+        )
+        queries.append(
+            jnp.concatenate(
+                [q[:, j * HD : (j + 1) * HD] * scale for j in range(packed * group)], axis=0
+            )
+        )
+    cosine, sine = cosine_ref[...], sine_ref[...]
+    scores = []
+    for p in every:
+        q = queries[p].T
         first, second = q[: HD // 2], q[HD // 2 :]
         q = jnp.concatenate(
             [first * cosine - second * sine, second * cosine + first * sine], axis=0
         )
         q = jnp.concatenate([jnp.where(owner == i, q, 0.0) for i in range(packed)], axis=0)
         keys = keys_ref[:, :, pl.ds(p * packed * HD, packed * HD)]
-        return (
+        scores.append(
             jnp.dot(
                 keys.reshape(keys_space, packed * HD)[:keys_count],
                 q.astype(jnp.bfloat16),
@@ -286,31 +273,32 @@
             )
             + bias_ref[...]
         )
-
-    def mix(p, scores):
-        top = jnp.max(scores, axis=0, keepdims=True)
-        powers = jnp.exp(scores - top)
-        total = jnp.sum(powers, axis=0, keepdims=True)
-        mixed = jnp.dot(
+    tops = [jnp.max(x, axis=0, keepdims=True) for x in scores]
+    powers = [jnp.exp(x - top) for x, top in zip(scores, tops)]
+    totals = [jnp.sum(x, axis=0, keepdims=True) for x in powers]
+    mixed = [
+        jnp.dot(
             values_ref[pl.ds(p * packed * HD, packed * HD), :],
-            jnp.concatenate([powers.astype(jnp.bfloat16), pad], axis=0),
+            jnp.concatenate([powers[p].astype(jnp.bfloat16), pad], axis=0),
             preferred_element_type=jnp.float32,
         )
-        out = mixed[:HD]
+        for p in every
+    ]
+    results = []
+    for p in every:
+        out = mixed[p][:HD]
         for i in range(1, packed):
-            out = jnp.where(owner == i, mixed[i * HD : (i + 1) * HD], out)
-        out = (out * (1.0 / total)).T
+            out = jnp.where(owner == i, mixed[p][i * HD : (i + 1) * HD], out)
+        out = (out * (1.0 / totals[p])).T
         for j in range(packed * group):
             cols = pl.ds((p * packed * group + j) * HD, HD)
             lower = j * 2 * rows
             kept_ref[:, cols] = out[lower : lower + rows]
             sent_ref[:, cols] = out[lower + rows : lower + 2 * rows].astype(jnp.bfloat16)
-        lse = top + jnp.log(total)
+        lse = tops[p] + jnp.log(totals[p])
         if lanes < HD:
             lse = jnp.concatenate([lse, jnp.zeros((1, HD - lanes), jnp.float32)], axis=1)
-        return lse
-
-    results = [mix(p, score(p)) for p in range(packs)]
+        results.append(lse)
 
     sublane = lax.broadcasted_iota(jnp.int32, (rows, HD), 0)
     kept_lse = jnp.zeros((rows, HD), jnp.float32)
@@ -415,7 +403,6 @@
     cache = (blocks + own + HD // history, history, kv * HD)
     packed = 2 - kv % 2
     packs = kv // packed
-    near = max(packs // 2, 1) * packed * group * HD
     lanes = packed * group * 2 * rows
     loaded = pl.pallas_call(
         functools.partial(load_kernel, (steps, own, tp, kv, group, history, packed)),
@@ -423,15 +410,14 @@
             jax.ShapeDtypeStruct((1, width), f32),
             jax.ShapeDtypeStruct((rows, width), bf16),
             jax.ShapeDtypeStruct((rows, HD), f32),
-            jax.ShapeDtypeStruct((width, near), bf16),
             jax.ShapeDtypeStruct(cache, bf16),
             jax.ShapeDtypeStruct((kv * HD, cache[0] * history), bf16),
             jax.ShapeDtypeStruct((HD // 2, lanes), f32),
             jax.ShapeDtypeStruct((HD // 2, lanes), f32),
             jax.ShapeDtypeStruct(((blocks + own) * history + rows, lanes), f32),
         ),
-        in_specs=[hbm] * 11 + [vmem] * (tp - 1),
-        out_specs=(vmem,) * 9,
+        in_specs=[hbm] * 10 + [vmem] * (tp - 1),
+        out_specs=(vmem,) * 8,
         scratch_shapes=[
             pltpu.SMEM(lengths.shape, jnp.int32),
             pltpu.SMEM(parents.shape, jnp.int32),
@@ -452,7 +438,6 @@
                 parents,
                 norm_gain[None, :],
                 hidden_in,
-                w_query,
                 w_key,
                 w_value,
                 prompt_keys.reshape(blocks, history, kv * HD),
@@ -471,17 +456,15 @@
             jax.ShapeDtypeStruct((rows, HD), f32),
             jax.ShapeDtypeStruct((rows, heads * HD + HD), bf16),
         ),
-        in_specs=[vmem] * 9 + [hbm] + [vmem] * tp,
+        in_specs=[vmem] * 9 + [vmem] * tp,
         out_specs=(vmem,) * 3,
         scratch_shapes=[
             pltpu.VMEM((tp, rows, part), f32),
             pltpu.VMEM((2 * rows, width), bf16),
-            pltpu.VMEM((packs, width, packed * group * HD), bf16),
-            pltpu.SemaphoreType.DMA((kv,)),
         ],
         compiler_params=params,
         name="attend",
-    )(*loaded, in_hbm(w_query), *far_pieces)
+    )(*loaded, pltpu.with_memory_space_constraint(w_query, pltpu.VMEM), *far_pieces)
 
     got = permute_by(sent, "req", 1)
     kept_lse, w_out_near = pl.pallas_call(

time: 18.8 us -> 16.9 us (0.90)
  Pallas kernels: 12 us -> 10.1 us
  waiting for transfers between devices: 0.72 us -> 1.08 us
  starting transfers between devices: 5.15 us -> 4.8 us
    pallas_call x1, Pallas kernels: 3.56 us -> 2.15 us  [body(): pl.pallas_call(functools.partial(attend_kernel, (steps, own, tp, kv, grou...]
    pallas_call x1, Pallas kernels: 4.35 us -> 3.86 us  [body(): pl.pallas_call(functools.partial(load_kernel, (steps, own, tp, kv, group,...]
    ppermute x1, starting transfers between devices: 2.09 us -> 1.7 us  [permute_by(): return lax.ppermute(value, axis, pairs)]
    ppermute x4, waiting for transfers between devices: 0.72 us -> 1.08 us  [across(): return lax.ppermute(value, ('req', 'tp'), pairs)]
  transfers between devices with their start and end apart: 5 -> 5, of which waited for: 1 -> 2; matrix products, arithmetic and copies ran while one was open for 0% -> 0% of each run, Pallas kernels for 42% -> 43%
where the time goes in v3:
time: 16.9 us; the launch traced here: 16.7 us
  Pallas kernels  10.1 us (60%)
  starting transfers between devices  4.8 us (28%)
  waiting for transfers between devices  1.08 us (6%)
  other arithmetic  0.65 us (4%)
    pallas_call x1, Pallas kernels, body(): pl.pallas_call(functools.partial(load_kernel, (steps, own, tp, kv, group,...  3.86 us
    ppermute x4, starting transfers between devices, across(): return lax.ppermute(value, ('req', 'tp'), pairs)  3.11 us
    pallas_call x1, Pallas kernels, body(): pl.pallas_call(fetch_kernel, out_shape=(jax.ShapeDtypeStruct((rows, HD),...  2.86 us
    pallas_call x1, Pallas kernels, body(): pl.pallas_call(functools.partial(attend_kernel, (steps, own, tp, kv, grou...  2.15 us
    ppermute x1, starting transfers between devices, permute_by(): return lax.ppermute(value, axis, pairs)  1.7 us
    ppermute x4, waiting for transfers between devices, across(): return lax.ppermute(value, ('req', 'tp'), pairs)  1.08 us
    pallas_call x1, Pallas kernels, body(): pl.pallas_call(functools.partial(project_kernel, (steps, own, tp, heads,...  0.75 us
    convert_element_type x1, other arithmetic, body(): return total.astype(bf16)  0.65 us
  transfers between devices with their start and end apart: 5, of which 2 were waited for; matrix products, arithmetic and copies ran while one was open for 0% of the time, Pallas kernels for 43%

profile of v3, /device:TPU:0, one launch (start us, length us, event | category | flops | bytes accessed | tf_op | source)
XLA Modules:
  0.0 16.7 jit_solution(12632800589445812003)
XLA Ops:
  0.0 0.0 copy-start
  0.0 0.5 %collective-permute-start = (bf16[4,4,1536]{2,1,0:T(4,128)(2,1)}, bf16[4,4,1536]{2,1,0:T(4,128)(2,1)S(1)}, u32[]{:S(2)}, u32[]{:S(2)}) collective-permute-start(bf16[4,4,1536]{2,1,0:T(4,128)(2,1)} %hidden.1), channel_id=1, source_target_pairs={{0,1},{1,0},{2,3},{3,2},{4,5},{5,4},{6,7},{7,6},{8,9},{9,8},{10,11... | collective-permute-start | bytes 147464 | tf_op jit(solution)/shard_map/ppermute | solution.py:39
  0.5 2.6 %collective-permute-start.2 = (bf16[4,4,1536]{2,1,0:T(4,128)(2,1)}, bf16[4,4,1536]{2,1,0:T(4,128)(2,1)S(1)}, u32[]{:S(2)}, u32[]{:S(2)}) collective-permute-start(bf16[4,4,1536]{2,1,0:T(4,128)(2,1)} %hidden.1), channel_id=1, source_target_pairs={{0,3},{1,2},{2,1},{3,0},{4,7},{5,6},{6,5},{7,4},{8,11},{9,10},{10,... | collective-permute-start | bytes 147464 | tf_op jit(solution)/shard_map/ppermute | solution.py:39
  3.1 0.1 collective-permute-start.1
  3.1 0.0 collective-permute-done.refs_0_
  3.1 3.9 %load.1 = (f32[1,3072]{1,0:T(1,128)S(1)}, bf16[16,3072]{1,0:T(8,128)(2,1)S(1)}, f32[16,128]{1,0:T(8,128)S(1)}, bf16[14,64,512]{2,1,0:T(8,128)(2,1)S(1)}, bf16[51...) custom-call(s32[8]{0:T(128)} %lengths.1, s32[4,64]{1,0:T(4,128)} %parents.1, ...), custom_call_target="tpu_custom_call" | custom-call | tf_op jit(solution)/shard_map/load/pallas_call | solution.py:407
  7.0 0.0 collective-permute-done.2.refs_1_
  7.0 0.4 %collective-permute-done.1.refs_0_ = bf16[4,4,1536]{2,1,0:T(4,128)(2,1)S(1)} collective-permute-done((bf16[4,4,1536]{2,1,0:T(4,128)(2,1)}, bf16[4,4,1536]{2,1,0:T(4,128)(2,1)S(1)}, u32[]{:S(2)}, u32[]{:S(2)}) %collective-permute-start.1) | collective-permute-done | bytes 49184 | tf_op jit(solution)/shard_map/ppermute | solution.py:39
  7.4 0.0 copy-done
  7.4 2.1 %attend.1 = (f32[16,1024]{1,0:T(8,128)S(1)}, f32[16,128]{1,0:T(8,128)S(1)}, bf16[16,1152]{1,0:T(8,128)(2,1)S(1)}) custom-call(f32[1,3072]{1,0:T(1,128)S(1)} %get-tuple-element.20.gain_ref, bf16[16,3072]{1,0:T(8,128)(2,1)S(1)} %get-tuple-element.21.xn_ref, f32[16,128]{1,0:T(8,128)S(1)} %get-tuple-element.22.scale_ref, ...), custom_call_target="tpu_custom_call" | custom-call | tf_op jit(solution)/shard_map/attend/pallas_call | solution.py:452
  9.5 1.7 %collective-permute-start.3 = (bf16[16,1152]{1,0:T(8,128)(2,1)S(1)}, bf16[16,1152]{1,0:T(8,128)(2,1)S(1)}, u32[]{:S(2)}, u32[]{:S(2)}) collective-permute-start(bf16[16,1152]{1,0:T(8,128)(2,1)S(1)} %get-tuple-element.31), channel_id=1, source_target_pairs={{0,2},{2,0},{4,6},{6,4},{8,10},{10,8},{12,14},{14,12},{16,18},{18,... | collective-permute-start | bytes 110600 | tf_op jit(solution)/shard_map/ppermute | solution.py:29
  11.2 2.9 %fetch.1 = (f32[16,128]{1,0:T(8,128)S(1)}, bf16[2,1024,1536]{2,1,0:T(8,128)(2,1)S(1)}) custom-call(f32[16,128]{1,0:T(8,128)S(1)} %get-tuple-element.29.kept_lse_ref, bf16[1024,3072]{1,0:T(8,128)(2,1)} %w_out.1), custom_call_target="tpu_custom_call" | custom-call | tf_op jit(solution)/shard_map/fetch/pallas_call | solution.py:470
  14.1 0.0 collective-permute-done.3.got_ref
  14.1 0.7 %project.1 = (bf16[16,1024]{1,0:T(8,128)(2,1)S(1)}, bf16[4,4,1536]{2,1,0:T(4,128)(2,1)S(1)}) custom-call(f32[16,1024]{1,0:T(8,128)S(1)} %get-tuple-element.28.kept_ref, f32[16,128]{1,0:T(8,128)S(1)} %get-tuple-element.30.kept_lse_ref, bf16[16,1152]{1,0:T(8,128)(2,1)S(1)} %collective-permute-done.3.got_ref, bf16[2,1024,1536]{2,1,0:T(8,128)(2,1)S(1)} %get-tuple-element.32.w_out_ref), custom_call_target="tpu_custom_call" | custom-call | tf_op jit(solution)/shard_map/project/pallas_call | solution.py:484
  14.8 0.0 collective-permute-start.4
  14.8 0.5 %project_own.1 = f32[4,4,1536]{2,1,0:T(4,128)S(1)} custom-call(bf16[16,1024]{1,0:T(8,128)(2,1)S(1)} %get-tuple-element.33.ctx_ref, bf16[2,1024,1536]{2,1,0:T(8,128)(2,1)S(1)} %get-tuple-element.32.w_out_ref), custom_call_target="tpu_custom_call" | custom-call | tf_op jit(solution)/shard_map/project_own/pallas_call | solution.py:496
  15.4 0.7 %collective-permute-done.4 = bf16[4,4,1536]{2,1,0:T(4,128)(2,1)S(1)} collective-permute-done((bf16[4,4,1536]{2,1,0:T(4,128)(2,1)S(1)}, bf16[4,4,1536]{2,1,0:T(4,128)(2,1)S(1)}, u32[]{:S(2)}, u32[]{:S(2)}) %collective-permute-start.4) | collective-permute-done | bytes 49184 | tf_op jit(solution)/shard_map/ppermute | solution.py:39
  16.1 0.6 %add_convert_fusion = bf16[4,4,1536]{2,1,0:T(4,128)(2,1)} fusion(f32[4,4,1536]{2,1,0:T(4,128)S(1)} %project_own.1, bf16[4,4,1536]{2,1,0:T(4,128)(2,1)S(1)} %collective-permute-done.4), kind=kLoop, calls=%fused_computation | loop fusion | flops 73728 | bytes 196608 | tf_op jit(solution)/shard_map/convert_element_type | solution.py:506
Async XLA Ops:
  0.0 7.4 %copy-start = (bf16[3072,1024]{1,0:T(8,128)(2,1)S(1)}, bf16[3072,1024]{1,0:T(8,128)(2,1)}, u32[]{:S(2)}) copy-start(bf16[3072,1024]{1,0:T(8,128)(2,1)} %wq_ref.1) | copy-start | bytes 18874372
  0.0 3.1 %collective-permute-start = (bf16[4,4,1536]{2,1,0:T(4,128)(2,1)}, bf16[4,4,1536]{2,1,0:T(4,128)(2,1)S(1)}, u32[]{:S(2)}, u32[]{:S(2)}) collective-permute-start(bf16[4,4,1536]{2,1,0:T(4,128)(2,1)} %hidden.1), channel_id=1, source_target_pairs={{0,1},{1,0},{2,3},{3,2},{4,5},{5,4},{6,7},{7,6},{8,9},{9,8},{10,11... | collective-permute-start | bytes 147464 | tf_op jit(solution)/shard_map/ppermute | solution.py:39
  0.5 6.5 %collective-permute-start.2 = (bf16[4,4,1536]{2,1,0:T(4,128)(2,1)}, bf16[4,4,1536]{2,1,0:T(4,128)(2,1)S(1)}, u32[]{:S(2)}, u32[]{:S(2)}) collective-permute-start(bf16[4,4,1536]{2,1,0:T(4,128)(2,1)} %hidden.1), channel_id=1, source_target_pairs={{0,3},{1,2},{2,1},{3,0},{4,7},{5,6},{6,5},{7,4},{8,11},{9,10},{10,... | collective-permute-start | bytes 147464 | tf_op jit(solution)/shard_map/ppermute | solution.py:39
  3.1 4.3 %collective-permute-start.1 = (bf16[4,4,1536]{2,1,0:T(4,128)(2,1)}, bf16[4,4,1536]{2,1,0:T(4,128)(2,1)S(1)}, u32[]{:S(2)}, u32[]{:S(2)}) collective-permute-start(bf16[4,4,1536]{2,1,0:T(4,128)(2,1)} %hidden.1), channel_id=1, source_target_pairs={{0,2},{1,3},{2,0},{3,1},{4,6},{5,7},{6,4},{7,5},{8,10},{9,11},{10,... | collective-permute-start | bytes 147464 | tf_op jit(solution)/shard_map/ppermute | solution.py:39
  9.5 4.6 %collective-permute-start.3 = (bf16[16,1152]{1,0:T(8,128)(2,1)S(1)}, bf16[16,1152]{1,0:T(8,128)(2,1)S(1)}, u32[]{:S(2)}, u32[]{:S(2)}) collective-permute-start(bf16[16,1152]{1,0:T(8,128)(2,1)S(1)} %get-tuple-element.31), channel_id=1, source_target_pairs={{0,2},{2,0},{4,6},{6,4},{8,10},{10,8},{12,14},{14,12},{16,18},{18,... | collective-permute-start | bytes 110600 | tf_op jit(solution)/shard_map/ppermute | solution.py:29
  14.8 1.2 %collective-permute-start.4 = (bf16[4,4,1536]{2,1,0:T(4,128)(2,1)S(1)}, bf16[4,4,1536]{2,1,0:T(4,128)(2,1)S(1)}, u32[]{:S(2)}, u32[]{:S(2)}) collective-permute-start(bf16[4,4,1536]{2,1,0:T(4,128)(2,1)S(1)} %get-tuple-element.34), channel_id=1, source_target_pairs={{0,1},{1,0},{2,3},{3,2},{4,5},{5,4},{6,7},{7,6},{8,9},{9,8},{10,11... | collective-permute-start | bytes 147464 | tf_op jit(solution)/shard_map/ppermute | solution.py:39

commit v4 on v3

--- a/solution.py
+++ b/solution.py
@@ -71,9 +71,7 @@
     hidden,
     wk,
     wv,
-    pk,
     pv,
-    gk,
     gv,
     *refs,
 ):
@@ -83,7 +81,7 @@
         gain_ref,
         xn_ref,
         scale_ref,
-        keys_ref,
+        new_keys_ref,
         values_ref,
         cosine_ref,
         sine_ref,
@@ -98,7 +96,8 @@
         sems,
     ) = refs[tp - 1 :]
     rows = steps * own
-    blocks = pk.shape[0]
+    quarters = 4
+    blocks = pv.shape[0]
     half_len = blocks * history
     device = lax.axis_index("req")
     request = device // 2
@@ -112,12 +111,11 @@
     ]
     old = blocks + own
     large = [(pv, values_s.at[pl.ds(0, blocks)]), (gv, values_s.at[pl.ds(blocks, own)])]
-    for source, target, parts in ((wk, wk_s, 2), (wv, wv_s, 2)):
-        size = source.shape[0] // parts
-        for n in range(parts):
+    for source, target in ((wk, wk_s), (wv, wv_s)):
+        size = source.shape[0] // quarters
+        for n in range(quarters):
             place = pl.ds(n * size, size)
             large.append((source.at[place], target.at[place]))
-    large += [(pk, keys_ref.at[pl.ds(0, blocks)]), (gk, keys_ref.at[pl.ds(blocks, own)])]
     copies = [
         pltpu.make_async_copy(source, target, sems.at[n])
         for n, (source, target) in enumerate(small + large)
@@ -160,10 +158,10 @@
             out = jnp.where(beam == j, parents_s[s, request * BEAMS + j], out)
         return out
 
-    row = remainder(lax.broadcasted_iota(jnp.int32, (8, lanes), 1), 2 * rows)
-    row_step = quotient(remainder(row, rows), own)
-    row_parity = jnp.where(row < rows, parity, 1 - parity)
-    beam = row_parity * own + remainder(row, own)
+    lane = lax.broadcasted_iota(jnp.int32, (8, lanes), 1)
+    row_step = quotient(remainder(lane, rows), own)
+    row_parity = jnp.where(lane < lanes // 2, parity, 1 - parity)
+    beam = row_parity * own + remainder(lane, own)
     ancestors = [None] * steps
     at = beam
     for s in reversed(range(steps)):
@@ -191,26 +189,25 @@
     for copy in large[:2]:
         copy.wait()
     values_ref[:, pl.ds(0, old * history)] = values_s[...].reshape(old * history, kv * HD).T
-    keys_ref[pl.ds(old, HD // history)] = jnp.zeros(
-        (HD // history, history, kv * HD), jnp.bfloat16
-    )
-    for copy in large[2:4]:
-        copy.wait()
-    fresh = jnp.dot(xn_ref[...], wk_s[...], preferred_element_type=jnp.float32)
+
+    def project(w_s, copies):
+        size = w_s.shape[0] // quarters
+        out = jnp.zeros((rows, kv * HD), jnp.float32)
+        for n, copy in enumerate(copies):
+            place = pl.ds(n * size, size)
+            copy.wait()
+            out += jnp.dot(xn_ref[:, place], w_s[place], preferred_element_type=jnp.float32)
+        return out
+
+    fresh = project(wk_s, large[2 : 2 + quarters])
     for g in range(kv):
         cols = pl.ds(g * HD, HD)
-        keys_ref[old, pl.ds(0, rows), cols] = rotate(
-            fresh[:, g * HD : (g + 1) * HD], key_cosine, key_sine
-        )
-    for copy in large[4:6]:
-        copy.wait()
-    fresh = jnp.dot(xn_ref[...], wv_s[...], preferred_element_type=jnp.float32) * scale
+        new_keys_ref[:, cols] = rotate(fresh[:, g * HD : (g + 1) * HD], key_cosine, key_sine)
+    fresh = project(wv_s, large[2 + quarters :]) * scale
     fresh = jnp.concatenate(
         [fresh, jnp.zeros((HD - rows, kv * HD), jnp.float32)], axis=0
     ).astype(jnp.bfloat16)
     values_ref[:, pl.ds(old * history, HD)] = fresh.T
-    for copy in large[6:]:
-        copy.wait()
 
 
 def attend_kernel(
@@ -218,59 +215,64 @@
     gain_ref,
     xn_ref,
     scale_ref,
-    keys_ref,
+    new_keys_ref,
     values_ref,
     cosine_ref,
     sine_ref,
     bias_ref,
     wq_ref,
+    pk_ref,
+    gk_ref,
     *refs,
 ):
     steps, own, tp, kv, group, packed = sizes
     pieces = refs[:tp]
     kept_ref, kept_lse_ref, sent_ref, x_s, xn_s = refs[tp:]
     rows = steps * own
+    part = pieces[0].shape[-1]
     packs = kv // packed
+    each = packed * group
+    size = each * HD
+    lanes = each * 2 * rows
     keys_count = bias_ref.shape[0]
     keys_space = values_ref.shape[1]
-    size = packed * group * HD
+    lane = lax.broadcasted_iota(jnp.int32, (HD, lanes), 1)
+    owner = quotient(remainder(lane, lanes // 2), group * rows)
+    pad = jnp.zeros((keys_space - keys_count, lanes), jnp.bfloat16)
 
     xn_s[pl.ds(0, rows), :] = xn_ref[...]
     scale = lay_out(pieces, gain_ref, x_s, xn_s, rows)
+    me_tp = lax.axis_index("tp")
+    product = jnp.zeros((2 * rows, kv * group * HD), jnp.float32)
+    for t in range(tp):
+        place = pl.ds(pl.multiple_of((me_tp ^ t) * part, HD), part)
+        product += jnp.dot(xn_s[:, place], wq_ref[place, :], preferred_element_type=jnp.float32)
     scale = jnp.concatenate([scale_ref[...], jnp.broadcast_to(scale, (rows, HD))], axis=0)
     scale = scale * HD**-0.5
-    lanes = size // HD * 2 * rows
-    lane = lax.broadcasted_iota(jnp.int32, (HD, lanes), 1)
-    owner = quotient(lane, group * 2 * rows)
-    pad = jnp.zeros((keys_space - keys_count, lanes), jnp.bfloat16)
+    product = [product[:, h * HD : (h + 1) * HD] * scale for h in range(kv * group)]
 
     every = range(packs)
-    queries = []
-    for p in every:
-        q = jnp.dot(
-            xn_s[...], wq_ref[:, pl.ds(p * size, size)], preferred_element_type=jnp.float32
-        )
-        queries.append(
-            jnp.concatenate(
-                [q[:, j * HD : (j + 1) * HD] * scale for j in range(packed * group)], axis=0
-            )
-        )
     cosine, sine = cosine_ref[...], sine_ref[...]
     scores = []
     for p in every:
-        q = queries[p].T
+        q = product[p * each : (p + 1) * each]
+        q = jnp.concatenate([x[:rows] for x in q] + [x[rows:] for x in q], axis=0).T
         first, second = q[: HD // 2], q[HD // 2 :]
         q = jnp.concatenate(
             [first * cosine - second * sine, second * cosine + first * sine], axis=0
         )
         q = jnp.concatenate([jnp.where(owner == i, q, 0.0) for i in range(packed)], axis=0)
-        keys = keys_ref[:, :, pl.ds(p * packed * HD, packed * HD)]
+        cols = pl.ds(p * packed * HD, packed * HD)
+        keys = jnp.concatenate(
+            [
+                pk_ref[0, :, cols],
+                gk_ref[:, :, cols].reshape(-1, packed * HD),
+                new_keys_ref[:, cols],
+            ],
+            axis=0,
+        )
         scores.append(
-            jnp.dot(
-                keys.reshape(keys_space, packed * HD)[:keys_count],
-                q.astype(jnp.bfloat16),
-                preferred_element_type=jnp.float32,
-            )
+            jnp.dot(keys, q.astype(jnp.bfloat16), preferred_element_type=jnp.float32)
             + bias_ref[...]
         )
     tops = [jnp.max(x, axis=0, keepdims=True) for x in scores]
@@ -284,34 +286,36 @@
         )
         for p in every
     ]
-    results = []
+    results, logs = [], []
     for p in every:
         out = mixed[p][:HD]
         for i in range(1, packed):
             out = jnp.where(owner == i, mixed[p][i * HD : (i + 1) * HD], out)
-        out = (out * (1.0 / totals[p])).T
-        for j in range(packed * group):
-            cols = pl.ds((p * packed * group + j) * HD, HD)
-            lower = j * 2 * rows
-            kept_ref[:, cols] = out[lower : lower + rows]
-            sent_ref[:, cols] = out[lower + rows : lower + 2 * rows].astype(jnp.bfloat16)
-        lse = tops[p] + jnp.log(totals[p])
-        if lanes < HD:
-            lse = jnp.concatenate([lse, jnp.zeros((1, HD - lanes), jnp.float32)], axis=1)
-        results.append(lse)
-
-    sublane = lax.broadcasted_iota(jnp.int32, (rows, HD), 0)
-    kept_lse = jnp.zeros((rows, HD), jnp.float32)
-    terms = jnp.zeros((rows, HD), jnp.float32)
-    for p, lse in enumerate(results):
-        kept_lse = jnp.where(sublane == p, lse, kept_lse)
-        rest = lse
-        for n in range(3):
-            term = rest.astype(jnp.bfloat16).astype(jnp.float32)
-            terms = jnp.where(sublane == n * packs + p, term, terms)
-            rest = rest - term
-    kept_lse_ref[...] = kept_lse
-    sent_ref[:, pl.ds(kv * group * HD, HD)] = terms.astype(jnp.bfloat16)
+        results.append(out * (1.0 / totals[p]))
+        logs.append(jnp.broadcast_to(tops[p] + jnp.log(totals[p]), (8, lanes)))
+
+    def sort(parts):
+        half = lanes // 2
+        if packs == 1:
+            return parts[0][:, :half], parts[0][:, half:]
+        low = lax.broadcasted_iota(jnp.int32, parts[0].shape, 1) < half
+        first, second = parts
+        return (
+            jnp.where(low, first, pltpu.roll(second, half, 1)),
+            jnp.where(low, pltpu.roll(first, half, 1), second),
+        )
+
+    kept_ref[...], sent = sort(results)
+    kept_lse_ref[...], rest = sort(logs)
+    sent_ref[pl.ds(0, HD), :] = sent.astype(jnp.bfloat16)
+    rest = jnp.concatenate([rest] * (rows // 8), axis=0)
+    sublane = lax.broadcasted_iota(jnp.int32, rest.shape, 0)
+    terms = jnp.zeros(rest.shape, jnp.float32)
+    for n in range(3):
+        term = rest.astype(jnp.bfloat16).astype(jnp.float32)
+        terms = jnp.where(sublane == n, term, terms)
+        rest = rest - term
+    sent_ref[pl.ds(HD, rows), :] = terms.astype(jnp.bfloat16)
 
 
 def fetch_kernel(kept_lse_ref, w_out, kept_lse_out, w_out_ref, sems):
@@ -338,32 +342,26 @@
             out_ref[s, :, cols] = out[s * own : (s + 1) * own].astype(out_ref.dtype)
 
 
-def project_own_kernel(sizes, ctx_ref, w_out_ref, out_ref):
-    multiply_out(sizes, ctx_ref[...], w_out_ref, 0, out_ref)
-
-
-def project_kernel(sizes, kept_ref, kept_lse_ref, got_ref, w_out_ref, *refs):
-    steps, own, tp, heads, packs, chunk = sizes
-    ctx_ref, outs = refs[0], refs[1:]
+def project_kernel(sizes, kept_ref, kept_lse_ref, got_ref, w_out_ref, ctx_ref, *outs):
+    steps, own, tp, heads, chunk = sizes
     rows = steps * own
-    base = heads * HD
-    terms = got_ref[:, pl.ds(base, HD)].astype(jnp.float32)
-    lse_got = sum(terms[n * packs : (n + 1) * packs] for n in range(3))
-    lse_got = pltpu.roll(jnp.concatenate([lse_got] * (8 // packs), axis=0), HD - rows, 1)
-    lse_mine = kept_lse_ref[pl.ds(0, 8), :]
+    terms = got_ref[pl.ds(HD, rows), :].astype(jnp.float32)
+    lse_got = terms[0:1] + terms[1:2] + terms[2:3]
+    lse_mine = kept_lse_ref[pl.ds(0, 1), :]
     top = jnp.maximum(lse_mine, lse_got)
     mine = jnp.exp(lse_mine - top)
     got = jnp.exp(lse_got - top)
-    share = (mine / (mine + got)).T
-    for h in range(heads):
-        cols = pl.ds(h * HD, HD)
-        p, j = divmod(h, heads // packs)
-        w = share[j * 2 * rows : j * 2 * rows + rows, p : p + 1]
-        ctx_ref[:, cols] = (
-            kept_ref[:, cols] * w + got_ref[:, cols].astype(jnp.float32) * (1.0 - w)
-        ).astype(jnp.bfloat16)
+    share = mine / (mine + got)
+    ctx = kept_ref[...] * share + got_ref[pl.ds(0, HD), :].astype(jnp.float32) * (1.0 - share)
+    ctx = ctx.T.astype(jnp.bfloat16)
+    ctx = jnp.concatenate([ctx[h * rows : (h + 1) * rows] for h in range(heads)], axis=1)
+    ctx_ref[...] = ctx
     for d in range(1, tp):
-        multiply_out((steps, own, chunk), ctx_ref[...], w_out_ref, d, outs[d - 1])
+        multiply_out((steps, own, chunk), ctx, w_out_ref, d, outs[d - 1])
+
+
+def project_own_kernel(sizes, ctx_ref, w_out_ref, out_ref):
+    multiply_out(sizes, ctx_ref[...], w_out_ref, 0, out_ref)
 
 
 def body(
@@ -395,12 +393,15 @@
     def in_hbm(x):
         return pltpu.with_memory_space_constraint(x, pltpu.HBM)
 
+    def in_vmem(x):
+        return pltpu.with_memory_space_constraint(x, pltpu.VMEM)
+
     vmem = pl.BlockSpec(memory_space=pltpu.VMEM)
     hbm = pl.BlockSpec(memory_space=pltpu.HBM)
     params = pltpu.CompilerParams(vmem_limit_bytes=16 * 2**20)
     f32, bf16 = jnp.float32, jnp.bfloat16
     blocks = prompt_keys.shape[1] // history
-    cache = (blocks + own + HD // history, history, kv * HD)
+    old = (blocks + own) * history
     packed = 2 - kv % 2
     packs = kv // packed
     lanes = packed * group * 2 * rows
@@ -410,13 +411,13 @@
             jax.ShapeDtypeStruct((1, width), f32),
             jax.ShapeDtypeStruct((rows, width), bf16),
             jax.ShapeDtypeStruct((rows, HD), f32),
-            jax.ShapeDtypeStruct(cache, bf16),
-            jax.ShapeDtypeStruct((kv * HD, cache[0] * history), bf16),
+            jax.ShapeDtypeStruct((rows, kv * HD), bf16),
+            jax.ShapeDtypeStruct((kv * HD, old + HD), bf16),
             jax.ShapeDtypeStruct((HD // 2, lanes), f32),
             jax.ShapeDtypeStruct((HD // 2, lanes), f32),
-            jax.ShapeDtypeStruct(((blocks + own) * history + rows, lanes), f32),
+            jax.ShapeDtypeStruct((old + rows, lanes), f32),
         ),
-        in_specs=[hbm] * 10 + [vmem] * (tp - 1),
+        in_specs=[hbm] * 8 + [vmem] * (tp - 1),
         out_specs=(vmem,) * 8,
         scratch_shapes=[
             pltpu.SMEM(lengths.shape, jnp.int32),
@@ -440,9 +441,7 @@
                 hidden_in,
                 w_key,
                 w_value,
-                prompt_keys.reshape(blocks, history, kv * HD),
                 prompt_values.reshape(blocks, history, kv * HD),
-                gen_keys,
                 gen_values,
             )
         ),
@@ -452,11 +451,11 @@
     kept, kept_lse, sent = pl.pallas_call(
         functools.partial(attend_kernel, (steps, own, tp, kv, group, packed)),
         out_shape=(
-            jax.ShapeDtypeStruct((rows, heads * HD), f32),
-            jax.ShapeDtypeStruct((rows, HD), f32),
-            jax.ShapeDtypeStruct((rows, heads * HD + HD), bf16),
+            jax.ShapeDtypeStruct((HD, heads * rows), f32),
+            jax.ShapeDtypeStruct((8, heads * rows), f32),
+            jax.ShapeDtypeStruct((HD + rows, heads * rows), bf16),
         ),
-        in_specs=[vmem] * 9 + [vmem] * tp,
+        in_specs=[vmem] * (11 + tp),
         out_specs=(vmem,) * 3,
         scratch_shapes=[
             pltpu.VMEM((tp, rows, part), f32),
@@ -464,13 +463,13 @@
         ],
         compiler_params=params,
         name="attend",
-    )(*loaded, pltpu.with_memory_space_constraint(w_query, pltpu.VMEM), *far_pieces)
+    )(*loaded, in_vmem(w_query), in_vmem(prompt_keys), in_vmem(gen_keys), *far_pieces)
 
     got = permute_by(sent, "req", 1)
     kept_lse, w_out_near = pl.pallas_call(
         fetch_kernel,
         out_shape=(
-            jax.ShapeDtypeStruct((rows, HD), f32),
+            jax.ShapeDtypeStruct((8, heads * rows), f32),
             jax.ShapeDtypeStruct((tp, heads * HD, part), bf16),
         ),
         in_specs=[vmem, hbm],
@@ -482,7 +481,7 @@
 
     chunk = math.gcd(part, 512)
     ctx, *sums = pl.pallas_call(
-        functools.partial(project_kernel, (steps, own, tp, heads, packs, chunk)),
+        functools.partial(project_kernel, (steps, own, tp, heads, chunk)),
         out_shape=(
             jax.ShapeDtypeStruct((rows, heads * HD), bf16),
             *[jax.ShapeDtypeStruct((steps, own, part), bf16)] * (tp - 1),

time: 16.9 us -> 16.4 us (0.970)
  Pallas kernels: 10.1 us -> 9.6 us
  waiting for transfers between devices: 1.08 us -> 1.45 us
  starting transfers between devices: 4.8 us -> 4.52 us
    ppermute x4, waiting for transfers between devices: 1.08 us -> 1.45 us  [across(): return lax.ppermute(value, ('req', 'tp'), pairs)]
    pallas_call x1, Pallas kernels: 3.86 us -> 3.5 us  [body(): pl.pallas_call(functools.partial(load_kernel, (steps, own, tp, kv, group,...]
    ppermute x1, starting transfers between devices: 1.7 us -> 1.34 us  [permute_by(): return lax.ppermute(value, axis, pairs)]
  transfers between devices with their start and end apart: 5 -> 5, of which waited for: 2 -> 2; matrix products, arithmetic and copies ran while one was open for 0% -> 0% of each run, Pallas kernels for 43% -> 42%
where the time goes in v4:
time: 16.4 us; the launch traced here: 16.3 us
  Pallas kernels  9.6 us (59%)
  starting transfers between devices  4.52 us (28%)
  waiting for transfers between devices  1.45 us (9%)
  other arithmetic  0.65 us (4%)
    pallas_call x1, Pallas kernels, body(): pl.pallas_call(functools.partial(load_kernel, (steps, own, tp, kv, group,...  3.5 us
    ppermute x4, starting transfers between devices, across(): return lax.ppermute(value, ('req', 'tp'), pairs)  3.18 us
    pallas_call x1, Pallas kernels, body(): pl.pallas_call(fetch_kernel, out_shape=(jax.ShapeDtypeStruct((8, heads *...  2.86 us
    pallas_call x1, Pallas kernels, body(): pl.pallas_call(functools.partial(attend_kernel, (steps, own, tp, kv, grou...  2.12 us
    ppermute x4, waiting for transfers between devices, across(): return lax.ppermute(value, ('req', 'tp'), pairs)  1.45 us
    ppermute x1, starting transfers between devices, permute_by(): return lax.ppermute(value, axis, pairs)  1.34 us
    convert_element_type x1, other arithmetic, body(): return total.astype(bf16)  0.65 us
    pallas_call x1, Pallas kernels, body(): pl.pallas_call(functools.partial(project_kernel, (steps, own, tp, heads,...  0.59 us
  transfers between devices with their start and end apart: 5, of which 2 were waited for; matrix products, arithmetic and copies ran while one was open for 0% of the time, Pallas kernels for 42%

profile of v4, /device:TPU:0, one launch (start us, length us, event | category | flops | bytes accessed | tf_op | source)
XLA Modules:
  0.0 16.3 jit_solution(8355349478064437790)
XLA Ops:
  0.0 0.0 copy-start.2
  0.0 0.0 copy-start.1
  0.0 0.0 copy-start
  0.0 0.5 %collective-permute-start = (bf16[4,4,1536]{2,1,0:T(4,128)(2,1)}, bf16[4,4,1536]{2,1,0:T(4,128)(2,1)S(1)}, u32[]{:S(2)}, u32[]{:S(2)}) collective-permute-start(bf16[4,4,1536]{2,1,0:T(4,128)(2,1)} %hidden.1), channel_id=1, source_target_pairs={{0,1},{1,0},{2,3},{3,2},{4,5},{5,4},{6,7},{7,6},{8,9},{9,8},{10,11... | collective-permute-start | bytes 147464 | tf_op jit(solution)/shard_map/ppermute | solution.py:39
  0.5 2.6 %collective-permute-start.2 = (bf16[4,4,1536]{2,1,0:T(4,128)(2,1)}, bf16[4,4,1536]{2,1,0:T(4,128)(2,1)S(1)}, u32[]{:S(2)}, u32[]{:S(2)}) collective-permute-start(bf16[4,4,1536]{2,1,0:T(4,128)(2,1)} %hidden.1), channel_id=1, source_target_pairs={{0,3},{1,2},{2,1},{3,0},{4,7},{5,6},{6,5},{7,4},{8,11},{9,10},{10,... | collective-permute-start | bytes 147464 | tf_op jit(solution)/shard_map/ppermute | solution.py:39
  3.1 0.0 collective-permute-start.1
  3.2 0.0 collective-permute-done.refs_0_
  3.2 3.5 %load.1 = (f32[1,3072]{1,0:T(1,128)S(1)}, bf16[16,3072]{1,0:T(8,128)(2,1)S(1)}, f32[16,128]{1,0:T(8,128)S(1)}, bf16[16,512]{1,0:T(8,128)(2,1)S(1)}, bf16[512,896...) custom-call(s32[8]{0:T(128)} %lengths.1, s32[4,64]{1,0:T(4,128)} %parents.1, ...), custom_call_target="tpu_custom_call" | custom-call | tf_op jit(solution)/shard_map/load/pallas_call | solution.py:408
  6.7 0.0 collective-permute-done.2.refs_1_
  6.7 0.7 %collective-permute-done.1.refs_0_ = bf16[4,4,1536]{2,1,0:T(4,128)(2,1)S(1)} collective-permute-done((bf16[4,4,1536]{2,1,0:T(4,128)(2,1)}, bf16[4,4,1536]{2,1,0:T(4,128)(2,1)S(1)}, u32[]{:S(2)}, u32[]{:S(2)}) %collective-permute-start.1) | collective-permute-done | bytes 49184 | tf_op jit(solution)/shard_map/ppermute | solution.py:39
  7.4 0.0 copy-done.2
  7.4 0.0 copy-done.1
  7.4 0.0 copy-done
  7.5 2.1 %attend.1 = (f32[128,128]{1,0:T(8,128)S(1)}, f32[8,128]{1,0:T(8,128)S(1)}, bf16[144,128]{1,0:T(8,128)(2,1)S(1)}) custom-call(f32[1,3072]{1,0:T(1,128)S(1)} %get-tuple-element.20.gain_ref, bf16[16,3072]{1,0:T(8,128)(2,1)S(1)} %get-tuple-element.21.xn_ref, f32[16,128]{1,0:T(8,128)S(1)} %get-tuple-element.22.scale_ref, ...), custom_call_target="tpu_custom_call" | custom-call | tf_op jit(solution)/shard_map/attend/pallas_call | solution.py:451
  9.6 1.3 %collective-permute-start.3 = (bf16[144,128]{1,0:T(8,128)(2,1)S(1)}, bf16[144,128]{1,0:T(8,128)(2,1)S(1)}, u32[]{:S(2)}, u32[]{:S(2)}) collective-permute-start(bf16[144,128]{1,0:T(8,128)(2,1)S(1)} %get-tuple-element.31), channel_id=1, source_target_pairs={{0,2},{2,0},{4,6},{6,4},{8,10},{10,8},{12,14},{14,12},{16,18},{18,... | collective-permute-start | bytes 110600 | tf_op jit(solution)/shard_map/ppermute | solution.py:29
  10.9 2.9 %fetch.1 = (f32[8,128]{1,0:T(8,128)S(1)}, bf16[2,1024,1536]{2,1,0:T(8,128)(2,1)S(1)}) custom-call(f32[8,128]{1,0:T(8,128)S(1)} %get-tuple-element.29.kept_lse_ref, bf16[1024,3072]{1,0:T(8,128)(2,1)} %w_out.1), custom_call_target="tpu_custom_call" | custom-call | tf_op jit(solution)/shard_map/fetch/pallas_call | solution.py:469
  13.8 0.0 collective-permute-done.3.got_ref
  13.8 0.6 %project.1 = (bf16[16,1024]{1,0:T(8,128)(2,1)S(1)}, bf16[4,4,1536]{2,1,0:T(4,128)(2,1)S(1)}) custom-call(f32[128,128]{1,0:T(8,128)S(1)} %get-tuple-element.28.kept_ref, f32[8,128]{1,0:T(8,128)S(1)} %get-tuple-element.30.kept_lse_ref, bf16[144,128]{1,0:T(8,128)(2,1)S(1)} %collective-permute-done.3.got_ref, bf16[2,1024,1536]{2,1,0:T(8,128)(2,1)S(1)} %get-tuple-element.32.w_out_ref), custom_call_target="tpu_custom_call" | custom-call | tf_op jit(solution)/shard_map/project/pallas_call | solution.py:483
  14.4 0.0 collective-permute-start.4
  14.4 0.5 %project_own.1 = f32[4,4,1536]{2,1,0:T(4,128)S(1)} custom-call(bf16[16,1024]{1,0:T(8,128)(2,1)S(1)} %get-tuple-element.33.ctx_ref, bf16[2,1024,1536]{2,1,0:T(8,128)(2,1)S(1)} %get-tuple-element.32.w_out_ref), custom_call_target="tpu_custom_call" | custom-call | tf_op jit(solution)/shard_map/project_own/pallas_call | solution.py:495
  14.9 0.7 %collective-permute-done.4 = bf16[4,4,1536]{2,1,0:T(4,128)(2,1)S(1)} collective-permute-done((bf16[4,4,1536]{2,1,0:T(4,128)(2,1)S(1)}, bf16[4,4,1536]{2,1,0:T(4,128)(2,1)S(1)}, u32[]{:S(2)}, u32[]{:S(2)}) %collective-permute-start.4) | collective-permute-done | bytes 49184 | tf_op jit(solution)/shard_map/ppermute | solution.py:39
  15.6 0.6 %add_convert_fusion = bf16[4,4,1536]{2,1,0:T(4,128)(2,1)} fusion(f32[4,4,1536]{2,1,0:T(4,128)S(1)} %project_own.1, bf16[4,4,1536]{2,1,0:T(4,128)(2,1)S(1)} %collective-permute-done.4), kind=kLoop, calls=%fused_computation | loop fusion | flops 73728 | bytes 196608 | tf_op jit(solution)/shard_map/convert_element_type | solution.py:505
Async XLA Ops:
  0.0 7.4 %copy-start.2 = (bf16[4,64,512]{2,1,0:T(8,128)(2,1)S(1)}, bf16[4,64,512]{2,1,0:T(8,128)(2,1)}, u32[]{:S(2)}) copy-start(bf16[4,64,512]{2,1,0:T(8,128)(2,1)} %gk_ref.1) | copy-start | bytes 786436
  0.0 7.4 %copy-start.1 = (bf16[1,512,512]{2,1,0:T(8,128)(2,1)S(1)}, bf16[1,512,512]{2,1,0:T(8,128)(2,1)}, u32[]{:S(2)}) copy-start(bf16[1,512,512]{2,1,0:T(8,128)(2,1)} %pk_ref.1) | copy-start | bytes 1572868
  0.0 7.4 %copy-start = (bf16[3072,1024]{1,0:T(8,128)(2,1)S(1)}, bf16[3072,1024]{1,0:T(8,128)(2,1)}, u32[]{:S(2)}) copy-start(bf16[3072,1024]{1,0:T(8,128)(2,1)} %wq_ref.1) | copy-start | bytes 18874372
  0.0 3.2 %collective-permute-start = (bf16[4,4,1536]{2,1,0:T(4,128)(2,1)}, bf16[4,4,1536]{2,1,0:T(4,128)(2,1)S(1)}, u32[]{:S(2)}, u32[]{:S(2)}) collective-permute-start(bf16[4,4,1536]{2,1,0:T(4,128)(2,1)} %hidden.1), channel_id=1, source_target_pairs={{0,1},{1,0},{2,3},{3,2},{4,5},{5,4},{6,7},{7,6},{8,9},{9,8},{10,11... | collective-permute-start | bytes 147464 | tf_op jit(solution)/shard_map/ppermute | solution.py:39
  0.5 6.2 %collective-permute-start.2 = (bf16[4,4,1536]{2,1,0:T(4,128)(2,1)}, bf16[4,4,1536]{2,1,0:T(4,128)(2,1)S(1)}, u32[]{:S(2)}, u32[]{:S(2)}) collective-permute-start(bf16[4,4,1536]{2,1,0:T(4,128)(2,1)} %hidden.1), channel_id=1, source_target_pairs={{0,3},{1,2},{2,1},{3,0},{4,7},{5,6},{6,5},{7,4},{8,11},{9,10},{10,... | collective-permute-start | bytes 147464 | tf_op jit(solution)/shard_map/ppermute | solution.py:39
  3.1 4.3 %collective-permute-start.1 = (bf16[4,4,1536]{2,1,0:T(4,128)(2,1)}, bf16[4,4,1536]{2,1,0:T(4,128)(2,1)S(1)}, u32[]{:S(2)}, u32[]{:S(2)}) collective-permute-start(bf16[4,4,1536]{2,1,0:T(4,128)(2,1)} %hidden.1), channel_id=1, source_target_pairs={{0,2},{1,3},{2,0},{3,1},{4,6},{5,7},{6,4},{7,5},{8,10},{9,11},{10,... | collective-permute-start | bytes 147464 | tf_op jit(solution)/shard_map/ppermute | solution.py:39
  9.6 4.2 %collective-permute-start.3 = (bf16[144,128]{1,0:T(8,128)(2,1)S(1)}, bf16[144,128]{1,0:T(8,128)(2,1)S(1)}, u32[]{:S(2)}, u32[]{:S(2)}) collective-permute-start(bf16[144,128]{1,0:T(8,128)(2,1)S(1)} %get-tuple-element.31), channel_id=1, source_target_pairs={{0,2},{2,0},{4,6},{6,4},{8,10},{10,8},{12,14},{14,12},{16,18},{18,... | collective-permute-start | bytes 110600 | tf_op jit(solution)/shard_map/ppermute | solution.py:29
  14.4 1.2 %collective-permute-start.4 = (bf16[4,4,1536]{2,1,0:T(4,128)(2,1)S(1)}, bf16[4,4,1536]{2,1,0:T(4,128)(2,1)S(1)}, u32[]{:S(2)}, u32[]{:S(2)}) collective-permute-start(bf16[4,4,1536]{2,1,0:T(4,128)(2,1)S(1)} %get-tuple-element.34), channel_id=1, source_target_pairs={{0,1},{1,0},{2,3},{3,2},{4,5},{5,4},{6,7},{7,6},{8,9},{9,8},{10,11... | collective-permute-start | bytes 147464 | tf_op jit(solution)/shard_map/ppermute | solution.py:39

commit v5 on v4

--- a/solution.py
+++ b/solution.py
@@ -96,9 +96,10 @@
         sems,
     ) = refs[tp - 1 :]
     rows = steps * own
-    quarters = 4
+    chunks = 6
     blocks = pv.shape[0]
     half_len = blocks * history
+    free = half_len // 2
     device = lax.axis_index("req")
     request = device // 2
     parity = device % 2
@@ -111,9 +112,9 @@
     ]
     old = blocks + own
     large = [(pv, values_s.at[pl.ds(0, blocks)]), (gv, values_s.at[pl.ds(blocks, own)])]
-    for source, target in ((wk, wk_s), (wv, wv_s)):
-        size = source.shape[0] // quarters
-        for n in range(quarters):
+    for source, target in ((wv, wv_s), (wk, wk_s)):
+        size = source.shape[0] // chunks
+        for n in range(chunks):
             place = pl.ds(n * size, size)
             large.append((source.at[place], target.at[place]))
     copies = [
@@ -170,12 +171,13 @@
         ancestors[s] = jnp.where(row_step >= s, at, -1)
     origin = parent_of(0, at)
 
-    place = parity * half_len + lax.broadcasted_iota(jnp.int32, (half_len, lanes), 0)
-    bias_ref[pl.ds(0, half_len), :] = jnp.where(place < length, 0.0, masked_score)
+    place = lax.broadcasted_iota(jnp.int32, (half_len - free, lanes), 0)
+    place = parity * half_len + free + place
+    bias_ref[pl.ds(0, half_len - free), :] = jnp.where(place < length, 0.0, masked_score)
     for n in range(own):
         seen = jnp.where(origin == parity * own + n, 0.0, masked_score)
         for c in range(0, history, 8):
-            bias_ref[pl.ds(half_len + n * history + c, 8), :] = seen
+            bias_ref[pl.ds(half_len - free + n * history + c, 8), :] = seen
     sublane = lax.broadcasted_iota(jnp.int32, (8, lanes), 0)
     for c in range(0, rows, 8):
         seen = jnp.full((8, lanes), masked_score, jnp.float32)
@@ -184,14 +186,14 @@
                 ancestors[s] == parity * own + remainder(c + sublane, own)
             )
             seen = jnp.where(hit, 0.0, seen)
-        bias_ref[pl.ds(old * history + c, 8), :] = seen
+        bias_ref[pl.ds(old * history - free + c, 8), :] = seen
 
     for copy in large[:2]:
         copy.wait()
     values_ref[:, pl.ds(0, old * history)] = values_s[...].reshape(old * history, kv * HD).T
 
     def project(w_s, copies):
-        size = w_s.shape[0] // quarters
+        size = w_s.shape[0] // chunks
         out = jnp.zeros((rows, kv * HD), jnp.float32)
         for n, copy in enumerate(copies):
             place = pl.ds(n * size, size)
@@ -199,15 +201,15 @@
             out += jnp.dot(xn_ref[:, place], w_s[place], preferred_element_type=jnp.float32)
         return out
 
-    fresh = project(wk_s, large[2 : 2 + quarters])
-    for g in range(kv):
-        cols = pl.ds(g * HD, HD)
-        new_keys_ref[:, cols] = rotate(fresh[:, g * HD : (g + 1) * HD], key_cosine, key_sine)
-    fresh = project(wv_s, large[2 + quarters :]) * scale
+    fresh = project(wv_s, large[2 : 2 + chunks]) * scale
     fresh = jnp.concatenate(
         [fresh, jnp.zeros((HD - rows, kv * HD), jnp.float32)], axis=0
     ).astype(jnp.bfloat16)
     values_ref[:, pl.ds(old * history, HD)] = fresh.T
+    fresh = project(wk_s, large[2 + chunks :])
+    for g in range(kv):
+        cols = pl.ds(g * HD, HD)
+        new_keys_ref[:, cols] = rotate(fresh[:, g * HD : (g + 1) * HD], key_cosine, key_sine)
 
 
 def attend_kernel(
@@ -223,26 +225,37 @@
     wq_ref,
     pk_ref,
     gk_ref,
+    w_out,
     *refs,
 ):
     steps, own, tp, kv, group, packed = sizes
-    pieces = refs[:tp]
-    kept_ref, kept_lse_ref, sent_ref, x_s, xn_s = refs[tp:]
+    pieces = refs[:tp][::-1]
+    kept_ref, kept_lse_ref, sent_ref, w_out_ref, x_s, xn_s, sems = refs[tp:]
     rows = steps * own
     part = pieces[0].shape[-1]
     packs = kv // packed
     each = packed * group
     size = each * HD
     lanes = each * 2 * rows
-    keys_count = bias_ref.shape[0]
     keys_space = values_ref.shape[1]
+    keys_count = keys_space - HD + rows
+    free = keys_count - bias_ref.shape[0]
     lane = lax.broadcasted_iota(jnp.int32, (HD, lanes), 1)
     owner = quotient(remainder(lane, lanes // 2), group * rows)
     pad = jnp.zeros((keys_space - keys_count, lanes), jnp.bfloat16)
 
+    me_tp = lax.axis_index("tp")
+    copies = []
+    for d in range(1, tp):
+        place = pl.ds(pl.multiple_of((me_tp ^ d) * part, HD), part)
+        copies.append(
+            pltpu.make_async_copy(w_out.at[:, place], w_out_ref.at[d - 1], sems.at[d - 1])
+        )
+    for copy in copies:
+        copy.start()
+
     xn_s[pl.ds(0, rows), :] = xn_ref[...]
     scale = lay_out(pieces, gain_ref, x_s, xn_s, rows)
-    me_tp = lax.axis_index("tp")
     product = jnp.zeros((2 * rows, kv * group * HD), jnp.float32)
     for t in range(tp):
         place = pl.ds(pl.multiple_of((me_tp ^ t) * part, HD), part)
@@ -271,10 +284,8 @@
             ],
             axis=0,
         )
-        scores.append(
-            jnp.dot(keys, q.astype(jnp.bfloat16), preferred_element_type=jnp.float32)
-            + bias_ref[...]
-        )
+        score = jnp.dot(keys, q.astype(jnp.bfloat16), preferred_element_type=jnp.float32)
+        scores.append(jnp.concatenate([score[:free], score[free:] + bias_ref[...]], axis=0))
     tops = [jnp.max(x, axis=0, keepdims=True) for x in scores]
     powers = [jnp.exp(x - top) for x, top in zip(scores, tops)]
     totals = [jnp.sum(x, axis=0, keepdims=True) for x in powers]
@@ -316,28 +327,24 @@
         terms = jnp.where(sublane == n, term, terms)
         rest = rest - term
     sent_ref[pl.ds(HD, rows), :] = terms.astype(jnp.bfloat16)
-
-
-def fetch_kernel(kept_lse_ref, w_out, kept_lse_out, w_out_ref, sems):
-    copies = []
-    tp = w_out_ref.shape[0]
-    part = w_out_ref.shape[-1]
-    me_tp = lax.axis_index("tp")
-    for d in range(tp):
-        place = pl.ds(pl.multiple_of((me_tp ^ d) * part, HD), part)
-        copies.append(pltpu.make_async_copy(w_out.at[:, place], w_out_ref.at[d], sems.at[d]))
-    for copy in copies:
-        copy.start()
-    kept_lse_out[...] = kept_lse_ref[...]
     for copy in copies:
         copy.wait()
 
 
-def multiply_out(sizes, ctx, w_out_ref, d, out_ref):
+def fetch_kernel(kept_lse_ref, w_out, kept_lse_out, w_out_ref, sem):
+    part = w_out_ref.shape[-1]
+    place = pl.ds(pl.multiple_of(lax.axis_index("tp") * part, HD), part)
+    copy = pltpu.make_async_copy(w_out.at[:, place], w_out_ref.at[0], sem.at[0])
+    copy.start()
+    kept_lse_out[...] = kept_lse_ref[...]
+    copy.wait()
+
+
+def multiply_out(sizes, ctx, w_out_ref, out_ref):
     steps, own, chunk = sizes
     for lower in range(0, out_ref.shape[-1], chunk):
         cols = pl.ds(lower, chunk)
-        out = jnp.dot(ctx, w_out_ref[d, :, cols], preferred_element_type=jnp.float32)
+        out = jnp.dot(ctx, w_out_ref[:, cols], preferred_element_type=jnp.float32)
         for s in range(steps):
             out_ref[s, :, cols] = out[s * own : (s + 1) * own].astype(out_ref.dtype)
 
@@ -357,11 +364,11 @@
     ctx = jnp.concatenate([ctx[h * rows : (h + 1) * rows] for h in range(heads)], axis=1)
     ctx_ref[...] = ctx
     for d in range(1, tp):
-        multiply_out((steps, own, chunk), ctx, w_out_ref, d, outs[d - 1])
+        multiply_out((steps, own, chunk), ctx, w_out_ref.at[d - 1], outs[d - 1])
 
 
 def project_own_kernel(sizes, ctx_ref, w_out_ref, out_ref):
-    multiply_out(sizes, ctx_ref[...], w_out_ref, 0, out_ref)
+    multiply_out(sizes, ctx_ref[...], w_out_ref.at[0], out_ref)
 
 
 def body(
@@ -415,7 +422,7 @@
             jax.ShapeDtypeStruct((kv * HD, old + HD), bf16),
             jax.ShapeDtypeStruct((HD // 2, lanes), f32),
             jax.ShapeDtypeStruct((HD // 2, lanes), f32),
-            jax.ShapeDtypeStruct((old + rows, lanes), f32),
+            jax.ShapeDtypeStruct((old + rows - prompt_keys.shape[1] // 2, lanes), f32),
         ),
         in_specs=[hbm] * 8 + [vmem] * (tp - 1),
         out_specs=(vmem,) * 8,
@@ -427,7 +434,7 @@
             pltpu.VMEM(w_key.shape, bf16),
             pltpu.VMEM(w_value.shape, bf16),
             pltpu.VMEM((blocks + own, history, kv * HD), bf16),
-            pltpu.SemaphoreType.DMA((16,)),
+            pltpu.SemaphoreType.DMA((18,)),
         ],
         compiler_params=params,
         name="load",
@@ -448,22 +455,24 @@
         *near_pieces,
     )
 
-    kept, kept_lse, sent = pl.pallas_call(
+    kept, kept_lse, sent, w_out_far = pl.pallas_call(
         functools.partial(attend_kernel, (steps, own, tp, kv, group, packed)),
         out_shape=(
             jax.ShapeDtypeStruct((HD, heads * rows), f32),
             jax.ShapeDtypeStruct((8, heads * rows), f32),
             jax.ShapeDtypeStruct((HD + rows, heads * rows), bf16),
+            jax.ShapeDtypeStruct((tp - 1, heads * HD, part), bf16),
         ),
-        in_specs=[vmem] * (11 + tp),
-        out_specs=(vmem,) * 3,
+        in_specs=[vmem] * 11 + [hbm] + [vmem] * tp,
+        out_specs=(vmem,) * 4,
         scratch_shapes=[
             pltpu.VMEM((tp, rows, part), f32),
             pltpu.VMEM((2 * rows, width), bf16),
+            pltpu.SemaphoreType.DMA((tp - 1,)),
         ],
         compiler_params=params,
         name="attend",
-    )(*loaded, in_vmem(w_query), in_vmem(prompt_keys), in_vmem(gen_keys), *far_pieces)
+    )(*loaded, in_vmem(w_query), in_vmem(prompt_keys), in_vmem(gen_keys), in_hbm(w_out), *far_pieces[::-1])
 
     got = permute_by(sent, "req", 1)
     kept_lse, w_out_near = pl.pallas_call(
@@ -474,7 +483,7 @@
         ),
         in_specs=[vmem, hbm],
         out_specs=(vmem, vmem),
-        scratch_shapes=[pltpu.SemaphoreType.DMA((tp,))],
+        scratch_shapes=[pltpu.SemaphoreType.DMA((1,))],
         compiler_params=params,
         name="fetch",
     )(kept_lse, in_hbm(w_out))
@@ -490,7 +499,7 @@
         out_specs=(vmem,) * tp,
         compiler_params=params,
         name="project",
-    )(kept, kept_lse, got, w_out_near)
+    )(kept, kept_lse, got, w_out_far)
     sums = [across(x, 0, t + 1) for t, x in enumerate(sums)]
     total = pl.pallas_call(
         functools.partial(project_own_kernel, (steps, own, chunk)),

time: 16.4 us -> 17.6 us (1.073)
  Pallas kernels: 9.6 us -> 10.3 us
  waiting for transfers between devices: 1.45 us -> 1.83 us
    pallas_call x1, Pallas kernels: 2.12 us -> 3.79 us  [body(): pl.pallas_call(functools.partial(attend_kernel, (steps, own, tp, kv, grou...]
    pallas_call x1, Pallas kernels: 2.86 us -> 1.9 us  [body(): pl.pallas_call(fetch_kernel, out_shape=(jax.ShapeDtypeStruct((8, heads *...]
    ppermute x1, waiting for transfers between devices: 0.01 us -> 0.67 us  [permute_by(): return lax.ppermute(value, axis, pairs)]
    ppermute x4, waiting for transfers between devices: 1.45 us -> 1.16 us  [across(): return lax.ppermute(value, ('req', 'tp'), pairs)]
  transfers between devices with their start and end apart: 5 -> 5, of which waited for: 2 -> 3; matrix products, arithmetic and copies ran while one was open for 0% -> 0% of each run, Pallas kernels for 42% -> 34%
where the time goes in v5:
time: 17.6 us; the launch traced here: 17.4 us
  Pallas kernels  10.3 us (59%)
  starting transfers between devices  4.61 us (26%)
  waiting for transfers between devices  1.83 us (10%)
  other arithmetic  0.65 us (4%)
    pallas_call x1, Pallas kernels, body(): pl.pallas_call(functools.partial(attend_kernel, (steps, own, tp, kv, grou...  3.79 us
    pallas_call x1, Pallas kernels, body(): pl.pallas_call(functools.partial(load_kernel, (steps, own, tp, kv, group,...  3.46 us
    ppermute x4, starting transfers between devices, across(): return lax.ppermute(value, ('req', 'tp'), pairs)  3.16 us
    pallas_call x1, Pallas kernels, body(): pl.pallas_call(fetch_kernel, out_shape=(jax.ShapeDtypeStruct((8, heads *...  1.9 us
    ppermute x1, starting transfers between devices, permute_by(): return lax.ppermute(value, axis, pairs)  1.45 us
    ppermute x4, waiting for transfers between devices, across(): return lax.ppermute(value, ('req', 'tp'), pairs)  1.16 us
    ppermute x1, waiting for transfers between devices, permute_by(): return lax.ppermute(value, axis, pairs)  0.67 us
    convert_element_type x1, other arithmetic, body(): return total.astype(bf16)  0.65 us
  transfers between devices with their start and end apart: 5, of which 3 were waited for; matrix products, arithmetic and copies ran while one was open for 0% of the time, Pallas kernels for 34%

profile of v5, /device:TPU:0, one launch (start us, length us, event | category | flops | bytes accessed | tf_op | source)
XLA Modules:
  0.0 17.4 jit_solution(1148001577543849026)
XLA Ops:
  0.0 0.0 copy-start.2
  0.0 0.0 copy-start.1
  0.0 0.0 copy-start
  0.0 0.5 %collective-permute-start = (bf16[4,4,1536]{2,1,0:T(4,128)(2,1)}, bf16[4,4,1536]{2,1,0:T(4,128)(2,1)S(1)}, u32[]{:S(2)}, u32[]{:S(2)}) collective-permute-start(bf16[4,4,1536]{2,1,0:T(4,128)(2,1)} %hidden.1), channel_id=1, source_target_pairs={{0,1},{1,0},{2,3},{3,2},{4,5},{5,4},{6,7},{7,6},{8,9},{9,8},{10,11... | collective-permute-start | bytes 147464 | tf_op jit(solution)/shard_map/ppermute | solution.py:39
  0.5 2.6 %collective-permute-start.2 = (bf16[4,4,1536]{2,1,0:T(4,128)(2,1)}, bf16[4,4,1536]{2,1,0:T(4,128)(2,1)S(1)}, u32[]{:S(2)}, u32[]{:S(2)}) collective-permute-start(bf16[4,4,1536]{2,1,0:T(4,128)(2,1)} %hidden.1), channel_id=1, source_target_pairs={{0,2},{1,3},{2,0},{3,1},{4,6},{5,7},{6,4},{7,5},{8,10},{9,11},{10,... | collective-permute-start | bytes 147464 | tf_op jit(solution)/shard_map/ppermute | solution.py:39
  3.1 0.1 collective-permute-start.1
  3.2 0.0 collective-permute-done.refs_0_
  3.2 3.5 %load.1 = (f32[1,3072]{1,0:T(1,128)S(1)}, bf16[16,3072]{1,0:T(8,128)(2,1)S(1)}, f32[16,128]{1,0:T(8,128)S(1)}, bf16[16,512]{1,0:T(8,128)(2,1)S(1)}, bf16[512,896...) custom-call(s32[8]{0:T(128)} %lengths.1, s32[4,64]{1,0:T(4,128)} %parents.1, ...), custom_call_target="tpu_custom_call" | custom-call | tf_op jit(solution)/shard_map/load/pallas_call | solution.py:415
  6.6 0.0 collective-permute-done.2.refs_1_
  6.6 0.4 %collective-permute-done.1.refs_0_ = bf16[4,4,1536]{2,1,0:T(4,128)(2,1)S(1)} collective-permute-done((bf16[4,4,1536]{2,1,0:T(4,128)(2,1)}, bf16[4,4,1536]{2,1,0:T(4,128)(2,1)S(1)}, u32[]{:S(2)}, u32[]{:S(2)}) %collective-permute-start.1) | collective-permute-done | bytes 49184 | tf_op jit(solution)/shard_map/ppermute | solution.py:39
  7.1 0.0 copy-done.2
  7.1 0.0 copy-done.1
  7.1 0.0 copy-done
  7.1 3.8 %attend.1 = (f32[128,128]{1,0:T(8,128)S(1)}, f32[8,128]{1,0:T(8,128)S(1)}, bf16[144,128]{1,0:T(8,128)(2,1)S(1)}, bf16[1,1024,1536]{2,1,0:T(8,128)(2,1)S(1)}) custom-call(f32[1,3072]{1,0:T(1,128)S(1)} %get-tuple-element.21.gain_ref, bf16[16,3072]{1,0:T(8,128)(2,1)S(1)} %get-tuple-element.22.xn_ref, f32[16,128]{1,0:T(8,128)S(1)} %get-tuple-element.23.scale_ref, ...), custom_call_target="tpu_custom_call" | custom-call | tf_op jit(solution)/shard_map/attend/pallas_call | solution.py:458
  10.9 1.4 %collective-permute-start.3 = (bf16[144,128]{1,0:T(8,128)(2,1)S(1)}, bf16[144,128]{1,0:T(8,128)(2,1)S(1)}, u32[]{:S(2)}, u32[]{:S(2)}) collective-permute-start(bf16[144,128]{1,0:T(8,128)(2,1)S(1)} %get-tuple-element.32), channel_id=1, source_target_pairs={{0,2},{2,0},{4,6},{6,4},{8,10},{10,8},{12,14},{14,12},{16,18},{18,... | collective-permute-start | bytes 110600 | tf_op jit(solution)/shard_map/ppermute | solution.py:29
  12.3 1.9 %fetch.1 = (f32[8,128]{1,0:T(8,128)S(1)}, bf16[2,1024,1536]{2,1,0:T(8,128)(2,1)S(1)}) custom-call(f32[8,128]{1,0:T(8,128)S(1)} %get-tuple-element.30.kept_lse_ref, bf16[1024,3072]{1,0:T(8,128)(2,1)} %w_out.3), custom_call_target="tpu_custom_call" | custom-call | tf_op jit(solution)/shard_map/fetch/pallas_call | solution.py:478
  14.2 0.7 %collective-permute-done.3.got_ref = bf16[144,128]{1,0:T(8,128)(2,1)S(1)} collective-permute-done((bf16[144,128]{1,0:T(8,128)(2,1)S(1)}, bf16[144,128]{1,0:T(8,128)(2,1)S(1)}, u32[]{:S(2)}, u32[]{:S(2)}) %collective-permute-start.3) | collective-permute-done | bytes 36896 | tf_op jit(solution)/shard_map/ppermute | solution.py:29
  14.9 0.6 %project.1 = (bf16[16,1024]{1,0:T(8,128)(2,1)S(1)}, bf16[4,4,1536]{2,1,0:T(4,128)(2,1)S(1)}) custom-call(f32[128,128]{1,0:T(8,128)S(1)} %get-tuple-element.29.kept_ref, f32[8,128]{1,0:T(8,128)S(1)} %get-tuple-element.31.kept_lse_ref, bf16[144,128]{1,0:T(8,128)(2,1)S(1)} %collective-permute-done.3.got_ref, bf16[1,1024,1536]{2,1,0:T(8,128)(2,1)S(1)} %get-tuple-element.33.w_out_ref), custom_call_target="tpu_custom_call" | custom-call | tf_op jit(solution)/shard_map/project/pallas_call | solution.py:492
  15.5 0.0 collective-permute-start.4
  15.5 0.5 %project_own.1 = f32[4,4,1536]{2,1,0:T(4,128)S(1)} custom-call(bf16[16,1024]{1,0:T(8,128)(2,1)S(1)} %get-tuple-element.34.ctx_ref, bf16[2,1024,1536]{2,1,0:T(8,128)(2,1)S(1)} %get-tuple-element.35.w_out_ref), custom_call_target="tpu_custom_call" | custom-call | tf_op jit(solution)/shard_map/project_own/pallas_call | solution.py:504
  16.0 0.7 %collective-permute-done.4 = bf16[4,4,1536]{2,1,0:T(4,128)(2,1)S(1)} collective-permute-done((bf16[4,4,1536]{2,1,0:T(4,128)(2,1)S(1)}, bf16[4,4,1536]{2,1,0:T(4,128)(2,1)S(1)}, u32[]{:S(2)}, u32[]{:S(2)}) %collective-permute-start.4) | collective-permute-done | bytes 49184 | tf_op jit(solution)/shard_map/ppermute | solution.py:39
  16.7 0.6 %add_convert_fusion = bf16[4,4,1536]{2,1,0:T(4,128)(2,1)} fusion(f32[4,4,1536]{2,1,0:T(4,128)S(1)} %project_own.1, bf16[4,4,1536]{2,1,0:T(4,128)(2,1)S(1)} %collective-permute-done.4), kind=kLoop, calls=%fused_computation | loop fusion | flops 73728 | bytes 196608 | tf_op jit(solution)/shard_map/convert_element_type | solution.py:514
Async XLA Ops:
  0.0 7.1 %copy-start.2 = (bf16[4,64,512]{2,1,0:T(8,128)(2,1)S(1)}, bf16[4,64,512]{2,1,0:T(8,128)(2,1)}, u32[]{:S(2)}) copy-start(bf16[4,64,512]{2,1,0:T(8,128)(2,1)} %gk_ref.1) | copy-start | bytes 786436
  0.0 7.1 %copy-start.1 = (bf16[1,512,512]{2,1,0:T(8,128)(2,1)S(1)}, bf16[1,512,512]{2,1,0:T(8,128)(2,1)}, u32[]{:S(2)}) copy-start(bf16[1,512,512]{2,1,0:T(8,128)(2,1)} %pk_ref.1) | copy-start | bytes 1572868
  0.0 7.1 %copy-start = (bf16[3072,1024]{1,0:T(8,128)(2,1)S(1)}, bf16[3072,1024]{1,0:T(8,128)(2,1)}, u32[]{:S(2)}) copy-start(bf16[3072,1024]{1,0:T(8,128)(2,1)} %wq_ref.1) | copy-start | bytes 18874372
  0.0 3.2 %collective-permute-start = (bf16[4,4,1536]{2,1,0:T(4,128)(2,1)}, bf16[4,4,1536]{2,1,0:T(4,128)(2,1)S(1)}, u32[]{:S(2)}, u32[]{:S(2)}) collective-permute-start(bf16[4,4,1536]{2,1,0:T(4,128)(2,1)} %hidden.1), channel_id=1, source_target_pairs={{0,1},{1,0},{2,3},{3,2},{4,5},{5,4},{6,7},{7,6},{8,9},{9,8},{10,11... | collective-permute-start | bytes 147464 | tf_op jit(solution)/shard_map/ppermute | solution.py:39
  0.5 6.1 %collective-permute-start.2 = (bf16[4,4,1536]{2,1,0:T(4,128)(2,1)}, bf16[4,4,1536]{2,1,0:T(4,128)(2,1)S(1)}, u32[]{:S(2)}, u32[]{:S(2)}) collective-permute-start(bf16[4,4,1536]{2,1,0:T(4,128)(2,1)} %hidden.1), channel_id=1, source_target_pairs={{0,2},{1,3},{2,0},{3,1},{4,6},{5,7},{6,4},{7,5},{8,10},{9,11},{10,... | collective-permute-start | bytes 147464 | tf_op jit(solution)/shard_map/ppermute | solution.py:39
  3.1 4.0 %collective-permute-start.1 = (bf16[4,4,1536]{2,1,0:T(4,128)(2,1)}, bf16[4,4,1536]{2,1,0:T(4,128)(2,1)S(1)}, u32[]{:S(2)}, u32[]{:S(2)}) collective-permute-start(bf16[4,4,1536]{2,1,0:T(4,128)(2,1)} %hidden.1), channel_id=1, source_target_pairs={{0,3},{1,2},{2,1},{3,0},{4,7},{5,6},{6,5},{7,4},{8,11},{9,10},{10,... | collective-permute-start | bytes 147464 | tf_op jit(solution)/shard_map/ppermute | solution.py:39
  10.9 4.0 %collective-permute-start.3 = (bf16[144,128]{1,0:T(8,128)(2,1)S(1)}, bf16[144,128]{1,0:T(8,128)(2,1)S(1)}, u32[]{:S(2)}, u32[]{:S(2)}) collective-permute-start(bf16[144,128]{1,0:T(8,128)(2,1)S(1)} %get-tuple-element.32), channel_id=1, source_target_pairs={{0,2},{2,0},{4,6},{6,4},{8,10},{10,8},{12,14},{14,12},{16,18},{18,... | collective-permute-start | bytes 110600 | tf_op jit(solution)/shard_map/ppermute | solution.py:29
  15.5 1.2 %collective-permute-start.4 = (bf16[4,4,1536]{2,1,0:T(4,128)(2,1)S(1)}, bf16[4,4,1536]{2,1,0:T(4,128)(2,1)S(1)}, u32[]{:S(2)}, u32[]{:S(2)}) collective-permute-start(bf16[4,4,1536]{2,1,0:T(4,128)(2,1)S(1)} %get-tuple-element.36), channel_id=1, source_target_pairs={{0,1},{1,0},{2,3},{3,2},{4,5},{5,4},{6,7},{7,6},{8,9},{9,8},{10,11... | collective-permute-start | bytes 147464 | tf_op jit(solution)/shard_map/ppermute | solution.py:39

commit v6 on v5

--- a/solution.py
+++ b/solution.py
@@ -225,12 +225,11 @@
     wq_ref,
     pk_ref,
     gk_ref,
-    w_out,
     *refs,
 ):
     steps, own, tp, kv, group, packed = sizes
     pieces = refs[:tp][::-1]
-    kept_ref, kept_lse_ref, sent_ref, w_out_ref, x_s, xn_s, sems = refs[tp:]
+    kept_ref, kept_lse_ref, sent_ref, x_s, xn_s = refs[tp:]
     rows = steps * own
     part = pieces[0].shape[-1]
     packs = kv // packed
@@ -244,18 +243,9 @@
     owner = quotient(remainder(lane, lanes // 2), group * rows)
     pad = jnp.zeros((keys_space - keys_count, lanes), jnp.bfloat16)
 
-    me_tp = lax.axis_index("tp")
-    copies = []
-    for d in range(1, tp):
-        place = pl.ds(pl.multiple_of((me_tp ^ d) * part, HD), part)
-        copies.append(
-            pltpu.make_async_copy(w_out.at[:, place], w_out_ref.at[d - 1], sems.at[d - 1])
-        )
-    for copy in copies:
-        copy.start()
-
     xn_s[pl.ds(0, rows), :] = xn_ref[...]
     scale = lay_out(pieces, gain_ref, x_s, xn_s, rows)
+    me_tp = lax.axis_index("tp")
     product = jnp.zeros((2 * rows, kv * group * HD), jnp.float32)
     for t in range(tp):
         place = pl.ds(pl.multiple_of((me_tp ^ t) * part, HD), part)
@@ -327,26 +317,35 @@
         terms = jnp.where(sublane == n, term, terms)
         rest = rest - term
     sent_ref[pl.ds(HD, rows), :] = terms.astype(jnp.bfloat16)
+
+
+def fetch_kernel(kept_lse_ref, w_out, kept_lse_out, w_out_ref, sems):
+    tp, depth, part = w_out_ref.shape
+    me_tp = lax.axis_index("tp")
+    copies = []
+    for d in range(1, tp):
+        cols = pl.ds(pl.multiple_of((me_tp ^ d) * part, HD), part)
+        for n in range(2):
+            rows = pl.ds(n * (depth // 2), depth // 2)
+            copies.append(
+                pltpu.make_async_copy(
+                    w_out.at[rows, cols], w_out_ref.at[d - 1, rows], sems.at[2 * d - 2 + n]
+                )
+            )
+    for copy in copies:
+        copy.start()
+    kept_lse_out[...] = kept_lse_ref[...]
     for copy in copies:
         copy.wait()
 
 
-def fetch_kernel(kept_lse_ref, w_out, kept_lse_out, w_out_ref, sem):
-    part = w_out_ref.shape[-1]
-    place = pl.ds(pl.multiple_of(lax.axis_index("tp") * part, HD), part)
-    copy = pltpu.make_async_copy(w_out.at[:, place], w_out_ref.at[0], sem.at[0])
-    copy.start()
-    kept_lse_out[...] = kept_lse_ref[...]
-    copy.wait()
-
-
-def multiply_out(sizes, ctx, w_out_ref, out_ref):
+def multiply_out(sizes, ctx, w_out_ref, first, out_ref):
     steps, own, chunk = sizes
     for lower in range(0, out_ref.shape[-1], chunk):
-        cols = pl.ds(lower, chunk)
-        out = jnp.dot(ctx, w_out_ref[:, cols], preferred_element_type=jnp.float32)
+        place = pl.ds(pl.multiple_of(first + lower, HD), chunk)
+        out = jnp.dot(ctx, w_out_ref[:, place], preferred_element_type=jnp.float32)
         for s in range(steps):
-            out_ref[s, :, cols] = out[s * own : (s + 1) * own].astype(out_ref.dtype)
+            out_ref[s, :, pl.ds(lower, chunk)] = out[s * own : (s + 1) * own].astype(out_ref.dtype)
 
 
 def project_kernel(sizes, kept_ref, kept_lse_ref, got_ref, w_out_ref, ctx_ref, *outs):
@@ -364,11 +363,12 @@
     ctx = jnp.concatenate([ctx[h * rows : (h + 1) * rows] for h in range(heads)], axis=1)
     ctx_ref[...] = ctx
     for d in range(1, tp):
-        multiply_out((steps, own, chunk), ctx, w_out_ref.at[d - 1], outs[d - 1])
+        multiply_out((steps, own, chunk), ctx, w_out_ref.at[d - 1], 0, outs[d - 1])
 
 
 def project_own_kernel(sizes, ctx_ref, w_out_ref, out_ref):
-    multiply_out(sizes, ctx_ref[...], w_out_ref.at[0], out_ref)
+    first = lax.axis_index("tp") * out_ref.shape[-1]
+    multiply_out(sizes, ctx_ref[...], w_out_ref, first, out_ref)
 
 
 def body(
@@ -455,27 +455,25 @@
         *near_pieces,
     )
 
-    kept, kept_lse, sent, w_out_far = pl.pallas_call(
+    kept, kept_lse, sent = pl.pallas_call(
         functools.partial(attend_kernel, (steps, own, tp, kv, group, packed)),
         out_shape=(
             jax.ShapeDtypeStruct((HD, heads * rows), f32),
             jax.ShapeDtypeStruct((8, heads * rows), f32),
             jax.ShapeDtypeStruct((HD + rows, heads * rows), bf16),
-            jax.ShapeDtypeStruct((tp - 1, heads * HD, part), bf16),
         ),
-        in_specs=[vmem] * 11 + [hbm] + [vmem] * tp,
-        out_specs=(vmem,) * 4,
+        in_specs=[vmem] * (11 + tp),
+        out_specs=(vmem,) * 3,
         scratch_shapes=[
             pltpu.VMEM((tp, rows, part), f32),
             pltpu.VMEM((2 * rows, width), bf16),
-            pltpu.SemaphoreType.DMA((tp - 1,)),
         ],
         compiler_params=params,
         name="attend",
-    )(*loaded, in_vmem(w_query), in_vmem(prompt_keys), in_vmem(gen_keys), in_hbm(w_out), *far_pieces[::-1])
+    )(*loaded, in_vmem(w_query), in_vmem(prompt_keys), in_vmem(gen_keys), *far_pieces[::-1])
 
     got = permute_by(sent, "req", 1)
-    kept_lse, w_out_near = pl.pallas_call(
+    kept_lse, w_out_far = pl.pallas_call(
         fetch_kernel,
         out_shape=(
             jax.ShapeDtypeStruct((8, heads * rows), f32),
@@ -483,7 +481,7 @@
         ),
         in_specs=[vmem, hbm],
         out_specs=(vmem, vmem),
-        scratch_shapes=[pltpu.SemaphoreType.DMA((1,))],
+        scratch_shapes=[pltpu.SemaphoreType.DMA((2 * tp - 2,))],
         compiler_params=params,
         name="fetch",
     )(kept_lse, in_hbm(w_out))
@@ -508,7 +506,7 @@
         out_specs=vmem,
         compiler_params=params,
         name="project_own",
-    )(ctx, w_out_near)
+    )(ctx, in_vmem(w_out))
     for x in sums:
         total = total + x.astype(f32)
     return total.astype(bf16)

time: 17.6 us -> 15.9 us (0.903)
  Pallas kernels: 10.3 us -> 8.72 us
  waiting for transfers between devices: 1.83 us -> 1.65 us
    pallas_call x1, Pallas kernels: 3.79 us -> 2.1 us  [body(): pl.pallas_call(functools.partial(attend_kernel, (steps, own, tp, kv, grou...]
  transfers between devices with their start and end apart: 5 -> 5, of which waited for: 3 -> 3; matrix products, arithmetic and copies ran while one was open for 0% -> 0% of each run, Pallas kernels for 34% -> 38%
where the time goes in v6:
time: 15.9 us; the launch traced here: 15.7 us
  Pallas kernels  8.72 us (55%)
  starting transfers between devices  4.6 us (29%)
  waiting for transfers between devices  1.65 us (10%)
  other arithmetic  0.65 us (4%)
    pallas_call x1, Pallas kernels, body(): pl.pallas_call(functools.partial(load_kernel, (steps, own, tp, kv, group,...  3.46 us
    ppermute x4, starting transfers between devices, across(): return lax.ppermute(value, ('req', 'tp'), pairs)  3.16 us
    pallas_call x1, Pallas kernels, body(): pl.pallas_call(functools.partial(attend_kernel, (steps, own, tp, kv, grou...  2.1 us
    pallas_call x1, Pallas kernels, body(): pl.pallas_call(fetch_kernel, out_shape=(jax.ShapeDtypeStruct((8, heads *...  2.05 us
    ppermute x1, starting transfers between devices, permute_by(): return lax.ppermute(value, axis, pairs)  1.45 us
    ppermute x4, waiting for transfers between devices, across(): return lax.ppermute(value, ('req', 'tp'), pairs)  1.13 us
    convert_element_type x1, other arithmetic, body(): return total.astype(bf16)  0.65 us
    pallas_call x1, Pallas kernels, body(): pl.pallas_call(functools.partial(project_kernel, (steps, own, tp, heads,...  0.59 us
  transfers between devices with their start and end apart: 5, of which 3 were waited for; matrix products, arithmetic and copies ran while one was open for 0% of the time, Pallas kernels for 38%

profile of v6, /device:TPU:0, one launch (start us, length us, event | category | flops | bytes accessed | tf_op | source)
XLA Modules:
  0.0 15.7 jit_solution(1476793805888502175)
XLA Ops:
  0.0 0.0 copy-start.2
  0.0 0.0 copy-start.1
  0.0 0.5 %collective-permute-start = (bf16[4,4,1536]{2,1,0:T(4,128)(2,1)}, bf16[4,4,1536]{2,1,0:T(4,128)(2,1)S(1)}, u32[]{:S(2)}, u32[]{:S(2)}) collective-permute-start(bf16[4,4,1536]{2,1,0:T(4,128)(2,1)} %hidden.1), channel_id=1, source_target_pairs={{0,1},{1,0},{2,3},{3,2},{4,5},{5,4},{6,7},{7,6},{8,9},{9,8},{10,11... | collective-permute-start | bytes 147464 | tf_op jit(solution)/shard_map/ppermute | solution.py:39
  0.5 2.6 %collective-permute-start.2 = (bf16[4,4,1536]{2,1,0:T(4,128)(2,1)}, bf16[4,4,1536]{2,1,0:T(4,128)(2,1)S(1)}, u32[]{:S(2)}, u32[]{:S(2)}) collective-permute-start(bf16[4,4,1536]{2,1,0:T(4,128)(2,1)} %hidden.1), channel_id=1, source_target_pairs={{0,2},{1,3},{2,0},{3,1},{4,6},{5,7},{6,4},{7,5},{8,10},{9,11},{10,... | collective-permute-start | bytes 147464 | tf_op jit(solution)/shard_map/ppermute | solution.py:39
  3.1 0.1 collective-permute-start.1
  3.2 0.0 collective-permute-done.refs_0_
  3.2 3.5 %load.1 = (f32[1,3072]{1,0:T(1,128)S(1)}, bf16[16,3072]{1,0:T(8,128)(2,1)S(1)}, f32[16,128]{1,0:T(8,128)S(1)}, bf16[16,512]{1,0:T(8,128)(2,1)S(1)}, bf16[512,896...) custom-call(s32[8]{0:T(128)} %lengths.1, s32[4,64]{1,0:T(4,128)} %parents.1, ...), custom_call_target="tpu_custom_call" | custom-call | tf_op jit(solution)/shard_map/load/pallas_call | solution.py:415
  6.6 0.0 collective-permute-done.2.refs_1_
  6.6 0.4 %collective-permute-done.1.refs_0_ = bf16[4,4,1536]{2,1,0:T(4,128)(2,1)S(1)} collective-permute-done((bf16[4,4,1536]{2,1,0:T(4,128)(2,1)}, bf16[4,4,1536]{2,1,0:T(4,128)(2,1)S(1)}, u32[]{:S(2)}, u32[]{:S(2)}) %collective-permute-start.1) | collective-permute-done | bytes 49184 | tf_op jit(solution)/shard_map/ppermute | solution.py:39
  7.1 0.0 copy-done.2
  7.1 0.0 copy-done.1
  7.1 0.0 copy-done
  7.1 0.0 slice-start
  7.1 2.1 %attend.1 = (f32[128,128]{1,0:T(8,128)S(1)}, f32[8,128]{1,0:T(8,128)S(1)}, bf16[144,128]{1,0:T(8,128)(2,1)S(1)}) custom-call(f32[1,3072]{1,0:T(1,128)S(1)} %get-tuple-element.20.gain_ref, bf16[16,3072]{1,0:T(8,128)(2,1)S(1)} %get-tuple-element.21.xn_ref, f32[16,128]{1,0:T(8,128)S(1)} %get-tuple-element.22.scale_ref, ...), custom_call_target="tpu_custom_call" | custom-call | tf_op jit(solution)/shard_map/attend/pallas_call | solution.py:458
  9.2 1.4 %collective-permute-start.3 = (bf16[144,128]{1,0:T(8,128)(2,1)S(1)}, bf16[144,128]{1,0:T(8,128)(2,1)S(1)}, u32[]{:S(2)}, u32[]{:S(2)}) collective-permute-start(bf16[144,128]{1,0:T(8,128)(2,1)S(1)} %get-tuple-element.31), channel_id=1, source_target_pairs={{0,2},{2,0},{4,6},{6,4},{8,10},{10,8},{12,14},{14,12},{16,18},{18,... | collective-permute-start | bytes 110600 | tf_op jit(solution)/shard_map/ppermute | solution.py:29
  10.7 2.0 %fetch.1 = (f32[8,128]{1,0:T(8,128)S(1)}, bf16[2,1024,1536]{2,1,0:T(8,128)(2,1)S(1)}) custom-call(f32[8,128]{1,0:T(8,128)S(1)} %get-tuple-element.29.kept_lse_ref, bf16[1024,3072]{1,0:T(8,128)(2,1)} %w_out_ref.1), custom_call_target="tpu_custom_call" | custom-call | tf_op jit(solution)/shard_map/fetch/pallas_call | solution.py:476
  12.7 0.5 %collective-permute-done.3.got_ref = bf16[144,128]{1,0:T(8,128)(2,1)S(1)} collective-permute-done((bf16[144,128]{1,0:T(8,128)(2,1)S(1)}, bf16[144,128]{1,0:T(8,128)(2,1)S(1)}, u32[]{:S(2)}, u32[]{:S(2)}) %collective-permute-start.3) | collective-permute-done | bytes 36896 | tf_op jit(solution)/shard_map/ppermute | solution.py:29
  13.2 0.6 %project.1 = (bf16[16,1024]{1,0:T(8,128)(2,1)S(1)}, bf16[4,4,1536]{2,1,0:T(4,128)(2,1)S(1)}) custom-call(f32[128,128]{1,0:T(8,128)S(1)} %get-tuple-element.28.kept_ref, f32[8,128]{1,0:T(8,128)S(1)} %get-tuple-element.30.kept_lse_ref, bf16[144,128]{1,0:T(8,128)(2,1)S(1)} %collective-permute-done.3.got_ref, bf16[2,1024,1536]{2,1,0:T(8,128)(2,1)S(1)} %get-tuple-element.32.w_out_ref), custom_call_target="tpu_custom_call" | custom-call | tf_op jit(solution)/shard_map/project/pallas_call | solution.py:490
  13.8 0.0 collective-permute-start.4
  13.8 0.0 slice-done
  13.8 0.0 slice-done.1
  13.9 0.5 %project_own.1 = f32[4,4,1536]{2,1,0:T(4,128)S(1)} custom-call(bf16[16,1024]{1,0:T(8,128)(2,1)S(1)} %get-tuple-element.33.ctx_ref, bf16[1024,3072]{1,0:T(8,128)(2,1)S(1)} %bitcast.3), custom_call_target="tpu_custom_call" | custom-call | tf_op jit(solution)/shard_map/project_own/pallas_call | solution.py:502
  14.4 0.7 %collective-permute-done.4 = bf16[4,4,1536]{2,1,0:T(4,128)(2,1)S(1)} collective-permute-done((bf16[4,4,1536]{2,1,0:T(4,128)(2,1)S(1)}, bf16[4,4,1536]{2,1,0:T(4,128)(2,1)S(1)}, u32[]{:S(2)}, u32[]{:S(2)}) %collective-permute-start.4) | collective-permute-done | bytes 49184 | tf_op jit(solution)/shard_map/ppermute | solution.py:39
  15.1 0.6 %add_convert_fusion = bf16[4,4,1536]{2,1,0:T(4,128)(2,1)} fusion(f32[4,4,1536]{2,1,0:T(4,128)S(1)} %project_own.1, bf16[4,4,1536]{2,1,0:T(4,128)(2,1)S(1)} %collective-permute-done.4), kind=kLoop, calls=%fused_computation | loop fusion | flops 73728 | bytes 196608 | tf_op jit(solution)/shard_map/convert_element_type | solution.py:512
  (3 shorter events, 0.0 us)
Async XLA Ops:
  0.0 7.1 %copy-start.2 = (bf16[4,64,512]{2,1,0:T(8,128)(2,1)S(1)}, bf16[4,64,512]{2,1,0:T(8,128)(2,1)}, u32[]{:S(2)}) copy-start(bf16[4,64,512]{2,1,0:T(8,128)(2,1)} %gk_ref.1) | copy-start | bytes 786436
  0.0 7.1 %copy-start.1 = (bf16[1,512,512]{2,1,0:T(8,128)(2,1)S(1)}, bf16[1,512,512]{2,1,0:T(8,128)(2,1)}, u32[]{:S(2)}) copy-start(bf16[1,512,512]{2,1,0:T(8,128)(2,1)} %pk_ref.1) | copy-start | bytes 1572868
  0.0 7.1 %copy-start = (bf16[3072,1024]{1,0:T(8,128)(2,1)S(1)}, bf16[3072,1024]{1,0:T(8,128)(2,1)}, u32[]{:S(2)}) copy-start(bf16[3072,1024]{1,0:T(8,128)(2,1)} %wq_ref.1) | copy-start | bytes 18874372
  0.0 3.2 %collective-permute-start = (bf16[4,4,1536]{2,1,0:T(4,128)(2,1)}, bf16[4,4,1536]{2,1,0:T(4,128)(2,1)S(1)}, u32[]{:S(2)}, u32[]{:S(2)}) collective-permute-start(bf16[4,4,1536]{2,1,0:T(4,128)(2,1)} %hidden.1), channel_id=1, source_target_pairs={{0,1},{1,0},{2,3},{3,2},{4,5},{5,4},{6,7},{7,6},{8,9},{9,8},{10,11... | collective-permute-start | bytes 147464 | tf_op jit(solution)/shard_map/ppermute | solution.py:39
  0.5 6.1 %collective-permute-start.2 = (bf16[4,4,1536]{2,1,0:T(4,128)(2,1)}, bf16[4,4,1536]{2,1,0:T(4,128)(2,1)S(1)}, u32[]{:S(2)}, u32[]{:S(2)}) collective-permute-start(bf16[4,4,1536]{2,1,0:T(4,128)(2,1)} %hidden.1), channel_id=1, source_target_pairs={{0,2},{1,3},{2,0},{3,1},{4,6},{5,7},{6,4},{7,5},{8,10},{9,11},{10,... | collective-permute-start | bytes 147464 | tf_op jit(solution)/shard_map/ppermute | solution.py:39
  3.1 4.0 %collective-permute-start.1 = (bf16[4,4,1536]{2,1,0:T(4,128)(2,1)}, bf16[4,4,1536]{2,1,0:T(4,128)(2,1)S(1)}, u32[]{:S(2)}, u32[]{:S(2)}) collective-permute-start(bf16[4,4,1536]{2,1,0:T(4,128)(2,1)} %hidden.1), channel_id=1, source_target_pairs={{0,3},{1,2},{2,1},{3,0},{4,7},{5,6},{6,5},{7,4},{8,11},{9,10},{10,... | collective-permute-start | bytes 147464 | tf_op jit(solution)/shard_map/ppermute | solution.py:39
  7.1 6.7 %slice-start = ((s8[6291456]{0:T(1024)(128)(4,1)}), s8[2097152]{0:T(1024)(128)(4,1)S(1)}, s32[]{:S(2)}) async-start(s8[6291456]{0:T(1024)(128)(4,1)} %bitcast.2), calls=%async_computation | async-start | bytes 4194304
  9.2 4.0 %collective-permute-start.3 = (bf16[144,128]{1,0:T(8,128)(2,1)S(1)}, bf16[144,128]{1,0:T(8,128)(2,1)S(1)}, u32[]{:S(2)}, u32[]{:S(2)}) collective-permute-start(bf16[144,128]{1,0:T(8,128)(2,1)S(1)} %get-tuple-element.31), channel_id=1, source_target_pairs={{0,2},{2,0},{4,6},{6,4},{8,10},{10,8},{12,14},{14,12},{16,18},{18,... | collective-permute-start | bytes 110600 | tf_op jit(solution)/shard_map/ppermute | solution.py:29
  10.7 3.2 %slice-start.1 = ((s8[6291456]{0:T(1024)(128)(4,1)}), s8[4194304]{0:T(1024)(128)(4,1)S(1)}, s32[]{:S(2)}) async-start(s8[6291456]{0:T(1024)(128)(4,1)} %bitcast.2), calls=%async_computation.1 | async-start | bytes 8388608
  13.8 1.2 %collective-permute-start.4 = (bf16[4,4,1536]{2,1,0:T(4,128)(2,1)S(1)}, bf16[4,4,1536]{2,1,0:T(4,128)(2,1)S(1)}, u32[]{:S(2)}, u32[]{:S(2)}) collective-permute-start(bf16[4,4,1536]{2,1,0:T(4,128)(2,1)S(1)} %get-tuple-element.34), channel_id=1, source_target_pairs={{0,1},{1,0},{2,3},{3,2},{4,5},{5,4},{6,7},{7,6},{8,9},{9,8},{10,11... | collective-permute-start | bytes 147464 | tf_op jit(solution)/shard_map/ppermute | solution.py:39

commit v7 on v6

--- a/solution.py
+++ b/solution.py
@@ -63,26 +63,15 @@
     return (x * cosine + pltpu.roll(x, HD // 2, 1) * sine).astype(jnp.bfloat16)
 
 
-def load_kernel(
-    sizes,
-    lengths,
-    parents,
-    gain,
-    hidden,
-    wk,
-    wv,
-    pv,
-    gv,
-    *refs,
-):
-    steps, own, tp, kv, group, history, packed = sizes
+def prepare_kernel(sizes, lengths, parents, gain, hidden, *refs):
+    steps, own, tp, group, history, half_len, packed = sizes
     pieces = refs[: tp - 1]
     (
         gain_ref,
         xn_ref,
         scale_ref,
-        new_keys_ref,
-        values_ref,
+        key_cosine_ref,
+        key_sine_ref,
         cosine_ref,
         sine_ref,
         bias_ref,
@@ -90,41 +79,23 @@
         parents_s,
         hidden_s,
         x_s,
-        wk_s,
-        wv_s,
-        values_s,
         sems,
     ) = refs[tp - 1 :]
     rows = steps * own
-    chunks = 6
-    blocks = pv.shape[0]
-    half_len = blocks * history
     free = half_len // 2
     device = lax.axis_index("req")
     request = device // 2
     parity = device % 2
 
-    small = [
-        (gain, gain_ref),
-        (hidden, hidden_s),
-        (lengths, lengths_s),
-        (parents, parents_s),
-    ]
-    old = blocks + own
-    large = [(pv, values_s.at[pl.ds(0, blocks)]), (gv, values_s.at[pl.ds(blocks, own)])]
-    for source, target in ((wv, wv_s), (wk, wk_s)):
-        size = source.shape[0] // chunks
-        for n in range(chunks):
-            place = pl.ds(n * size, size)
-            large.append((source.at[place], target.at[place]))
     copies = [
         pltpu.make_async_copy(source, target, sems.at[n])
-        for n, (source, target) in enumerate(small + large)
+        for n, (source, target) in enumerate(
+            ((gain, gain_ref), (hidden, hidden_s), (lengths, lengths_s), (parents, parents_s))
+        )
     ]
     for copy in copies:
         copy.start()
-    large = copies[len(small) :]
-    for copy in copies[: len(small)]:
+    for copy in copies:
         copy.wait()
 
     scale = lay_out((hidden_s, *pieces), gain_ref, x_s, xn_ref, 0)
@@ -142,9 +113,9 @@
     row = lax.broadcasted_iota(jnp.int32, (rows, HD), 0)
     lane = lax.broadcasted_iota(jnp.int32, (rows, HD), 1)
     angle = angles(quotient(row, own), remainder(lane, half_dim))
-    key_cosine = jnp.cos(angle) * scale
+    key_cosine_ref[...] = jnp.cos(angle) * scale
     key_sine = jnp.sin(angle) * scale
-    key_sine = jnp.where(lane < half_dim, -key_sine, key_sine)
+    key_sine_ref[...] = jnp.where(lane < half_dim, -key_sine, key_sine)
 
     lanes = packed * group * 2 * rows
     place = lax.broadcasted_iota(jnp.int32, (half_dim, lanes), 0)
@@ -186,30 +157,40 @@
                 ancestors[s] == parity * own + remainder(c + sublane, own)
             )
             seen = jnp.where(hit, 0.0, seen)
-        bias_ref[pl.ds(old * history - free + c, 8), :] = seen
-
-    for copy in large[:2]:
-        copy.wait()
-    values_ref[:, pl.ds(0, old * history)] = values_s[...].reshape(old * history, kv * HD).T
-
-    def project(w_s, copies):
-        size = w_s.shape[0] // chunks
-        out = jnp.zeros((rows, kv * HD), jnp.float32)
-        for n, copy in enumerate(copies):
-            place = pl.ds(n * size, size)
-            copy.wait()
-            out += jnp.dot(xn_ref[:, place], w_s[place], preferred_element_type=jnp.float32)
-        return out
-
-    fresh = project(wv_s, large[2 : 2 + chunks]) * scale
-    fresh = jnp.concatenate(
-        [fresh, jnp.zeros((HD - rows, kv * HD), jnp.float32)], axis=0
-    ).astype(jnp.bfloat16)
-    values_ref[:, pl.ds(old * history, HD)] = fresh.T
-    fresh = project(wk_s, large[2 + chunks :])
-    for g in range(kv):
+        bias_ref[pl.ds(half_len + own * history - free + c, 8), :] = seen
+
+
+def fresh_kernel(
+    xn_ref,
+    scale_ref,
+    key_cosine_ref,
+    key_sine_ref,
+    wk_ref,
+    wv_ref,
+    pv_ref,
+    gv_ref,
+    new_keys_ref,
+    values_ref,
+):
+    rows = xn_ref.shape[0]
+    half_len, width = pv_ref.shape[1:]
+    old = values_ref.shape[1] - HD
+    xn = xn_ref[...]
+    keys = jnp.dot(xn, wk_ref[...], preferred_element_type=jnp.float32)
+    values = jnp.dot(xn, wv_ref[...], preferred_element_type=jnp.float32)
+    values_ref[:, pl.ds(0, half_len)] = pv_ref[0].T
+    values_ref[:, pl.ds(half_len, old - half_len)] = gv_ref[...].reshape(-1, width).T
+    for g in range(width // HD):
         cols = pl.ds(g * HD, HD)
-        new_keys_ref[:, cols] = rotate(fresh[:, g * HD : (g + 1) * HD], key_cosine, key_sine)
+        new_keys_ref[:, cols] = rotate(
+            keys[:, g * HD : (g + 1) * HD], key_cosine_ref[...], key_sine_ref[...]
+        )
+    scale = scale_ref[...]
+    values = [values[:, g * HD : (g + 1) * HD] * scale for g in range(width // HD)]
+    values = jnp.concatenate(
+        [jnp.concatenate(values, axis=1), jnp.zeros((HD - rows, width), jnp.float32)], axis=0
+    )
+    values_ref[:, pl.ds(old, HD)] = values.astype(jnp.bfloat16).T
 
 
 def attend_kernel(
@@ -245,14 +226,13 @@
 
     xn_s[pl.ds(0, rows), :] = xn_ref[...]
     scale = lay_out(pieces, gain_ref, x_s, xn_s, rows)
-    me_tp = lax.axis_index("tp")
-    product = jnp.zeros((2 * rows, kv * group * HD), jnp.float32)
-    for t in range(tp):
-        place = pl.ds(pl.multiple_of((me_tp ^ t) * part, HD), part)
-        product += jnp.dot(xn_s[:, place], wq_ref[place, :], preferred_element_type=jnp.float32)
+    product = [
+        jnp.dot(xn_s[...], wq_ref[:, pl.ds(p * size, size)], preferred_element_type=jnp.float32)
+        for p in range(packs)
+    ]
     scale = jnp.concatenate([scale_ref[...], jnp.broadcast_to(scale, (rows, HD))], axis=0)
     scale = scale * HD**-0.5
-    product = [product[:, h * HD : (h + 1) * HD] * scale for h in range(kv * group)]
+    product = [x[:, h * HD : (h + 1) * HD] * scale for x in product for h in range(each)]
 
     every = range(packs)
     cosine, sine = cosine_ref[...], sine_ref[...]
@@ -407,52 +387,54 @@
     hbm = pl.BlockSpec(memory_space=pltpu.HBM)
     params = pltpu.CompilerParams(vmem_limit_bytes=16 * 2**20)
     f32, bf16 = jnp.float32, jnp.bfloat16
-    blocks = prompt_keys.shape[1] // history
-    old = (blocks + own) * history
+    half_len = prompt_keys.shape[1]
+    old = half_len + own * history
     packed = 2 - kv % 2
-    packs = kv // packed
     lanes = packed * group * 2 * rows
-    loaded = pl.pallas_call(
-        functools.partial(load_kernel, (steps, own, tp, kv, group, history, packed)),
+    gain, xn, scale, key_cosine, key_sine, cosine, sine, bias = pl.pallas_call(
+        functools.partial(prepare_kernel, (steps, own, tp, group, history, half_len, packed)),
         out_shape=(
             jax.ShapeDtypeStruct((1, width), f32),
             jax.ShapeDtypeStruct((rows, width), bf16),
             jax.ShapeDtypeStruct((rows, HD), f32),
-            jax.ShapeDtypeStruct((rows, kv * HD), bf16),
-            jax.ShapeDtypeStruct((kv * HD, old + HD), bf16),
+            jax.ShapeDtypeStruct((rows, HD), f32),
+            jax.ShapeDtypeStruct((rows, HD), f32),
             jax.ShapeDtypeStruct((HD // 2, lanes), f32),
             jax.ShapeDtypeStruct((HD // 2, lanes), f32),
-            jax.ShapeDtypeStruct((old + rows - prompt_keys.shape[1] // 2, lanes), f32),
+            jax.ShapeDtypeStruct((old + rows - half_len // 2, lanes), f32),
         ),
-        in_specs=[hbm] * 8 + [vmem] * (tp - 1),
+        in_specs=[hbm] * 4 + [vmem] * (tp - 1),
         out_specs=(vmem,) * 8,
         scratch_shapes=[
             pltpu.SMEM(lengths.shape, jnp.int32),
             pltpu.SMEM(parents.shape, jnp.int32),
             pltpu.VMEM(hidden_in.shape, bf16),
             pltpu.VMEM((tp, rows, part), f32),
-            pltpu.VMEM(w_key.shape, bf16),
-            pltpu.VMEM(w_value.shape, bf16),
-            pltpu.VMEM((blocks + own, history, kv * HD), bf16),
-            pltpu.SemaphoreType.DMA((18,)),
+            pltpu.SemaphoreType.DMA((4,)),
         ],
         compiler_params=params,
-        name="load",
+        cost_estimate=pl.CostEstimate(
+            flops=2000 * 10**6, bytes_accessed=2**20, transcendentals=0
+        ),
+        name="prepare",
+    )(*(in_hbm(x) for x in (lengths, parents, norm_gain[None, :], hidden_in)), *near_pieces)
+
+    new_keys, values = pl.pallas_call(
+        fresh_kernel,
+        out_shape=(
+            jax.ShapeDtypeStruct((rows, kv * HD), bf16),
+            jax.ShapeDtypeStruct((kv * HD, old + HD), bf16),
+        ),
+        in_specs=[vmem] * 8,
+        out_specs=(vmem,) * 2,
+        compiler_params=params,
+        name="fresh",
     )(
-        *(
-            in_hbm(x)
-            for x in (
-                lengths,
-                parents,
-                norm_gain[None, :],
-                hidden_in,
-                w_key,
-                w_value,
-                prompt_values.reshape(blocks, history, kv * HD),
-                gen_values,
-            )
-        ),
-        *near_pieces,
+        xn,
+        scale,
+        key_cosine,
+        key_sine,
+        *(in_vmem(x) for x in (w_key, w_value, prompt_values, gen_values)),
     )
 
     kept, kept_lse, sent = pl.pallas_call(
@@ -470,7 +452,7 @@
         ],
         compiler_params=params,
         name="attend",
-    )(*loaded, in_vmem(w_query), in_vmem(prompt_keys), in_vmem(gen_keys), *far_pieces[::-1])
+    )(gain, xn, scale, new_keys, values, cosine, sine, bias, in_vmem(w_query), in_vmem(prompt_keys), in_vmem(gen_keys), *far_pieces[::-1])
 
     got = permute_by(sent, "req", 1)
     kept_lse, w_out_far = pl.pallas_call(

time: 15.9 us -> 15.9 us (level)
  waiting for transfers between devices: 1.65 us -> 3.13 us
  Pallas kernels: 8.72 us -> 7.58 us
  starting transfers between devices: 4.6 us -> 4.24 us
    pallas_call x1 -> x2, Pallas kernels: 3.46 us -> 2.29 us  [the longest x1 1.27 us: body(): pl.pallas_call(functools.partial(prepare_kernel, (steps, own, tp, group,...]
    ppermute x4, waiting for transfers between devices: 1.13 us -> 2.24 us  [across(): return lax.ppermute(value, ('req', 'tp'), pairs)]
    ppermute x1, starting transfers between devices: 1.45 us -> 1.07 us  [permute_by(): return lax.ppermute(value, axis, pairs)]
    ppermute x1, waiting for transfers between devices: 0.52 us -> 0.89 us  [permute_by(): return lax.ppermute(value, axis, pairs)]
  transfers between devices with their start and end apart: 5 -> 5, of which waited for: 3 -> 4; matrix products, arithmetic and copies ran while one was open for 0% -> 0% of each run, Pallas kernels for 38% -> 31%
where the time goes in v7:
time: 15.9 us; the launch traced here: 15.8 us
  Pallas kernels  7.58 us (48%)
  starting transfers between devices  4.24 us (27%)
  waiting for transfers between devices  3.13 us (20%)
  other arithmetic  0.65 us (4%)
    ppermute x4, starting transfers between devices, across(): return lax.ppermute(value, ('req', 'tp'), pairs)  3.16 us
    ppermute x4, waiting for transfers between devices, across(): return lax.ppermute(value, ('req', 'tp'), pairs)  2.24 us
    pallas_call x1, Pallas kernels, body(): pl.pallas_call(functools.partial(attend_kernel, (steps, own, tp, kv, grou...  2.12 us
    pallas_call x1, Pallas kernels, body(): pl.pallas_call(fetch_kernel, out_shape=(jax.ShapeDtypeStruct((8, heads *...  2.05 us
    pallas_call x1, Pallas kernels, body(): pl.pallas_call(functools.partial(prepare_kernel, (steps, own, tp, group,...  1.27 us
    ppermute x1, starting transfers between devices, permute_by(): return lax.ppermute(value, axis, pairs)  1.07 us
    pallas_call x1, Pallas kernels, body(): pl.pallas_call(fresh_kernel, out_shape=(jax.ShapeDtypeStruct((rows, kv *...  1.01 us
    ppermute x1, waiting for transfers between devices, permute_by(): return lax.ppermute(value, axis, pairs)  0.89 us
  transfers between devices with their start and end apart: 5, of which 4 were waited for; matrix products, arithmetic and copies ran while one was open for 0% of the time, Pallas kernels for 31%

profile of v7, /device:TPU:0, one launch (start us, length us, event | category | flops | bytes accessed | tf_op | source)
XLA Modules:
  0.0 15.8 jit_solution(17938081051088297728)
XLA Ops:
  0.0 0.5 %collective-permute-start = (bf16[4,4,1536]{2,1,0:T(4,128)(2,1)}, bf16[4,4,1536]{2,1,0:T(4,128)(2,1)S(1)}, u32[]{:S(2)}, u32[]{:S(2)}) collective-permute-start(bf16[4,4,1536]{2,1,0:T(4,128)(2,1)} %hidden.1), channel_id=1, source_target_pairs={{0,1},{1,0},{2,3},{3,2},{4,5},{5,4},{6,7},{7,6},{8,9},{9,8},{10,11... | collective-permute-start | bytes 147464 | tf_op jit(solution)/shard_map/ppermute | solution.py:39
  0.5 2.6 %collective-permute-start.2 = (bf16[4,4,1536]{2,1,0:T(4,128)(2,1)}, bf16[4,4,1536]{2,1,0:T(4,128)(2,1)S(1)}, u32[]{:S(2)}, u32[]{:S(2)}) collective-permute-start(bf16[4,4,1536]{2,1,0:T(4,128)(2,1)} %hidden.1), channel_id=1, source_target_pairs={{0,2},{1,3},{2,0},{3,1},{4,6},{5,7},{6,4},{7,5},{8,10},{9,11},{10,... | collective-permute-start | bytes 147464 | tf_op jit(solution)/shard_map/ppermute | solution.py:39
  3.1 0.1 collective-permute-start.1
  3.2 0.0 collective-permute-done.refs_0_
  3.2 0.0 copy-start.5
  3.2 1.3 %prepare.1 = (f32[1,3072]{1,0:T(1,128)S(1)}, bf16[16,3072]{1,0:T(8,128)(2,1)S(1)}, f32[16,128]{1,0:T(8,128)S(1)}, f32[16,128]{1,0:T(8,128)S(1)}, f32[16,128]{1,0...) custom-call(s32[8]{0:T(128)} %lengths.1, s32[4,64]{1,0:T(4,128)} %parents.1, ...), custom_call_target="tpu_custom_call" | custom-call | flops 2000000000 | bytes 1048576 | tf_op jit(solution)/shard_map/prepare/pallas_call | solution.py:394
  4.5 0.0 copy-done.4
  4.5 0.0 copy-done.3
  4.5 0.0 copy-done.1
  4.5 1.0 %fresh.1 = (bf16[16,512]{1,0:T(8,128)(2,1)S(1)}, bf16[512,896]{1,0:T(8,128)(2,1)S(1)}) custom-call(bf16[16,3072]{1,0:T(8,128)(2,1)S(1)} %get-tuple-element.23.xn_ref, f32[16,128]{1,0:T(8,128)S(1)} %get-tuple-element.24.scale_ref, f32[16,128]{1,0:T(8,128)S(1)} %get-tuple-element.25.key_cosine_ref, f32[16,128]{1,0:T(8,128)S(1)} %get-tuple-element.26.key_sine_ref, ...), custom_call_target="tpu_custom_call" | custom-call | tf_op jit(solution)/shard_map/fresh/pallas_call | solution.py:422
  5.5 0.1 collective-permute-done.2.refs_1_
  5.6 1.4 %collective-permute-done.1.refs_0_ = bf16[4,4,1536]{2,1,0:T(4,128)(2,1)S(1)} collective-permute-done((bf16[4,4,1536]{2,1,0:T(4,128)(2,1)}, bf16[4,4,1536]{2,1,0:T(4,128)(2,1)S(1)}, u32[]{:S(2)}, u32[]{:S(2)}) %collective-permute-start.1) | collective-permute-done | bytes 49184 | tf_op jit(solution)/shard_map/ppermute | solution.py:39
  7.1 0.0 slice-done.3
  7.1 0.0 slice-start
  7.1 2.1 %attend.1 = (f32[128,128]{1,0:T(8,128)S(1)}, f32[8,128]{1,0:T(8,128)S(1)}, bf16[144,128]{1,0:T(8,128)(2,1)S(1)}) custom-call(f32[1,3072]{1,0:T(1,128)S(1)} %get-tuple-element.22.gain_ref, bf16[16,3072]{1,0:T(8,128)(2,1)S(1)} %get-tuple-element.23.xn_ref, f32[16,128]{1,0:T(8,128)S(1)} %get-tuple-element.24.scale_ref, ...), custom_call_target="tpu_custom_call" | custom-call | tf_op jit(solution)/shard_map/attend/pallas_call | solution.py:440
  9.3 1.1 %collective-permute-start.3 = (bf16[144,128]{1,0:T(8,128)(2,1)S(1)}, bf16[144,128]{1,0:T(8,128)(2,1)S(1)}, u32[]{:S(2)}, u32[]{:S(2)}) collective-permute-start(bf16[144,128]{1,0:T(8,128)(2,1)S(1)} %get-tuple-element.35), channel_id=1, source_target_pairs={{0,2},{2,0},{4,6},{6,4},{8,10},{10,8},{12,14},{14,12},{16,18},{18,... | collective-permute-start | bytes 110600 | tf_op jit(solution)/shard_map/ppermute | solution.py:29
  10.3 2.0 %fetch.1 = (f32[8,128]{1,0:T(8,128)S(1)}, bf16[2,1024,1536]{2,1,0:T(8,128)(2,1)S(1)}) custom-call(f32[8,128]{1,0:T(8,128)S(1)} %get-tuple-element.33.kept_lse_ref, bf16[1024,3072]{1,0:T(8,128)(2,1)} %w_out_ref.1), custom_call_target="tpu_custom_call" | custom-call | tf_op jit(solution)/shard_map/fetch/pallas_call | solution.py:458
  12.4 0.9 %collective-permute-done.3.got_ref = bf16[144,128]{1,0:T(8,128)(2,1)S(1)} collective-permute-done((bf16[144,128]{1,0:T(8,128)(2,1)S(1)}, bf16[144,128]{1,0:T(8,128)(2,1)S(1)}, u32[]{:S(2)}, u32[]{:S(2)}) %collective-permute-start.3) | collective-permute-done | bytes 36896 | tf_op jit(solution)/shard_map/ppermute | solution.py:29
  13.3 0.6 %project.1 = (bf16[16,1024]{1,0:T(8,128)(2,1)S(1)}, bf16[4,4,1536]{2,1,0:T(4,128)(2,1)S(1)}) custom-call(f32[128,128]{1,0:T(8,128)S(1)} %get-tuple-element.32.kept_ref, f32[8,128]{1,0:T(8,128)S(1)} %get-tuple-element.34.kept_lse_ref, bf16[144,128]{1,0:T(8,128)(2,1)S(1)} %collective-permute-done.3.got_ref, bf16[2,1024,1536]{2,1,0:T(8,128)(2,1)S(1)} %get-tuple-element.36.w_out_ref), custom_call_target="tpu_custom_call" | custom-call | tf_op jit(solution)/shard_map/project/pallas_call | solution.py:472
  13.9 0.0 collective-permute-start.4
  13.9 0.0 slice-done
  13.9 0.5 %project_own.1 = f32[4,4,1536]{2,1,0:T(4,128)S(1)} custom-call(bf16[16,1024]{1,0:T(8,128)(2,1)S(1)} %get-tuple-element.37.ctx_ref, bf16[1024,3072]{1,0:T(8,128)(2,1)S(1)} %bitcast.2), custom_call_target="tpu_custom_call" | custom-call | tf_op jit(solution)/shard_map/project_own/pallas_call | solution.py:484
  14.4 0.7 %collective-permute-done.4 = bf16[4,4,1536]{2,1,0:T(4,128)(2,1)S(1)} collective-permute-done((bf16[4,4,1536]{2,1,0:T(4,128)(2,1)S(1)}, bf16[4,4,1536]{2,1,0:T(4,128)(2,1)S(1)}, u32[]{:S(2)}, u32[]{:S(2)}) %collective-permute-start.4) | collective-permute-done | bytes 49184 | tf_op jit(solution)/shard_map/ppermute | solution.py:39
  15.1 0.6 %add_convert_fusion = bf16[4,4,1536]{2,1,0:T(4,128)(2,1)} fusion(f32[4,4,1536]{2,1,0:T(4,128)S(1)} %project_own.1, bf16[4,4,1536]{2,1,0:T(4,128)(2,1)S(1)} %collective-permute-done.4), kind=kLoop, calls=%fused_computation | loop fusion | flops 73728 | bytes 196608 | tf_op jit(solution)/shard_map/convert_element_type | solution.py:494
  (15 shorter events, 0.0 us)
Async XLA Ops:
  0.0 4.5 %copy-start.4 = (bf16[4,64,512]{2,1,0:T(8,128)(2,1)S(1)}, bf16[4,64,512]{2,1,0:T(8,128)(2,1)}, u32[]{:S(2)}) copy-start(bf16[4,64,512]{2,1,0:T(8,128)(2,1)} %gv_ref.1) | copy-start | bytes 786436
  0.0 4.5 %copy-start.3 = (bf16[1,512,512]{2,1,0:T(8,128)(2,1)S(1)}, bf16[1,512,512]{2,1,0:T(8,128)(2,1)}, u32[]{:S(2)}) copy-start(bf16[1,512,512]{2,1,0:T(8,128)(2,1)} %pv_ref.1) | copy-start | bytes 1572868
  0.0 4.5 %copy-start.1 = (bf16[3072,512]{1,0:T(8,128)(2,1)S(1)}, bf16[3072,512]{1,0:T(8,128)(2,1)}, u32[]{:S(2)}) copy-start(bf16[3072,512]{1,0:T(8,128)(2,1)} %wv_ref.1) | copy-start | bytes 9437188
  0.0 4.5 %copy-start = (bf16[3072,512]{1,0:T(8,128)(2,1)S(1)}, bf16[3072,512]{1,0:T(8,128)(2,1)}, u32[]{:S(2)}) copy-start(bf16[3072,512]{1,0:T(8,128)(2,1)} %wk_ref.1) | copy-start | bytes 9437188
  0.0 3.2 %collective-permute-start = (bf16[4,4,1536]{2,1,0:T(4,128)(2,1)}, bf16[4,4,1536]{2,1,0:T(4,128)(2,1)S(1)}, u32[]{:S(2)}, u32[]{:S(2)}) collective-permute-start(bf16[4,4,1536]{2,1,0:T(4,128)(2,1)} %hidden.1), channel_id=1, source_target_pairs={{0,1},{1,0},{2,3},{3,2},{4,5},{5,4},{6,7},{7,6},{8,9},{9,8},{10,11... | collective-permute-start | bytes 147464 | tf_op jit(solution)/shard_map/ppermute | solution.py:39
  0.5 5.1 %collective-permute-start.2 = (bf16[4,4,1536]{2,1,0:T(4,128)(2,1)}, bf16[4,4,1536]{2,1,0:T(4,128)(2,1)S(1)}, u32[]{:S(2)}, u32[]{:S(2)}) collective-permute-start(bf16[4,4,1536]{2,1,0:T(4,128)(2,1)} %hidden.1), channel_id=1, source_target_pairs={{0,2},{1,3},{2,0},{3,1},{4,6},{5,7},{6,4},{7,5},{8,10},{9,11},{10,... | collective-permute-start | bytes 147464 | tf_op jit(solution)/shard_map/ppermute | solution.py:39
  3.1 4.0 %collective-permute-start.1 = (bf16[4,4,1536]{2,1,0:T(4,128)(2,1)}, bf16[4,4,1536]{2,1,0:T(4,128)(2,1)S(1)}, u32[]{:S(2)}, u32[]{:S(2)}) collective-permute-start(bf16[4,4,1536]{2,1,0:T(4,128)(2,1)} %hidden.1), channel_id=1, source_target_pairs={{0,3},{1,2},{2,1},{3,0},{4,7},{5,6},{6,5},{7,4},{8,11},{9,10},{10,... | collective-permute-start | bytes 147464 | tf_op jit(solution)/shard_map/ppermute | solution.py:39
  3.2 3.9 %slice-start.2 = ((s8[6291456]{0:T(1024)(128)(4,1)}), s8[4194304]{0:T(1024)(128)(4,1)S(1)}, s32[]{:S(2)}) async-start(s8[6291456]{0:T(1024)(128)(4,1)} %bitcast.3), calls=%async_computation.2 | async-start | bytes 8388608
  3.2 3.9 %slice-start.3 = ((s8[6291456]{0:T(1024)(128)(4,1)}), s8[2097152]{0:T(1024)(128)(4,1)S(1)}, s32[]{:S(2)}) async-start(s8[6291456]{0:T(1024)(128)(4,1)} %bitcast.3), calls=%async_computation.3 | async-start | bytes 4194304
  3.2 3.9 %copy-start.2 = (bf16[1,512,512]{2,1,0:T(8,128)(2,1)S(1)}, bf16[1,512,512]{2,1,0:T(8,128)(2,1)}, u32[]{:S(2)}) copy-start(bf16[1,512,512]{2,1,0:T(8,128)(2,1)} %pk_ref.1) | copy-start | bytes 1572868
  3.2 3.9 %copy-start.5 = (bf16[4,64,512]{2,1,0:T(8,128)(2,1)S(1)}, bf16[4,64,512]{2,1,0:T(8,128)(2,1)}, u32[]{:S(2)}) copy-start(bf16[4,64,512]{2,1,0:T(8,128)(2,1)} %gk_ref.1) | copy-start | bytes 786436
  7.1 6.8 %slice-start = ((s8[6291456]{0:T(1024)(128)(4,1)}), s8[2097152]{0:T(1024)(128)(4,1)S(1)}, s32[]{:S(2)}) async-start(s8[6291456]{0:T(1024)(128)(4,1)} %bitcast.1), calls=%async_computation | async-start | bytes 4194304
  9.3 4.0 %collective-permute-start.3 = (bf16[144,128]{1,0:T(8,128)(2,1)S(1)}, bf16[144,128]{1,0:T(8,128)(2,1)S(1)}, u32[]{:S(2)}, u32[]{:S(2)}) collective-permute-start(bf16[144,128]{1,0:T(8,128)(2,1)S(1)} %get-tuple-element.35), channel_id=1, source_target_pairs={{0,2},{2,0},{4,6},{6,4},{8,10},{10,8},{12,14},{14,12},{16,18},{18,... | collective-permute-start | bytes 110600 | tf_op jit(solution)/shard_map/ppermute | solution.py:29
  10.3 3.6 %slice-start.1 = ((s8[6291456]{0:T(1024)(128)(4,1)}), s8[4194304]{0:T(1024)(128)(4,1)S(1)}, s32[]{:S(2)}) async-start(s8[6291456]{0:T(1024)(128)(4,1)} %bitcast.1), calls=%async_computation.1 | async-start | bytes 8388608
  13.9 1.2 %collective-permute-start.4 = (bf16[4,4,1536]{2,1,0:T(4,128)(2,1)S(1)}, bf16[4,4,1536]{2,1,0:T(4,128)(2,1)S(1)}, u32[]{:S(2)}, u32[]{:S(2)}) collective-permute-start(bf16[4,4,1536]{2,1,0:T(4,128)(2,1)S(1)} %get-tuple-element.38), channel_id=1, source_target_pairs={{0,1},{1,0},{2,3},{3,2},{4,5},{5,4},{6,7},{7,6},{8,9},{9,8},{10,11... | collective-permute-start | bytes 147464 | tf_op jit(solution)/shard_map/ppermute | solution.py:39

commit v8 on v7

--- a/solution.py
+++ b/solution.py
@@ -375,7 +375,7 @@
     history = gen_keys.shape[1]
 
     near_pieces = [across(hidden_in, 0, t) for t in range(1, tp)]
-    far_pieces = [across(hidden_in, 1, t) for t in range(tp)]
+    far = across(hidden_in, 1, 0)
 
     def in_hbm(x):
         return pltpu.with_memory_space_constraint(x, pltpu.HBM)
@@ -419,6 +419,8 @@
         name="prepare",
     )(*(in_hbm(x) for x in (lengths, parents, norm_gain[None, :], hidden_in)), *near_pieces)
 
+    far, xn = lax.optimization_barrier((far, xn))
+    far_pieces = [far] + [across(far, 0, t) for t in range(1, tp)]
     new_keys, values = pl.pallas_call(
         fresh_kernel,
         out_shape=(

time: 15.9 us -> 15.7 us (0.987)
  waiting for transfers between devices: 3.13 us -> 1.94 us
  starting transfers between devices: 4.24 us -> 4.92 us
  local copies, waits for them, and re-layouts: 0.04 us -> 0.37 us
    ppermute x1, starting transfers between devices: 1.07 us -> 1.82 us  [permute_by(): return lax.ppermute(value, axis, pairs)]
    ppermute x1, waiting for transfers between devices: 0.89 us -> 0.14 us  [permute_by(): return lax.ppermute(value, axis, pairs)]
    ppermute x4, waiting for transfers between devices: 2.24 us -> 1.8 us  [across(): return lax.ppermute(value, ('req', 'tp'), pairs)]
    unnamed x20, local copies, waits for them, and re-layouts: 0.04 us -> 0.37 us
where the time goes in v8:
time: 15.7 us; the launch traced here: 15.5 us
  Pallas kernels  7.57 us (48%)
  starting transfers between devices  4.92 us (31%)
  waiting for transfers between devices  1.94 us (12%)
  other arithmetic  0.65 us (4%)
  local copies, waits for them, and re-layouts  0.37 us (2%)
    ppermute x4, starting transfers between devices, across(): return lax.ppermute(value, ('req', 'tp'), pairs)  3.1 us
    pallas_call x1, Pallas kernels, body(): pl.pallas_call(functools.partial(attend_kernel, (steps, own, tp, kv, grou...  2.12 us
    pallas_call x1, Pallas kernels, body(): pl.pallas_call(fetch_kernel, out_shape=(jax.ShapeDtypeStruct((8, heads *...  2.05 us
    ppermute x1, starting transfers between devices, permute_by(): return lax.ppermute(value, axis, pairs)  1.82 us
    ppermute x4, waiting for transfers between devices, across(): return lax.ppermute(value, ('req', 'tp'), pairs)  1.8 us
    pallas_call x1, Pallas kernels, body(): pl.pallas_call(functools.partial(prepare_kernel, (steps, own, tp, group,...  1.27 us
    pallas_call x1, Pallas kernels, body(): pl.pallas_call(fresh_kernel, out_shape=(jax.ShapeDtypeStruct((rows, kv *...  1.01 us
    convert_element_type x1, other arithmetic, body(): return total.astype(bf16)  0.65 us
  transfers between devices with their start and end apart: 5, of which 4 were waited for; matrix products, arithmetic and copies ran while one was open for 0% of the time, Pallas kernels for 31%

profile of v8, /device:TPU:0, one launch (start us, length us, event | category | flops | bytes accessed | tf_op | source)
XLA Modules:
  0.0 15.5 jit_solution(14943117997725968790)
XLA Ops:
  0.0 0.5 %collective-permute-start = (bf16[4,4,1536]{2,1,0:T(4,128)(2,1)}, bf16[4,4,1536]{2,1,0:T(4,128)(2,1)S(1)}, u32[]{:S(2)}, u32[]{:S(2)}) collective-permute-start(bf16[4,4,1536]{2,1,0:T(4,128)(2,1)} %hidden.1), channel_id=1, source_target_pairs={{0,1},{1,0},{2,3},{3,2},{4,5},{5,4},{6,7},{7,6},{8,9},{9,8},{10,11... | collective-permute-start | bytes 147464 | tf_op jit(solution)/shard_map/ppermute | solution.py:39
  0.5 2.6 %collective-permute-start.1 = (bf16[4,4,1536]{2,1,0:T(4,128)(2,1)}, bf16[4,4,1536]{2,1,0:T(4,128)(2,1)S(1)}, u32[]{:S(2)}, u32[]{:S(2)}) collective-permute-start(bf16[4,4,1536]{2,1,0:T(4,128)(2,1)} %hidden.1), channel_id=1, source_target_pairs={{0,2},{1,3},{2,0},{3,1},{4,6},{5,7},{6,4},{7,5},{8,10},{9,11},{10,... | collective-permute-start | bytes 147464 | tf_op jit(solution)/shard_map/ppermute | solution.py:39
  3.1 0.0 collective-permute-done.refs_0_
  3.1 0.0 copy-start.5
  3.1 1.3 %prepare.1 = (f32[1,3072]{1,0:T(1,128)S(1)}, bf16[16,3072]{1,0:T(8,128)(2,1)S(1)}, f32[16,128]{1,0:T(8,128)S(1)}, f32[16,128]{1,0:T(8,128)S(1)}, f32[16,128]{1,0...) custom-call(s32[8]{0:T(128)} %lengths.1, s32[4,64]{1,0:T(4,128)} %parents.1, ...), custom_call_target="tpu_custom_call" | custom-call | flops 2000000000 | bytes 1048576 | tf_op jit(solution)/shard_map/prepare/pallas_call | solution.py:394
  4.4 1.2 %collective-permute-done.1.refs_1_ = bf16[4,4,1536]{2,1,0:T(4,128)(2,1)S(1)} collective-permute-done((bf16[4,4,1536]{2,1,0:T(4,128)(2,1)}, bf16[4,4,1536]{2,1,0:T(4,128)(2,1)S(1)}, u32[]{:S(2)}, u32[]{:S(2)}) %collective-permute-start.1) | collective-permute-done | bytes 49184 | tf_op jit(solution)/shard_map/ppermute | solution.py:39
  5.6 0.0 collective-permute-start.2
  5.7 0.0 copy-done.4
  5.7 0.0 copy-done.3
  5.7 0.0 copy-done.1
  5.7 1.0 %fresh.1 = (bf16[16,512]{1,0:T(8,128)(2,1)S(1)}, bf16[512,896]{1,0:T(8,128)(2,1)S(1)}) custom-call(bf16[16,3072]{1,0:T(8,128)(2,1)S(1)} %get-tuple-element.26.xn_ref, f32[16,128]{1,0:T(8,128)S(1)} %get-tuple-element.27.scale_ref, f32[16,128]{1,0:T(8,128)S(1)} %get-tuple-element.28.key_cosine_ref, f32[16,128]{1,0:T(8,128)S(1)} %get-tuple-element.29.key_sine_ref, ...), custom_call_target="tpu_custom_call" | custom-call | tf_op jit(solution)/shard_map/fresh/pallas_call | solution.py:424
  6.7 0.2 %collective-permute-done.2.refs_0_ = bf16[4,4,1536]{2,1,0:T(4,128)(2,1)S(1)} collective-permute-done((bf16[4,4,1536]{2,1,0:T(4,128)(2,1)S(1)}, bf16[4,4,1536]{2,1,0:T(4,128)(2,1)S(1)}, u32[]{:S(2)}, u32[]{:S(2)}) %collective-permute-start.2) | collective-permute-done | bytes 49184 | tf_op jit(solution)/shard_map/ppermute | solution.py:39
  6.9 0.0 slice-start
  6.9 2.1 %attend.1 = (f32[128,128]{1,0:T(8,128)S(1)}, f32[8,128]{1,0:T(8,128)S(1)}, bf16[144,128]{1,0:T(8,128)(2,1)S(1)}) custom-call(f32[1,3072]{1,0:T(1,128)S(1)} %get-tuple-element.24.gain_ref, bf16[16,3072]{1,0:T(8,128)(2,1)S(1)} %get-tuple-element.26.xn_ref, f32[16,128]{1,0:T(8,128)S(1)} %get-tuple-element.27.scale_ref, ...), custom_call_target="tpu_custom_call" | custom-call | tf_op jit(solution)/shard_map/attend/pallas_call | solution.py:442
  9.0 1.8 %collective-permute-start.3 = (bf16[144,128]{1,0:T(8,128)(2,1)S(1)}, bf16[144,128]{1,0:T(8,128)(2,1)S(1)}, u32[]{:S(2)}, u32[]{:S(2)}) collective-permute-start(bf16[144,128]{1,0:T(8,128)(2,1)S(1)} %get-tuple-element.39), channel_id=1, source_target_pairs={{0,2},{2,0},{4,6},{6,4},{8,10},{10,8},{12,14},{14,12},{16,18},{18,... | collective-permute-start | bytes 110600 | tf_op jit(solution)/shard_map/ppermute | solution.py:29
  10.9 2.0 %fetch.1 = (f32[8,128]{1,0:T(8,128)S(1)}, bf16[2,1024,1536]{2,1,0:T(8,128)(2,1)S(1)}) custom-call(f32[8,128]{1,0:T(8,128)S(1)} %get-tuple-element.37.kept_lse_ref, bf16[1024,3072]{1,0:T(8,128)(2,1)} %w_out_ref.1), custom_call_target="tpu_custom_call" | custom-call | tf_op jit(solution)/shard_map/fetch/pallas_call | solution.py:460
  12.9 0.1 collective-permute-done.3.got_ref
  13.1 0.6 %project.1 = (bf16[16,1024]{1,0:T(8,128)(2,1)S(1)}, bf16[4,4,1536]{2,1,0:T(4,128)(2,1)S(1)}) custom-call(f32[128,128]{1,0:T(8,128)S(1)} %get-tuple-element.36.kept_ref, f32[8,128]{1,0:T(8,128)S(1)} %get-tuple-element.38.kept_lse_ref, bf16[144,128]{1,0:T(8,128)(2,1)S(1)} %collective-permute-done.3.got_ref, bf16[2,1024,1536]{2,1,0:T(8,128)(2,1)S(1)} %get-tuple-element.40.w_out_ref), custom_call_target="tpu_custom_call" | custom-call | tf_op jit(solution)/shard_map/project/pallas_call | solution.py:474
  13.7 0.0 collective-permute-start.4
  13.7 0.0 slice-done
  13.7 0.3 %slice-done.1 = s8[4194304]{0:T(1024)(128)(4,1)S(1)} async-done(((s8[6291456]{0:T(1024)(128)(4,1)}), s8[4194304]{0:T(1024)(128)(4,1)S(1)}, s32[]{:S(2)}) %slice-start.1) | async-done | bytes 4194328
  14.0 0.5 %project_own.1 = f32[4,4,1536]{2,1,0:T(4,128)S(1)} custom-call(bf16[16,1024]{1,0:T(8,128)(2,1)S(1)} %get-tuple-element.41.ctx_ref, bf16[1024,3072]{1,0:T(8,128)(2,1)S(1)} %bitcast.2), custom_call_target="tpu_custom_call" | custom-call | tf_op jit(solution)/shard_map/project_own/pallas_call | solution.py:486
  14.5 0.4 %collective-permute-done.4 = bf16[4,4,1536]{2,1,0:T(4,128)(2,1)S(1)} collective-permute-done((bf16[4,4,1536]{2,1,0:T(4,128)(2,1)S(1)}, bf16[4,4,1536]{2,1,0:T(4,128)(2,1)S(1)}, u32[]{:S(2)}, u32[]{:S(2)}) %collective-permute-start.4) | collective-permute-done | bytes 49184 | tf_op jit(solution)/shard_map/ppermute | solution.py:39
  14.9 0.6 %add_convert_fusion = bf16[4,4,1536]{2,1,0:T(4,128)(2,1)} fusion(f32[4,4,1536]{2,1,0:T(4,128)S(1)} %project_own.1, bf16[4,4,1536]{2,1,0:T(4,128)(2,1)S(1)} %collective-permute-done.4), kind=kLoop, calls=%fused_computation | loop fusion | flops 73728 | bytes 196608 | tf_op jit(solution)/shard_map/convert_element_type | solution.py:496
  (15 shorter events, 0.0 us)
Async XLA Ops:
  0.0 5.7 %copy-start.4 = (bf16[4,64,512]{2,1,0:T(8,128)(2,1)S(1)}, bf16[4,64,512]{2,1,0:T(8,128)(2,1)}, u32[]{:S(2)}) copy-start(bf16[4,64,512]{2,1,0:T(8,128)(2,1)} %gv_ref.1) | copy-start | bytes 786436
  0.0 5.7 %copy-start.3 = (bf16[1,512,512]{2,1,0:T(8,128)(2,1)S(1)}, bf16[1,512,512]{2,1,0:T(8,128)(2,1)}, u32[]{:S(2)}) copy-start(bf16[1,512,512]{2,1,0:T(8,128)(2,1)} %pv_ref.1) | copy-start | bytes 1572868
  0.0 5.7 %copy-start.1 = (bf16[3072,512]{1,0:T(8,128)(2,1)S(1)}, bf16[3072,512]{1,0:T(8,128)(2,1)}, u32[]{:S(2)}) copy-start(bf16[3072,512]{1,0:T(8,128)(2,1)} %wv_ref.1) | copy-start | bytes 9437188
  0.0 5.7 %copy-start = (bf16[3072,512]{1,0:T(8,128)(2,1)S(1)}, bf16[3072,512]{1,0:T(8,128)(2,1)}, u32[]{:S(2)}) copy-start(bf16[3072,512]{1,0:T(8,128)(2,1)} %wk_ref.1) | copy-start | bytes 9437188
  0.0 3.1 %collective-permute-start = (bf16[4,4,1536]{2,1,0:T(4,128)(2,1)}, bf16[4,4,1536]{2,1,0:T(4,128)(2,1)S(1)}, u32[]{:S(2)}, u32[]{:S(2)}) collective-permute-start(bf16[4,4,1536]{2,1,0:T(4,128)(2,1)} %hidden.1), channel_id=1, source_target_pairs={{0,1},{1,0},{2,3},{3,2},{4,5},{5,4},{6,7},{7,6},{8,9},{9,8},{10,11... | collective-permute-start | bytes 147464 | tf_op jit(solution)/shard_map/ppermute | solution.py:39
  0.5 5.1 %collective-permute-start.1 = (bf16[4,4,1536]{2,1,0:T(4,128)(2,1)}, bf16[4,4,1536]{2,1,0:T(4,128)(2,1)S(1)}, u32[]{:S(2)}, u32[]{:S(2)}) collective-permute-start(bf16[4,4,1536]{2,1,0:T(4,128)(2,1)} %hidden.1), channel_id=1, source_target_pairs={{0,2},{1,3},{2,0},{3,1},{4,6},{5,7},{6,4},{7,5},{8,10},{9,11},{10,... | collective-permute-start | bytes 147464 | tf_op jit(solution)/shard_map/ppermute | solution.py:39
  3.1 3.8 %slice-start.2 = ((s8[6291456]{0:T(1024)(128)(4,1)}), s8[4194304]{0:T(1024)(128)(4,1)S(1)}, s32[]{:S(2)}) async-start(s8[6291456]{0:T(1024)(128)(4,1)} %bitcast.3), calls=%async_computation.2 | async-start | bytes 8388608
  3.1 3.8 %slice-start.3 = ((s8[6291456]{0:T(1024)(128)(4,1)}), s8[2097152]{0:T(1024)(128)(4,1)S(1)}, s32[]{:S(2)}) async-start(s8[6291456]{0:T(1024)(128)(4,1)} %bitcast.3), calls=%async_computation.3 | async-start | bytes 4194304
  3.1 3.8 %copy-start.2 = (bf16[1,512,512]{2,1,0:T(8,128)(2,1)S(1)}, bf16[1,512,512]{2,1,0:T(8,128)(2,1)}, u32[]{:S(2)}) copy-start(bf16[1,512,512]{2,1,0:T(8,128)(2,1)} %pk_ref.1) | copy-start | bytes 1572868
  3.1 3.8 %copy-start.5 = (bf16[4,64,512]{2,1,0:T(8,128)(2,1)S(1)}, bf16[4,64,512]{2,1,0:T(8,128)(2,1)}, u32[]{:S(2)}) copy-start(bf16[4,64,512]{2,1,0:T(8,128)(2,1)} %gk_ref.1) | copy-start | bytes 786436
  5.6 1.2 %collective-permute-start.2 = (bf16[4,4,1536]{2,1,0:T(4,128)(2,1)S(1)}, bf16[4,4,1536]{2,1,0:T(4,128)(2,1)S(1)}, u32[]{:S(2)}, u32[]{:S(2)}) collective-permute-start(bf16[4,4,1536]{2,1,0:T(4,128)(2,1)S(1)} %collective-permute-done.1.refs_1_), channel_id=1, source_target_pairs={{0,1},{1,0},{2,3},{3,2},{4,5},{5,4},{6,7},{7,6},{8,9},{9,8},{10,11... | collective-permute-start | bytes 147464 | tf_op jit(solution)/shard_map/ppermute | solution.py:39
  6.9 6.8 %slice-start = ((s8[6291456]{0:T(1024)(128)(4,1)}), s8[2097152]{0:T(1024)(128)(4,1)S(1)}, s32[]{:S(2)}) async-start(s8[6291456]{0:T(1024)(128)(4,1)} %bitcast.1), calls=%async_computation | async-start | bytes 4194304
  9.0 4.0 %collective-permute-start.3 = (bf16[144,128]{1,0:T(8,128)(2,1)S(1)}, bf16[144,128]{1,0:T(8,128)(2,1)S(1)}, u32[]{:S(2)}, u32[]{:S(2)}) collective-permute-start(bf16[144,128]{1,0:T(8,128)(2,1)S(1)} %get-tuple-element.39), channel_id=1, source_target_pairs={{0,2},{2,0},{4,6},{6,4},{8,10},{10,8},{12,14},{14,12},{16,18},{18,... | collective-permute-start | bytes 110600 | tf_op jit(solution)/shard_map/ppermute | solution.py:29
  10.9 3.1 %slice-start.1 = ((s8[6291456]{0:T(1024)(128)(4,1)}), s8[4194304]{0:T(1024)(128)(4,1)S(1)}, s32[]{:S(2)}) async-start(s8[6291456]{0:T(1024)(128)(4,1)} %bitcast.1), calls=%async_computation.1 | async-start | bytes 8388608
  13.7 1.2 %collective-permute-start.4 = (bf16[4,4,1536]{2,1,0:T(4,128)(2,1)S(1)}, bf16[4,4,1536]{2,1,0:T(4,128)(2,1)S(1)}, u32[]{:S(2)}, u32[]{:S(2)}) collective-permute-start(bf16[4,4,1536]{2,1,0:T(4,128)(2,1)S(1)} %get-tuple-element.42), channel_id=1, source_target_pairs={{0,1},{1,0},{2,3},{3,2},{4,5},{5,4},{6,7},{7,6},{8,9},{9,8},{10,11... | collective-permute-start | bytes 147464 | tf_op jit(solution)/shard_map/ppermute | solution.py:39

commit v9 on v7

--- a/solution.py
+++ b/solution.py
@@ -39,24 +39,23 @@
     return lax.ppermute(value, ("req", "tp"), pairs)
 
 
-def lay_out(pieces, gain, x_s, xn_ref, first):
-    steps, own, part = pieces[0].shape
+def lay_out(piece, place, gain, x_s, xn_ref, first):
+    steps, own, part = piece.shape
     rows = steps * own
-    me_tp = lax.axis_index("tp")
-    total = jnp.zeros((rows, HD), jnp.float32)
-    for t, piece in enumerate(pieces):
-        column = pl.multiple_of((me_tp ^ t) * part, HD)
-        for s in range(steps):
-            x_s[t, pl.ds(s * own, own), :] = piece[s].astype(jnp.float32)
-        mine = x_s[t]
-        xn_ref[pl.ds(first, rows), pl.ds(column, part)] = (
-            mine * gain[:, pl.ds(column, part)]
-        ).astype(jnp.bfloat16)
-        mine = mine * mine
-        for c in range(part // HD):
-            total = total + mine[:, c * HD : (c + 1) * HD]
-    mean = jnp.sum(total, axis=-1, keepdims=True) / (part * len(pieces))
-    return lax.rsqrt(mean + norm_eps)
+    for s in range(steps):
+        x_s[pl.ds(s * own, own), :] = piece[s].astype(jnp.float32)
+    mine = x_s[...]
+    xn_ref[pl.ds(first, rows), place] = (mine * gain).astype(jnp.bfloat16)
+    mine = mine * mine
+    return sum(mine[:, c * HD : (c + 1) * HD] for c in range(part // HD))
+
+
+def norm_scale(squares, width):
+    return lax.rsqrt(jnp.sum(squares, axis=-1, keepdims=True) / width + norm_eps)
+
+
+def block_of(distance, part):
+    return pl.ds(pl.multiple_of((lax.axis_index("tp") ^ distance) * part, HD), part)
 
 
 def rotate(x, cosine, sine):
@@ -98,7 +97,11 @@
     for copy in copies:
         copy.wait()
 
-    scale = lay_out((hidden_s, *pieces), gain_ref, x_s, xn_ref, 0)
+    squares = []
+    for t, piece in enumerate((hidden_s, *pieces)):
+        place = block_of(t, piece.shape[-1])
+        squares.append(lay_out(piece, place, gain_ref[:, place], x_s.at[t], xn_ref, 0))
+    scale = norm_scale(sum(squares), xn_ref.shape[1])
     scale_ref[...] = jnp.broadcast_to(scale, scale_ref.shape)
 
     length = lengths_s[request]
@@ -193,6 +196,14 @@
     values_ref[:, pl.ds(old, HD)] = values.astype(jnp.bfloat16).T
 
 
+def query_kernel(gain_ref, xn_ref, wq_ref, piece, product_ref, squares_ref, x_s, xn_s):
+    rows = xn_ref.shape[0]
+    place = block_of(0, piece.shape[-1])
+    xn_s[pl.ds(0, rows), :] = xn_ref[:, place]
+    squares_ref[...] = lay_out(piece, slice(None), gain_ref[:, place], x_s, xn_s, rows)
+    product_ref[...] = jnp.dot(xn_s[...], wq_ref[place, :], preferred_element_type=jnp.float32)
+
+
 def attend_kernel(
     sizes,
     gain_ref,
@@ -206,11 +217,13 @@
     wq_ref,
     pk_ref,
     gk_ref,
+    product_ref,
+    squares_ref,
     *refs,
 ):
     steps, own, tp, kv, group, packed = sizes
-    pieces = refs[:tp][::-1]
-    kept_ref, kept_lse_ref, sent_ref, x_s, xn_s = refs[tp:]
+    pieces = refs[: tp - 1]
+    kept_ref, kept_lse_ref, sent_ref, x_s, xn_s = refs[tp - 1 :]
     rows = steps * own
     part = pieces[0].shape[-1]
     packs = kv // packed
@@ -224,15 +237,17 @@
     owner = quotient(remainder(lane, lanes // 2), group * rows)
     pad = jnp.zeros((keys_space - keys_count, lanes), jnp.bfloat16)
 
-    xn_s[pl.ds(0, rows), :] = xn_ref[...]
-    scale = lay_out(pieces, gain_ref, x_s, xn_s, rows)
-    product = [
-        jnp.dot(xn_s[...], wq_ref[:, pl.ds(p * size, size)], preferred_element_type=jnp.float32)
-        for p in range(packs)
-    ]
+    squares = squares_ref[...]
+    product = product_ref[...]
+    for n, piece in enumerate(pieces):
+        place = block_of(n + 1, part)
+        xn_s[n, pl.ds(0, rows), :] = xn_ref[:, place]
+        squares += lay_out(piece, slice(None), gain_ref[:, place], x_s.at[n], xn_s.at[n], rows)
+        product += jnp.dot(xn_s[n], wq_ref[place, :], preferred_element_type=jnp.float32)
+    scale = norm_scale(squares, xn_ref.shape[1])
     scale = jnp.concatenate([scale_ref[...], jnp.broadcast_to(scale, (rows, HD))], axis=0)
     scale = scale * HD**-0.5
-    product = [x[:, h * HD : (h + 1) * HD] * scale for x in product for h in range(each)]
+    product = [product[:, h * HD : (h + 1) * HD] * scale for h in range(kv * group)]
 
     every = range(packs)
     cosine, sine = cosine_ref[...], sine_ref[...]
@@ -375,7 +390,8 @@
     history = gen_keys.shape[1]
 
     near_pieces = [across(hidden_in, 0, t) for t in range(1, tp)]
-    far_pieces = [across(hidden_in, 1, t) for t in range(tp)]
+    later = lax.optimization_barrier((hidden_in, near_pieces[0]))[0]
+    far_pieces = [across(hidden_in, 1, 0)] + [across(later, 1, t) for t in range(1, tp)]
 
     def in_hbm(x):
         return pltpu.with_memory_space_constraint(x, pltpu.HBM)
@@ -437,6 +453,20 @@
         *(in_vmem(x) for x in (w_key, w_value, prompt_values, gen_values)),
     )
 
+    w_query = in_vmem(w_query)
+    product, squares = pl.pallas_call(
+        query_kernel,
+        out_shape=(
+            jax.ShapeDtypeStruct((2 * rows, heads * HD), f32),
+            jax.ShapeDtypeStruct((rows, HD), f32),
+        ),
+        in_specs=[vmem] * 4,
+        out_specs=(vmem,) * 2,
+        scratch_shapes=[pltpu.VMEM((rows, part), f32), pltpu.VMEM((2 * rows, part), bf16)],
+        compiler_params=params,
+        name="query",
+    )(gain, xn, w_query, far_pieces[0])
+
     kept, kept_lse, sent = pl.pallas_call(
         functools.partial(attend_kernel, (steps, own, tp, kv, group, packed)),
         out_shape=(
@@ -444,15 +474,15 @@
             jax.ShapeDtypeStruct((8, heads * rows), f32),
             jax.ShapeDtypeStruct((HD + rows, heads * rows), bf16),
         ),
-        in_specs=[vmem] * (11 + tp),
+        in_specs=[vmem] * (12 + tp),
         out_specs=(vmem,) * 3,
         scratch_shapes=[
-            pltpu.VMEM((tp, rows, part), f32),
-            pltpu.VMEM((2 * rows, width), bf16),
+            pltpu.VMEM((tp - 1, rows, part), f32),
+            pltpu.VMEM((tp - 1, 2 * rows, part), bf16),
         ],
         compiler_params=params,
         name="attend",
-    )(gain, xn, scale, new_keys, values, cosine, sine, bias, in_vmem(w_query), in_vmem(prompt_keys), in_vmem(gen_keys), *far_pieces[::-1])
+    )(gain, xn, scale, new_keys, values, cosine, sine, bias, w_query, in_vmem(prompt_keys), in_vmem(gen_keys), product, squares, *far_pieces[1:])
 
     got = permute_by(sent, "req", 1)
     kept_lse, w_out_far = pl.pallas_call(

time: 15.9 us -> 16 us (level)
  waiting for transfers between devices: 3.13 us -> 1.65 us
  starting transfers between devices: 4.24 us -> 5.22 us
  local copies, waits for them, and re-layouts: 0.04 us -> 0.58 us
    ppermute x4, waiting for transfers between devices: 2.24 us -> 0.68 us  [across(): return lax.ppermute(value, ('req', 'tp'), pairs)]
    ppermute x4, starting transfers between devices: 3.16 us -> 4.22 us  [across(): return lax.ppermute(value, ('req', 'tp'), pairs)]
    pallas_call x0 -> x1, Pallas kernels: none -> 0.65 us  [body(): pl.pallas_call(query_kernel, out_shape=(jax.ShapeDtypeStruct((2 * rows, h...]
    pallas_call x1, Pallas kernels: 2.12 us -> 1.56 us  [body(): pl.pallas_call(functools.partial(attend_kernel, (steps, own, tp, kv, grou...]
    unnamed x20, local copies, waits for them, and re-layouts: 0.04 us -> 0.58 us
  transfers between devices with their start and end apart: 5 -> 5, of which waited for: 4 -> 2; matrix products, arithmetic and copies ran while one was open for 0% -> 0% of each run, Pallas kernels for 31% -> 35%
where the time goes in v9:
time: 16 us; the launch traced here: 15.9 us
  Pallas kernels  7.66 us (48%)
  starting transfers between devices  5.22 us (33%)
  waiting for transfers between devices  1.65 us (10%)
  other arithmetic  0.65 us (4%)
  local copies, waits for them, and re-layouts  0.58 us (4%)
    ppermute x4, starting transfers between devices, across(): return lax.ppermute(value, ('req', 'tp'), pairs)  4.22 us
    pallas_call x1, Pallas kernels, body(): pl.pallas_call(fetch_kernel, out_shape=(jax.ShapeDtypeStruct((8, heads *...  2.05 us
    pallas_call x1, Pallas kernels, body(): pl.pallas_call(functools.partial(attend_kernel, (steps, own, tp, kv, grou...  1.56 us
    pallas_call x1, Pallas kernels, body(): pl.pallas_call(functools.partial(prepare_kernel, (steps, own, tp, group,...  1.27 us
    pallas_call x1, Pallas kernels, body(): pl.pallas_call(fresh_kernel, out_shape=(jax.ShapeDtypeStruct((rows, kv *...  1.01 us
    ppermute x1, starting transfers between devices, permute_by(): return lax.ppermute(value, axis, pairs)  1 us
    ppermute x1, waiting for transfers between devices, permute_by(): return lax.ppermute(value, axis, pairs)  0.97 us
    ppermute x4, waiting for transfers between devices, across(): return lax.ppermute(value, ('req', 'tp'), pairs)  0.68 us
  transfers between devices with their start and end apart: 5, of which 2 were waited for; matrix products, arithmetic and copies ran while one was open for 0% of the time, Pallas kernels for 35%

profile of v9, /device:TPU:0, one launch (start us, length us, event | category | flops | bytes accessed | tf_op | source)
XLA Modules:
  0.0 15.9 jit_solution(5428358456325714520)
XLA Ops:
  0.0 0.5 %collective-permute-start = (bf16[4,4,1536]{2,1,0:T(4,128)(2,1)}, bf16[4,4,1536]{2,1,0:T(4,128)(2,1)S(1)}, u32[]{:S(2)}, u32[]{:S(2)}) collective-permute-start(bf16[4,4,1536]{2,1,0:T(4,128)(2,1)} %hidden.1), channel_id=1, source_target_pairs={{0,1},{1,0},{2,3},{3,2},{4,5},{5,4},{6,7},{7,6},{8,9},{9,8},{10,11... | collective-permute-start | bytes 147464 | tf_op jit(solution)/shard_map/ppermute | solution.py:39
  0.5 2.6 %collective-permute-start.1 = (bf16[4,4,1536]{2,1,0:T(4,128)(2,1)}, bf16[4,4,1536]{2,1,0:T(4,128)(2,1)S(1)}, u32[]{:S(2)}, u32[]{:S(2)}) collective-permute-start(bf16[4,4,1536]{2,1,0:T(4,128)(2,1)} %hidden.1), channel_id=1, source_target_pairs={{0,2},{1,3},{2,0},{3,1},{4,6},{5,7},{6,4},{7,5},{8,10},{9,11},{10,... | collective-permute-start | bytes 147464 | tf_op jit(solution)/shard_map/ppermute | solution.py:39
  3.1 0.0 collective-permute-done.refs_0_
  3.1 1.1 %collective-permute-start.2 = (bf16[4,4,1536]{2,1,0:T(4,128)(2,1)}, bf16[4,4,1536]{2,1,0:T(4,128)(2,1)S(1)}, u32[]{:S(2)}, u32[]{:S(2)}) collective-permute-start(bf16[4,4,1536]{2,1,0:T(4,128)(2,1)} %hidden.1), channel_id=1, source_target_pairs={{0,3},{1,2},{2,1},{3,0},{4,7},{5,6},{6,5},{7,4},{8,11},{9,10},{10,... | collective-permute-start | bytes 147464 | tf_op jit(solution)/shard_map/ppermute | solution.py:39
  4.2 1.3 %prepare.1 = (f32[1,3072]{1,0:T(1,128)S(1)}, bf16[16,3072]{1,0:T(8,128)(2,1)S(1)}, f32[16,128]{1,0:T(8,128)S(1)}, f32[16,128]{1,0:T(8,128)S(1)}, f32[16,128]{1,0...) custom-call(s32[8]{0:T(128)} %lengths.1, s32[4,64]{1,0:T(4,128)} %parents.1, ...), custom_call_target="tpu_custom_call" | custom-call | flops 2000000000 | bytes 1048576 | tf_op jit(solution)/shard_map/prepare/pallas_call | solution.py:410
  5.6 0.0 copy-start.3
  5.6 0.0 copy-start.5
  5.6 1.0 %fresh.1 = (bf16[16,512]{1,0:T(8,128)(2,1)S(1)}, bf16[512,896]{1,0:T(8,128)(2,1)S(1)}) custom-call(bf16[16,3072]{1,0:T(8,128)(2,1)S(1)} %get-tuple-element.26.xn_ref, f32[16,128]{1,0:T(8,128)S(1)} %get-tuple-element.27.scale_ref, f32[16,128]{1,0:T(8,128)S(1)} %get-tuple-element.28.key_cosine_ref, f32[16,128]{1,0:T(8,128)S(1)} %get-tuple-element.29.key_sine_ref, ...), custom_call_target="tpu_custom_call" | custom-call | tf_op jit(solution)/shard_map/fresh/pallas_call | solution.py:438
  6.6 0.0 collective-permute-done.1.piece
  6.6 0.5 %slice-done.3 = s8[2097152]{0:T(1024)(128)(4,1)S(1)} async-done(((s8[6291456]{0:T(1024)(128)(4,1)}), s8[2097152]{0:T(1024)(128)(4,1)S(1)}, s32[]{:S(2)}) %slice-start.3) | async-done | bytes 2097176
  7.1 0.7 %query.1 = (f32[32,1024]{1,0:T(8,128)S(1)}, f32[16,128]{1,0:T(8,128)S(1)}) custom-call(f32[1,3072]{1,0:T(1,128)S(1)} %get-tuple-element.25.gain_ref, bf16[16,3072]{1,0:T(8,128)(2,1)S(1)} %get-tuple-element.26.xn_ref, bf16[3072,1024]{1,0:T(8,128)(2,1)S(1)} %bitcast.4, bf16[4,4,1536]{2,1,0:T(4,128)(2,1)S(1)} %collective-permute-done.1.piece), custom_call_target="tpu_custom_call" | custom-call | tf_op jit(solution)/shard_map/query/pallas_call | solution.py:457
  7.8 0.0 collective-permute-done.2.refs_0_
  7.8 0.0 copy-done.3
  7.8 0.0 slice-start
  7.8 1.6 %attend.1 = (f32[128,128]{1,0:T(8,128)S(1)}, f32[8,128]{1,0:T(8,128)S(1)}, bf16[144,128]{1,0:T(8,128)(2,1)S(1)}) custom-call(f32[1,3072]{1,0:T(1,128)S(1)} %get-tuple-element.25.gain_ref, bf16[16,3072]{1,0:T(8,128)(2,1)S(1)} %get-tuple-element.26.xn_ref, f32[16,128]{1,0:T(8,128)S(1)} %get-tuple-element.27.scale_ref, ...), custom_call_target="tpu_custom_call" | custom-call | tf_op jit(solution)/shard_map/attend/pallas_call | solution.py:470
  9.4 1.0 %collective-permute-start.3 = (bf16[144,128]{1,0:T(8,128)(2,1)S(1)}, bf16[144,128]{1,0:T(8,128)(2,1)S(1)}, u32[]{:S(2)}, u32[]{:S(2)}) collective-permute-start(bf16[144,128]{1,0:T(8,128)(2,1)S(1)} %get-tuple-element.41), channel_id=1, source_target_pairs={{0,2},{2,0},{4,6},{6,4},{8,10},{10,8},{12,14},{14,12},{16,18},{18,... | collective-permute-start | bytes 110600 | tf_op jit(solution)/shard_map/ppermute | solution.py:29
  10.4 2.0 %fetch.1 = (f32[8,128]{1,0:T(8,128)S(1)}, bf16[2,1024,1536]{2,1,0:T(8,128)(2,1)S(1)}) custom-call(f32[8,128]{1,0:T(8,128)S(1)} %get-tuple-element.39.kept_lse_ref, bf16[1024,3072]{1,0:T(8,128)(2,1)} %w_out_ref.1), custom_call_target="tpu_custom_call" | custom-call | tf_op jit(solution)/shard_map/fetch/pallas_call | solution.py:488
  12.5 1.0 %collective-permute-done.3.got_ref = bf16[144,128]{1,0:T(8,128)(2,1)S(1)} collective-permute-done((bf16[144,128]{1,0:T(8,128)(2,1)S(1)}, bf16[144,128]{1,0:T(8,128)(2,1)S(1)}, u32[]{:S(2)}, u32[]{:S(2)}) %collective-permute-start.3) | collective-permute-done | bytes 36896 | tf_op jit(solution)/shard_map/ppermute | solution.py:29
  13.4 0.6 %project.1 = (bf16[16,1024]{1,0:T(8,128)(2,1)S(1)}, bf16[4,4,1536]{2,1,0:T(4,128)(2,1)S(1)}) custom-call(f32[128,128]{1,0:T(8,128)S(1)} %get-tuple-element.38.kept_ref, f32[8,128]{1,0:T(8,128)S(1)} %get-tuple-element.40.kept_lse_ref, bf16[144,128]{1,0:T(8,128)(2,1)S(1)} %collective-permute-done.3.got_ref, bf16[2,1024,1536]{2,1,0:T(8,128)(2,1)S(1)} %get-tuple-element.42.w_out_ref), custom_call_target="tpu_custom_call" | custom-call | tf_op jit(solution)/shard_map/project/pallas_call | solution.py:502
  14.0 0.0 collective-permute-start.4
  14.0 0.0 slice-done
  14.1 0.5 %project_own.1 = f32[4,4,1536]{2,1,0:T(4,128)S(1)} custom-call(bf16[16,1024]{1,0:T(8,128)(2,1)S(1)} %get-tuple-element.43.ctx_ref, bf16[1024,3072]{1,0:T(8,128)(2,1)S(1)} %bitcast.2), custom_call_target="tpu_custom_call" | custom-call | tf_op jit(solution)/shard_map/project_own/pallas_call | solution.py:514
  14.6 0.7 %collective-permute-done.4 = bf16[4,4,1536]{2,1,0:T(4,128)(2,1)S(1)} collective-permute-done((bf16[4,4,1536]{2,1,0:T(4,128)(2,1)S(1)}, bf16[4,4,1536]{2,1,0:T(4,128)(2,1)S(1)}, u32[]{:S(2)}, u32[]{:S(2)}) %collective-permute-start.4) | collective-permute-done | bytes 49184 | tf_op jit(solution)/shard_map/ppermute | solution.py:39
  15.3 0.6 %add_convert_fusion = bf16[4,4,1536]{2,1,0:T(4,128)(2,1)} fusion(f32[4,4,1536]{2,1,0:T(4,128)S(1)} %project_own.1, bf16[4,4,1536]{2,1,0:T(4,128)(2,1)S(1)} %collective-permute-done.4), kind=kLoop, calls=%fused_computation | loop fusion | flops 73728 | bytes 196608 | tf_op jit(solution)/shard_map/convert_element_type | solution.py:524
  (16 shorter events, 0.0 us)
Async XLA Ops:
  0.0 5.5 %copy-start.4 = (bf16[4,64,512]{2,1,0:T(8,128)(2,1)S(1)}, bf16[4,64,512]{2,1,0:T(8,128)(2,1)}, u32[]{:S(2)}) copy-start(bf16[4,64,512]{2,1,0:T(8,128)(2,1)} %gv_ref.1) | copy-start | bytes 786436
  0.0 5.5 %copy-start.2 = (bf16[1,512,512]{2,1,0:T(8,128)(2,1)S(1)}, bf16[1,512,512]{2,1,0:T(8,128)(2,1)}, u32[]{:S(2)}) copy-start(bf16[1,512,512]{2,1,0:T(8,128)(2,1)} %pv_ref.1) | copy-start | bytes 1572868
  0.0 5.5 %copy-start.1 = (bf16[3072,512]{1,0:T(8,128)(2,1)S(1)}, bf16[3072,512]{1,0:T(8,128)(2,1)}, u32[]{:S(2)}) copy-start(bf16[3072,512]{1,0:T(8,128)(2,1)} %wv_ref.1) | copy-start | bytes 9437188
  0.0 5.5 %copy-start = (bf16[3072,512]{1,0:T(8,128)(2,1)S(1)}, bf16[3072,512]{1,0:T(8,128)(2,1)}, u32[]{:S(2)}) copy-start(bf16[3072,512]{1,0:T(8,128)(2,1)} %wk_ref.1) | copy-start | bytes 9437188
  0.0 3.1 %collective-permute-start = (bf16[4,4,1536]{2,1,0:T(4,128)(2,1)}, bf16[4,4,1536]{2,1,0:T(4,128)(2,1)S(1)}, u32[]{:S(2)}, u32[]{:S(2)}) collective-permute-start(bf16[4,4,1536]{2,1,0:T(4,128)(2,1)} %hidden.1), channel_id=1, source_target_pairs={{0,1},{1,0},{2,3},{3,2},{4,5},{5,4},{6,7},{7,6},{8,9},{9,8},{10,11... | collective-permute-start | bytes 147464 | tf_op jit(solution)/shard_map/ppermute | solution.py:39
  0.5 6.1 %collective-permute-start.1 = (bf16[4,4,1536]{2,1,0:T(4,128)(2,1)}, bf16[4,4,1536]{2,1,0:T(4,128)(2,1)S(1)}, u32[]{:S(2)}, u32[]{:S(2)}) collective-permute-start(bf16[4,4,1536]{2,1,0:T(4,128)(2,1)} %hidden.1), channel_id=1, source_target_pairs={{0,2},{1,3},{2,0},{3,1},{4,6},{5,7},{6,4},{7,5},{8,10},{9,11},{10,... | collective-permute-start | bytes 147464 | tf_op jit(solution)/shard_map/ppermute | solution.py:39
  3.1 4.7 %collective-permute-start.2 = (bf16[4,4,1536]{2,1,0:T(4,128)(2,1)}, bf16[4,4,1536]{2,1,0:T(4,128)(2,1)S(1)}, u32[]{:S(2)}, u32[]{:S(2)}) collective-permute-start(bf16[4,4,1536]{2,1,0:T(4,128)(2,1)} %hidden.1), channel_id=1, source_target_pairs={{0,3},{1,2},{2,1},{3,0},{4,7},{5,6},{6,5},{7,4},{8,11},{9,10},{10,... | collective-permute-start | bytes 147464 | tf_op jit(solution)/shard_map/ppermute | solution.py:39
  4.2 2.4 %slice-start.2 = ((s8[6291456]{0:T(1024)(128)(4,1)}), s8[4194304]{0:T(1024)(128)(4,1)S(1)}, s32[]{:S(2)}) async-start(s8[6291456]{0:T(1024)(128)(4,1)} %bitcast.3), calls=%async_computation.2 | async-start | bytes 8388608
  4.2 2.9 %slice-start.3 = ((s8[6291456]{0:T(1024)(128)(4,1)}), s8[2097152]{0:T(1024)(128)(4,1)S(1)}, s32[]{:S(2)}) async-start(s8[6291456]{0:T(1024)(128)(4,1)} %bitcast.3), calls=%async_computation.3 | async-start | bytes 4194304
  5.6 2.3 %copy-start.3 = (bf16[1,512,512]{2,1,0:T(8,128)(2,1)S(1)}, bf16[1,512,512]{2,1,0:T(8,128)(2,1)}, u32[]{:S(2)}) copy-start(bf16[1,512,512]{2,1,0:T(8,128)(2,1)} %pk_ref.1) | copy-start | bytes 1572868
  5.6 2.3 %copy-start.5 = (bf16[4,64,512]{2,1,0:T(8,128)(2,1)S(1)}, bf16[4,64,512]{2,1,0:T(8,128)(2,1)}, u32[]{:S(2)}) copy-start(bf16[4,64,512]{2,1,0:T(8,128)(2,1)} %gk_ref.1) | copy-start | bytes 786436
  7.8 6.2 %slice-start = ((s8[6291456]{0:T(1024)(128)(4,1)}), s8[2097152]{0:T(1024)(128)(4,1)S(1)}, s32[]{:S(2)}) async-start(s8[6291456]{0:T(1024)(128)(4,1)} %bitcast.1), calls=%async_computation | async-start | bytes 4194304
  9.4 4.0 %collective-permute-start.3 = (bf16[144,128]{1,0:T(8,128)(2,1)S(1)}, bf16[144,128]{1,0:T(8,128)(2,1)S(1)}, u32[]{:S(2)}, u32[]{:S(2)}) collective-permute-start(bf16[144,128]{1,0:T(8,128)(2,1)S(1)} %get-tuple-element.41), channel_id=1, source_target_pairs={{0,2},{2,0},{4,6},{6,4},{8,10},{10,8},{12,14},{14,12},{16,18},{18,... | collective-permute-start | bytes 110600 | tf_op jit(solution)/shard_map/ppermute | solution.py:29
  10.4 3.6 %slice-start.1 = ((s8[6291456]{0:T(1024)(128)(4,1)}), s8[4194304]{0:T(1024)(128)(4,1)S(1)}, s32[]{:S(2)}) async-start(s8[6291456]{0:T(1024)(128)(4,1)} %bitcast.1), calls=%async_computation.1 | async-start | bytes 8388608
  14.0 1.2 %collective-permute-start.4 = (bf16[4,4,1536]{2,1,0:T(4,128)(2,1)S(1)}, bf16[4,4,1536]{2,1,0:T(4,128)(2,1)S(1)}, u32[]{:S(2)}, u32[]{:S(2)}) collective-permute-start(bf16[4,4,1536]{2,1,0:T(4,128)(2,1)S(1)} %get-tuple-element.44), channel_id=1, source_target_pairs={{0,1},{1,0},{2,3},{3,2},{4,5},{5,4},{6,7},{7,6},{8,9},{9,8},{10,11... | collective-permute-start | bytes 147464 | tf_op jit(solution)/shard_map/ppermute | solution.py:39

commit v10 on v9

--- a/solution.py
+++ b/solution.py
@@ -390,7 +390,8 @@
     history = gen_keys.shape[1]
 
     near_pieces = [across(hidden_in, 0, t) for t in range(1, tp)]
-    later = lax.optimization_barrier((hidden_in, near_pieces[0]))[0]
+    tiny = jnp.cos(lax.broadcasted_iota(jnp.float32, (8, HD), 1))
+    later = lax.optimization_barrier((hidden_in, tiny))[0]
     far_pieces = [across(hidden_in, 1, 0)] + [across(later, 1, t) for t in range(1, tp)]
 
     def in_hbm(x):

time: 16 us -> 15.3 us (0.956)
  waiting for transfers between devices: 1.65 us -> 1.16 us
  starting transfers between devices: 5.22 us -> 4.9 us
    ppermute x4, starting transfers between devices: 4.22 us -> 3.16 us  [across(): return lax.ppermute(value, ('req', 'tp'), pairs)]
    ppermute x1, starting transfers between devices: 1 us -> 1.74 us  [permute_by(): return lax.ppermute(value, axis, pairs)]
    ppermute x1, waiting for transfers between devices: 0.97 us -> 0.23 us  [permute_by(): return lax.ppermute(value, axis, pairs)]
    ppermute x4, waiting for transfers between devices: 0.68 us -> 0.93 us  [across(): return lax.ppermute(value, ('req', 'tp'), pairs)]
  transfers between devices with their start and end apart: 5 -> 5, of which waited for: 2 -> 4; matrix products, arithmetic and copies ran while one was open for 0% -> 0% of each run, Pallas kernels for 35% -> 36%
where the time goes in v10:
time: 15.3 us; the launch traced here: 15.2 us
  Pallas kernels  7.65 us (50%)
  starting transfers between devices  4.9 us (32%)
  waiting for transfers between devices  1.16 us (8%)
  local copies, waits for them, and re-layouts  0.71 us (5%)
  other arithmetic  0.65 us (4%)
    ppermute x4, starting transfers between devices, across(): return lax.ppermute(value, ('req', 'tp'), pairs)  3.16 us
    pallas_call x1, Pallas kernels, body(): pl.pallas_call(fetch_kernel, out_shape=(jax.ShapeDtypeStruct((8, heads *...  2.05 us
    ppermute x1, starting transfers between devices, permute_by(): return lax.ppermute(value, axis, pairs)  1.74 us
    pallas_call x1, Pallas kernels, body(): pl.pallas_call(functools.partial(attend_kernel, (steps, own, tp, kv, grou...  1.55 us
    pallas_call x1, Pallas kernels, body(): pl.pallas_call(functools.partial(prepare_kernel, (steps, own, tp, group,...  1.27 us
    pallas_call x1, Pallas kernels, body(): pl.pallas_call(fresh_kernel, out_shape=(jax.ShapeDtypeStruct((rows, kv *...  1.01 us
    ppermute x4, waiting for transfers between devices, across(): return lax.ppermute(value, ('req', 'tp'), pairs)  0.93 us
    unnamed x20, local copies, waits for them, and re-layouts  0.71 us
  transfers between devices with their start and end apart: 5, of which 4 were waited for; matrix products, arithmetic and copies ran while one was open for 0% of the time, Pallas kernels for 36%

profile of v10, /device:TPU:0, one launch (start us, length us, event | category | flops | bytes accessed | tf_op | source)
XLA Modules:
  0.0 15.2 jit_solution(16674242565049929741)
XLA Ops:
  0.0 0.5 %collective-permute-start = (bf16[4,4,1536]{2,1,0:T(4,128)(2,1)}, bf16[4,4,1536]{2,1,0:T(4,128)(2,1)S(1)}, u32[]{:S(2)}, u32[]{:S(2)}) collective-permute-start(bf16[4,4,1536]{2,1,0:T(4,128)(2,1)} %hidden.1), channel_id=1, source_target_pairs={{0,1},{1,0},{2,3},{3,2},{4,5},{5,4},{6,7},{7,6},{8,9},{9,8},{10,11... | collective-permute-start | bytes 147464 | tf_op jit(solution)/shard_map/ppermute | solution.py:39
  0.5 2.6 %collective-permute-start.1 = (bf16[4,4,1536]{2,1,0:T(4,128)(2,1)}, bf16[4,4,1536]{2,1,0:T(4,128)(2,1)S(1)}, u32[]{:S(2)}, u32[]{:S(2)}) collective-permute-start(bf16[4,4,1536]{2,1,0:T(4,128)(2,1)} %hidden.1), channel_id=1, source_target_pairs={{0,2},{1,3},{2,0},{3,1},{4,6},{5,7},{6,4},{7,5},{8,10},{9,11},{10,... | collective-permute-start | bytes 147464 | tf_op jit(solution)/shard_map/ppermute | solution.py:39
  3.1 0.1 collective-permute-start.2
  3.2 0.0 collective-permute-done.refs_0_
  3.2 1.3 %prepare.1 = (f32[1,3072]{1,0:T(1,128)S(1)}, bf16[16,3072]{1,0:T(8,128)(2,1)S(1)}, f32[16,128]{1,0:T(8,128)S(1)}, f32[16,128]{1,0:T(8,128)S(1)}, f32[16,128]{1,0...) custom-call(s32[8]{0:T(128)} %lengths.1, s32[4,64]{1,0:T(4,128)} %parents.1, ...), custom_call_target="tpu_custom_call" | custom-call | flops 2000000000 | bytes 1048576 | tf_op jit(solution)/shard_map/prepare/pallas_call | solution.py:411
  4.5 0.0 copy-done.4
  4.5 0.0 copy-start.3
  4.5 0.0 copy-start.5
  4.5 1.0 %fresh.1 = (bf16[16,512]{1,0:T(8,128)(2,1)S(1)}, bf16[512,896]{1,0:T(8,128)(2,1)S(1)}) custom-call(bf16[16,3072]{1,0:T(8,128)(2,1)S(1)} %get-tuple-element.25.xn_ref, f32[16,128]{1,0:T(8,128)S(1)} %get-tuple-element.26.scale_ref, f32[16,128]{1,0:T(8,128)S(1)} %get-tuple-element.27.key_cosine_ref, f32[16,128]{1,0:T(8,128)S(1)} %get-tuple-element.28.key_sine_ref, ...), custom_call_target="tpu_custom_call" | custom-call | tf_op jit(solution)/shard_map/fresh/pallas_call | solution.py:439
  5.5 0.1 collective-permute-done.1.piece
  5.7 0.4 %slice-done.3 = s8[2097152]{0:T(1024)(128)(4,1)S(1)} async-done(((s8[6291456]{0:T(1024)(128)(4,1)}), s8[2097152]{0:T(1024)(128)(4,1)S(1)}, s32[]{:S(2)}) %slice-start.3) | async-done | bytes 2097176
  6.1 0.7 %query.1 = (f32[32,1024]{1,0:T(8,128)S(1)}, f32[16,128]{1,0:T(8,128)S(1)}) custom-call(f32[1,3072]{1,0:T(1,128)S(1)} %get-tuple-element.24.gain_ref, bf16[16,3072]{1,0:T(8,128)(2,1)S(1)} %get-tuple-element.25.xn_ref, bf16[3072,1024]{1,0:T(8,128)(2,1)S(1)} %bitcast.4, bf16[4,4,1536]{2,1,0:T(4,128)(2,1)S(1)} %collective-permute-done.1.piece), custom_call_target="tpu_custom_call" | custom-call | tf_op jit(solution)/shard_map/query/pallas_call | solution.py:458
  6.7 0.4 %collective-permute-done.2.refs_0_ = bf16[4,4,1536]{2,1,0:T(4,128)(2,1)S(1)} collective-permute-done((bf16[4,4,1536]{2,1,0:T(4,128)(2,1)}, bf16[4,4,1536]{2,1,0:T(4,128)(2,1)S(1)}, u32[]{:S(2)}, u32[]{:S(2)}) %collective-permute-start.2) | collective-permute-done | bytes 49184 | tf_op jit(solution)/shard_map/ppermute | solution.py:39
  7.1 1.6 %attend.1 = (f32[128,128]{1,0:T(8,128)S(1)}, f32[8,128]{1,0:T(8,128)S(1)}, bf16[144,128]{1,0:T(8,128)(2,1)S(1)}) custom-call(f32[1,3072]{1,0:T(1,128)S(1)} %get-tuple-element.24.gain_ref, bf16[16,3072]{1,0:T(8,128)(2,1)S(1)} %get-tuple-element.25.xn_ref, f32[16,128]{1,0:T(8,128)S(1)} %get-tuple-element.26.scale_ref, ...), custom_call_target="tpu_custom_call" | custom-call | tf_op jit(solution)/shard_map/attend/pallas_call | solution.py:471
  8.7 1.7 %collective-permute-start.3 = (bf16[144,128]{1,0:T(8,128)(2,1)S(1)}, bf16[144,128]{1,0:T(8,128)(2,1)S(1)}, u32[]{:S(2)}, u32[]{:S(2)}) collective-permute-start(bf16[144,128]{1,0:T(8,128)(2,1)S(1)} %get-tuple-element.39), channel_id=1, source_target_pairs={{0,2},{2,0},{4,6},{6,4},{8,10},{10,8},{12,14},{14,12},{16,18},{18,... | collective-permute-start | bytes 110600 | tf_op jit(solution)/shard_map/ppermute | solution.py:29
  10.4 2.0 %fetch.1 = (f32[8,128]{1,0:T(8,128)S(1)}, bf16[2,1024,1536]{2,1,0:T(8,128)(2,1)S(1)}) custom-call(f32[8,128]{1,0:T(8,128)S(1)} %get-tuple-element.37.kept_lse_ref, bf16[1024,3072]{1,0:T(8,128)(2,1)} %w_out_ref.1), custom_call_target="tpu_custom_call" | custom-call | tf_op jit(solution)/shard_map/fetch/pallas_call | solution.py:489
  12.5 0.2 %collective-permute-done.3.got_ref = bf16[144,128]{1,0:T(8,128)(2,1)S(1)} collective-permute-done((bf16[144,128]{1,0:T(8,128)(2,1)S(1)}, bf16[144,128]{1,0:T(8,128)(2,1)S(1)}, u32[]{:S(2)}, u32[]{:S(2)}) %collective-permute-start.3) | collective-permute-done | bytes 36896 | tf_op jit(solution)/shard_map/ppermute | solution.py:29
  12.7 0.6 %project.1 = (bf16[16,1024]{1,0:T(8,128)(2,1)S(1)}, bf16[4,4,1536]{2,1,0:T(4,128)(2,1)S(1)}) custom-call(f32[128,128]{1,0:T(8,128)S(1)} %get-tuple-element.36.kept_ref, f32[8,128]{1,0:T(8,128)S(1)} %get-tuple-element.38.kept_lse_ref, bf16[144,128]{1,0:T(8,128)(2,1)S(1)} %collective-permute-done.3.got_ref, bf16[2,1024,1536]{2,1,0:T(8,128)(2,1)S(1)} %get-tuple-element.40.w_out_ref), custom_call_target="tpu_custom_call" | custom-call | tf_op jit(solution)/shard_map/project/pallas_call | solution.py:503
  13.3 0.0 collective-permute-start.4
  13.3 0.0 slice-done
  13.3 0.2 %slice-done.1 = s8[4194304]{0:T(1024)(128)(4,1)S(1)} async-done(((s8[6291456]{0:T(1024)(128)(4,1)}), s8[4194304]{0:T(1024)(128)(4,1)S(1)}, s32[]{:S(2)}) %slice-start.1) | async-done | bytes 4194328
  13.5 0.5 %project_own.1 = f32[4,4,1536]{2,1,0:T(4,128)S(1)} custom-call(bf16[16,1024]{1,0:T(8,128)(2,1)S(1)} %get-tuple-element.41.ctx_ref, bf16[1024,3072]{1,0:T(8,128)(2,1)S(1)} %bitcast.2), custom_call_target="tpu_custom_call" | custom-call | tf_op jit(solution)/shard_map/project_own/pallas_call | solution.py:515
  14.1 0.5 %collective-permute-done.4 = bf16[4,4,1536]{2,1,0:T(4,128)(2,1)S(1)} collective-permute-done((bf16[4,4,1536]{2,1,0:T(4,128)(2,1)S(1)}, bf16[4,4,1536]{2,1,0:T(4,128)(2,1)S(1)}, u32[]{:S(2)}, u32[]{:S(2)}) %collective-permute-start.4) | collective-permute-done | bytes 49184 | tf_op jit(solution)/shard_map/ppermute | solution.py:39
  14.5 0.6 %add_convert_fusion = bf16[4,4,1536]{2,1,0:T(4,128)(2,1)} fusion(f32[4,4,1536]{2,1,0:T(4,128)S(1)} %project_own.1, bf16[4,4,1536]{2,1,0:T(4,128)(2,1)S(1)} %collective-permute-done.4), kind=kLoop, calls=%fused_computation | loop fusion | flops 73728 | bytes 196608 | tf_op jit(solution)/shard_map/convert_element_type | solution.py:525
  (16 shorter events, 0.0 us)
Async XLA Ops:
  0.0 4.5 %copy-start.4 = (bf16[4,64,512]{2,1,0:T(8,128)(2,1)S(1)}, bf16[4,64,512]{2,1,0:T(8,128)(2,1)}, u32[]{:S(2)}) copy-start(bf16[4,64,512]{2,1,0:T(8,128)(2,1)} %gv_ref.1) | copy-start | bytes 786436
  0.0 4.5 %copy-start.2 = (bf16[1,512,512]{2,1,0:T(8,128)(2,1)S(1)}, bf16[1,512,512]{2,1,0:T(8,128)(2,1)}, u32[]{:S(2)}) copy-start(bf16[1,512,512]{2,1,0:T(8,128)(2,1)} %pv_ref.1) | copy-start | bytes 1572868
  0.0 4.5 %copy-start.1 = (bf16[3072,512]{1,0:T(8,128)(2,1)S(1)}, bf16[3072,512]{1,0:T(8,128)(2,1)}, u32[]{:S(2)}) copy-start(bf16[3072,512]{1,0:T(8,128)(2,1)} %wv_ref.1) | copy-start | bytes 9437188
  0.0 4.5 %copy-start = (bf16[3072,512]{1,0:T(8,128)(2,1)S(1)}, bf16[3072,512]{1,0:T(8,128)(2,1)}, u32[]{:S(2)}) copy-start(bf16[3072,512]{1,0:T(8,128)(2,1)} %wk_ref.1) | copy-start | bytes 9437188
  0.0 3.2 %collective-permute-start = (bf16[4,4,1536]{2,1,0:T(4,128)(2,1)}, bf16[4,4,1536]{2,1,0:T(4,128)(2,1)S(1)}, u32[]{:S(2)}, u32[]{:S(2)}) collective-permute-start(bf16[4,4,1536]{2,1,0:T(4,128)(2,1)} %hidden.1), channel_id=1, source_target_pairs={{0,1},{1,0},{2,3},{3,2},{4,5},{5,4},{6,7},{7,6},{8,9},{9,8},{10,11... | collective-permute-start | bytes 147464 | tf_op jit(solution)/shard_map/ppermute | solution.py:39
  0.5 5.1 %collective-permute-start.1 = (bf16[4,4,1536]{2,1,0:T(4,128)(2,1)}, bf16[4,4,1536]{2,1,0:T(4,128)(2,1)S(1)}, u32[]{:S(2)}, u32[]{:S(2)}) collective-permute-start(bf16[4,4,1536]{2,1,0:T(4,128)(2,1)} %hidden.1), channel_id=1, source_target_pairs={{0,2},{1,3},{2,0},{3,1},{4,6},{5,7},{6,4},{7,5},{8,10},{9,11},{10,... | collective-permute-start | bytes 147464 | tf_op jit(solution)/shard_map/ppermute | solution.py:39
  3.1 4.0 %collective-permute-start.2 = (bf16[4,4,1536]{2,1,0:T(4,128)(2,1)}, bf16[4,4,1536]{2,1,0:T(4,128)(2,1)S(1)}, u32[]{:S(2)}, u32[]{:S(2)}) collective-permute-start(bf16[4,4,1536]{2,1,0:T(4,128)(2,1)} %hidden.1), channel_id=1, source_target_pairs={{0,3},{1,2},{2,1},{3,0},{4,7},{5,6},{6,5},{7,4},{8,11},{9,10},{10,... | collective-permute-start | bytes 147464 | tf_op jit(solution)/shard_map/ppermute | solution.py:39
  3.2 2.5 %slice-start.2 = ((s8[6291456]{0:T(1024)(128)(4,1)}), s8[4194304]{0:T(1024)(128)(4,1)S(1)}, s32[]{:S(2)}) async-start(s8[6291456]{0:T(1024)(128)(4,1)} %bitcast.3), calls=%async_computation.2 | async-start | bytes 8388608
  3.2 2.9 %slice-start.3 = ((s8[6291456]{0:T(1024)(128)(4,1)}), s8[2097152]{0:T(1024)(128)(4,1)S(1)}, s32[]{:S(2)}) async-start(s8[6291456]{0:T(1024)(128)(4,1)} %bitcast.3), calls=%async_computation.3 | async-start | bytes 4194304
  4.5 2.6 %copy-start.3 = (bf16[1,512,512]{2,1,0:T(8,128)(2,1)S(1)}, bf16[1,512,512]{2,1,0:T(8,128)(2,1)}, u32[]{:S(2)}) copy-start(bf16[1,512,512]{2,1,0:T(8,128)(2,1)} %pk_ref.1) | copy-start | bytes 1572868
  4.5 2.6 %copy-start.5 = (bf16[4,64,512]{2,1,0:T(8,128)(2,1)S(1)}, bf16[4,64,512]{2,1,0:T(8,128)(2,1)}, u32[]{:S(2)}) copy-start(bf16[4,64,512]{2,1,0:T(8,128)(2,1)} %gk_ref.1) | copy-start | bytes 786436
  7.1 6.2 %slice-start = ((s8[6291456]{0:T(1024)(128)(4,1)}), s8[2097152]{0:T(1024)(128)(4,1)S(1)}, s32[]{:S(2)}) async-start(s8[6291456]{0:T(1024)(128)(4,1)} %bitcast.1), calls=%async_computation | async-start | bytes 4194304
  8.7 4.0 %collective-permute-start.3 = (bf16[144,128]{1,0:T(8,128)(2,1)S(1)}, bf16[144,128]{1,0:T(8,128)(2,1)S(1)}, u32[]{:S(2)}, u32[]{:S(2)}) collective-permute-start(bf16[144,128]{1,0:T(8,128)(2,1)S(1)} %get-tuple-element.39), channel_id=1, source_target_pairs={{0,2},{2,0},{4,6},{6,4},{8,10},{10,8},{12,14},{14,12},{16,18},{18,... | collective-permute-start | bytes 110600 | tf_op jit(solution)/shard_map/ppermute | solution.py:29
  10.4 3.1 %slice-start.1 = ((s8[6291456]{0:T(1024)(128)(4,1)}), s8[4194304]{0:T(1024)(128)(4,1)S(1)}, s32[]{:S(2)}) async-start(s8[6291456]{0:T(1024)(128)(4,1)} %bitcast.1), calls=%async_computation.1 | async-start | bytes 8388608
  13.3 1.2 %collective-permute-start.4 = (bf16[4,4,1536]{2,1,0:T(4,128)(2,1)S(1)}, bf16[4,4,1536]{2,1,0:T(4,128)(2,1)S(1)}, u32[]{:S(2)}, u32[]{:S(2)}) collective-permute-start(bf16[4,4,1536]{2,1,0:T(4,128)(2,1)S(1)} %get-tuple-element.42), channel_id=1, source_target_pairs={{0,1},{1,0},{2,3},{3,2},{4,5},{5,4},{6,7},{7,6},{8,9},{9,8},{10,11... | collective-permute-start | bytes 147464 | tf_op jit(solution)/shard_map/ppermute | solution.py:39

commit v11 on v10

--- a/solution.py
+++ b/solution.py
@@ -482,6 +482,9 @@
             pltpu.VMEM((tp - 1, 2 * rows, part), bf16),
         ],
         compiler_params=params,
+        cost_estimate=pl.CostEstimate(
+            flops=6000 * 10**6, bytes_accessed=2**20, transcendentals=2**18
+        ),
         name="attend",
     )(gain, xn, scale, new_keys, values, cosine, sine, bias, w_query, in_vmem(prompt_keys), in_vmem(gen_keys), product, squares, *far_pieces[1:])
 

time: 15.3 us -> 15.3 us (level)
  waiting for transfers between devices: 1.16 us -> 1.52 us
  local copies, waits for them, and re-layouts: 0.71 us -> 0.47 us
    unnamed x20, local copies, waits for them, and re-layouts: 0.71 us -> 0.47 us
    ppermute x4, waiting for transfers between devices: 0.93 us -> 1.13 us  [across(): return lax.ppermute(value, ('req', 'tp'), pairs)]
    ppermute x1, waiting for transfers between devices: 0.23 us -> 0.39 us  [permute_by(): return lax.ppermute(value, axis, pairs)]
  transfers between devices with their start and end apart: 5 -> 5, of which waited for: 4 -> 4; matrix products, arithmetic and copies ran while one was open for 0% -> 0% of each run, Pallas kernels for 36% -> 35%
where the time goes in v11:
time: 15.3 us; the launch traced here: 15.2 us
  Pallas kernels  7.51 us (49%)
  starting transfers between devices  4.9 us (32%)
  waiting for transfers between devices  1.52 us (10%)
  other arithmetic  0.65 us (4%)
  local copies, waits for them, and re-layouts  0.47 us (3%)
    ppermute x4, starting transfers between devices, across(): return lax.ppermute(value, ('req', 'tp'), pairs)  3.16 us
    pallas_call x1, Pallas kernels, body(): pl.pallas_call(fetch_kernel, out_shape=(jax.ShapeDtypeStruct((8, heads *...  1.9 us
    ppermute x1, starting transfers between devices, permute_by(): return lax.ppermute(value, axis, pairs)  1.73 us
    pallas_call x1, Pallas kernels, body(): pl.pallas_call(functools.partial(attend_kernel, (steps, own, tp, kv, grou...  1.55 us
    pallas_call x1, Pallas kernels, body(): pl.pallas_call(functools.partial(prepare_kernel, (steps, own, tp, group,...  1.27 us
    ppermute x4, waiting for transfers between devices, across(): return lax.ppermute(value, ('req', 'tp'), pairs)  1.13 us
    pallas_call x1, Pallas kernels, body(): pl.pallas_call(fresh_kernel, out_shape=(jax.ShapeDtypeStruct((rows, kv *...  1.02 us
    pallas_call x1, Pallas kernels, body(): pl.pallas_call(query_kernel, out_shape=(jax.ShapeDtypeStruct((2 * rows, h...  0.65 us
  transfers between devices with their start and end apart: 5, of which 4 were waited for; matrix products, arithmetic and copies ran while one was open for 0% of the time, Pallas kernels for 35%

profile of v11, /device:TPU:0, one launch (start us, length us, event | category | flops | bytes accessed | tf_op | source)
XLA Modules:
  0.0 15.2 jit_solution(11466605237940634652)
XLA Ops:
  0.0 0.5 %collective-permute-start = (bf16[4,4,1536]{2,1,0:T(4,128)(2,1)}, bf16[4,4,1536]{2,1,0:T(4,128)(2,1)S(1)}, u32[]{:S(2)}, u32[]{:S(2)}) collective-permute-start(bf16[4,4,1536]{2,1,0:T(4,128)(2,1)} %hidden.1), channel_id=1, source_target_pairs={{0,1},{1,0},{2,3},{3,2},{4,5},{5,4},{6,7},{7,6},{8,9},{9,8},{10,11... | collective-permute-start | bytes 147464 | tf_op jit(solution)/shard_map/ppermute | solution.py:39
  0.5 2.6 %collective-permute-start.1 = (bf16[4,4,1536]{2,1,0:T(4,128)(2,1)}, bf16[4,4,1536]{2,1,0:T(4,128)(2,1)S(1)}, u32[]{:S(2)}, u32[]{:S(2)}) collective-permute-start(bf16[4,4,1536]{2,1,0:T(4,128)(2,1)} %hidden.1), channel_id=1, source_target_pairs={{0,2},{1,3},{2,0},{3,1},{4,6},{5,7},{6,4},{7,5},{8,10},{9,11},{10,... | collective-permute-start | bytes 147464 | tf_op jit(solution)/shard_map/ppermute | solution.py:39
  3.1 0.1 collective-permute-start.2
  3.2 0.0 collective-permute-done.refs_0_
  3.2 1.3 %prepare.1 = (f32[1,3072]{1,0:T(1,128)S(1)}, bf16[16,3072]{1,0:T(8,128)(2,1)S(1)}, f32[16,128]{1,0:T(8,128)S(1)}, f32[16,128]{1,0:T(8,128)S(1)}, f32[16,128]{1,0...) custom-call(s32[8]{0:T(128)} %lengths.1, s32[4,64]{1,0:T(4,128)} %parents.1, ...), custom_call_target="tpu_custom_call" | custom-call | flops 2000000000 | bytes 1048576 | tf_op jit(solution)/shard_map/prepare/pallas_call | solution.py:411
  4.5 0.0 copy-done.3
  4.5 0.0 copy-done.2
  4.5 0.0 copy-start.4
  4.5 0.0 copy-start.5
  4.5 1.0 %fresh.1 = (bf16[16,512]{1,0:T(8,128)(2,1)S(1)}, bf16[512,896]{1,0:T(8,128)(2,1)S(1)}) custom-call(bf16[16,3072]{1,0:T(8,128)(2,1)S(1)} %get-tuple-element.25.xn_ref, f32[16,128]{1,0:T(8,128)S(1)} %get-tuple-element.26.scale_ref, f32[16,128]{1,0:T(8,128)S(1)} %get-tuple-element.27.key_cosine_ref, f32[16,128]{1,0:T(8,128)S(1)} %get-tuple-element.28.key_sine_ref, ...), custom_call_target="tpu_custom_call" | custom-call | tf_op jit(solution)/shard_map/fresh/pallas_call | solution.py:439
  5.6 0.1 collective-permute-done.1.piece
  5.7 0.4 %slice-done.3 = s8[2097152]{0:T(1024)(128)(4,1)S(1)} async-done(((s8[6291456]{0:T(1024)(128)(4,1)}), s8[2097152]{0:T(1024)(128)(4,1)S(1)}, s32[]{:S(2)}) %slice-start.3) | async-done | bytes 2097176
  6.1 0.7 %query.1 = (f32[32,1024]{1,0:T(8,128)S(1)}, f32[16,128]{1,0:T(8,128)S(1)}) custom-call(f32[1,3072]{1,0:T(1,128)S(1)} %get-tuple-element.24.gain_ref, bf16[16,3072]{1,0:T(8,128)(2,1)S(1)} %get-tuple-element.25.xn_ref, bf16[3072,1024]{1,0:T(8,128)(2,1)S(1)} %bitcast.4, bf16[4,4,1536]{2,1,0:T(4,128)(2,1)S(1)} %collective-permute-done.1.piece), custom_call_target="tpu_custom_call" | custom-call | tf_op jit(solution)/shard_map/query/pallas_call | solution.py:458
  6.7 0.4 %collective-permute-done.2.refs_0_ = bf16[4,4,1536]{2,1,0:T(4,128)(2,1)S(1)} collective-permute-done((bf16[4,4,1536]{2,1,0:T(4,128)(2,1)}, bf16[4,4,1536]{2,1,0:T(4,128)(2,1)S(1)}, u32[]{:S(2)}, u32[]{:S(2)}) %collective-permute-start.2) | collective-permute-done | bytes 49184 | tf_op jit(solution)/shard_map/ppermute | solution.py:39
  7.1 1.6 %attend.1 = (f32[128,128]{1,0:T(8,128)S(1)}, f32[8,128]{1,0:T(8,128)S(1)}, bf16[144,128]{1,0:T(8,128)(2,1)S(1)}) custom-call(f32[1,3072]{1,0:T(1,128)S(1)} %get-tuple-element.24.gain_ref, bf16[16,3072]{1,0:T(8,128)(2,1)S(1)} %get-tuple-element.25.xn_ref, f32[16,128]{1,0:T(8,128)S(1)} %get-tuple-element.26.scale_ref, ...), custom_call_target="tpu_custom_call" | custom-call | flops 6000000000 | bytes 1048576 | tf_op jit(solution)/shard_map/attend/pallas_call | solution.py:471
  8.7 1.7 %collective-permute-start.3 = (bf16[144,128]{1,0:T(8,128)(2,1)S(1)}, bf16[144,128]{1,0:T(8,128)(2,1)S(1)}, u32[]{:S(2)}, u32[]{:S(2)}) collective-permute-start(bf16[144,128]{1,0:T(8,128)(2,1)S(1)} %get-tuple-element.39), channel_id=1, source_target_pairs={{0,2},{2,0},{4,6},{6,4},{8,10},{10,8},{12,14},{14,12},{16,18},{18,... | collective-permute-start | bytes 110600 | tf_op jit(solution)/shard_map/ppermute | solution.py:29
  10.4 1.9 %fetch.1 = (f32[8,128]{1,0:T(8,128)S(1)}, bf16[2,1024,1536]{2,1,0:T(8,128)(2,1)S(1)}) custom-call(f32[8,128]{1,0:T(8,128)S(1)} %get-tuple-element.37.kept_lse_ref, bf16[1024,3072]{1,0:T(8,128)(2,1)} %w_out_ref.1), custom_call_target="tpu_custom_call" | custom-call | tf_op jit(solution)/shard_map/fetch/pallas_call | solution.py:492
  12.3 0.4 %collective-permute-done.3.got_ref = bf16[144,128]{1,0:T(8,128)(2,1)S(1)} collective-permute-done((bf16[144,128]{1,0:T(8,128)(2,1)S(1)}, bf16[144,128]{1,0:T(8,128)(2,1)S(1)}, u32[]{:S(2)}, u32[]{:S(2)}) %collective-permute-start.3) | collective-permute-done | bytes 36896 | tf_op jit(solution)/shard_map/ppermute | solution.py:29
  12.7 0.6 %project.1 = (bf16[16,1024]{1,0:T(8,128)(2,1)S(1)}, bf16[4,4,1536]{2,1,0:T(4,128)(2,1)S(1)}) custom-call(f32[128,128]{1,0:T(8,128)S(1)} %get-tuple-element.36.kept_ref, f32[8,128]{1,0:T(8,128)S(1)} %get-tuple-element.38.kept_lse_ref, bf16[144,128]{1,0:T(8,128)(2,1)S(1)} %collective-permute-done.3.got_ref, bf16[2,1024,1536]{2,1,0:T(8,128)(2,1)S(1)} %get-tuple-element.40.w_out_ref), custom_call_target="tpu_custom_call" | custom-call | tf_op jit(solution)/shard_map/project/pallas_call | solution.py:506
  13.3 0.0 collective-permute-start.4
  13.3 0.0 slice-done
  13.3 0.5 %project_own.1 = f32[4,4,1536]{2,1,0:T(4,128)S(1)} custom-call(bf16[16,1024]{1,0:T(8,128)(2,1)S(1)} %get-tuple-element.41.ctx_ref, bf16[1024,3072]{1,0:T(8,128)(2,1)S(1)} %bitcast.2), custom_call_target="tpu_custom_call" | custom-call | tf_op jit(solution)/shard_map/project_own/pallas_call | solution.py:518
  13.8 0.7 %collective-permute-done.4 = bf16[4,4,1536]{2,1,0:T(4,128)(2,1)S(1)} collective-permute-done((bf16[4,4,1536]{2,1,0:T(4,128)(2,1)S(1)}, bf16[4,4,1536]{2,1,0:T(4,128)(2,1)S(1)}, u32[]{:S(2)}, u32[]{:S(2)}) %collective-permute-start.4) | collective-permute-done | bytes 49184 | tf_op jit(solution)/shard_map/ppermute | solution.py:39
  14.5 0.6 %add_convert_fusion = bf16[4,4,1536]{2,1,0:T(4,128)(2,1)} fusion(f32[4,4,1536]{2,1,0:T(4,128)S(1)} %project_own.1, bf16[4,4,1536]{2,1,0:T(4,128)(2,1)S(1)} %collective-permute-done.4), kind=kLoop, calls=%fused_computation | loop fusion | flops 73728 | bytes 196608 | tf_op jit(solution)/shard_map/convert_element_type | solution.py:528
  (16 shorter events, 0.0 us)
Async XLA Ops:
  0.0 4.5 %copy-start.3 = (bf16[4,64,512]{2,1,0:T(8,128)(2,1)S(1)}, bf16[4,64,512]{2,1,0:T(8,128)(2,1)}, u32[]{:S(2)}) copy-start(bf16[4,64,512]{2,1,0:T(8,128)(2,1)} %gv_ref.1) | copy-start | bytes 786436
  0.0 4.5 %copy-start.2 = (bf16[1,512,512]{2,1,0:T(8,128)(2,1)S(1)}, bf16[1,512,512]{2,1,0:T(8,128)(2,1)}, u32[]{:S(2)}) copy-start(bf16[1,512,512]{2,1,0:T(8,128)(2,1)} %pv_ref.1) | copy-start | bytes 1572868
  0.0 4.5 %copy-start.1 = (bf16[3072,512]{1,0:T(8,128)(2,1)S(1)}, bf16[3072,512]{1,0:T(8,128)(2,1)}, u32[]{:S(2)}) copy-start(bf16[3072,512]{1,0:T(8,128)(2,1)} %wv_ref.1) | copy-start | bytes 9437188
  0.0 4.5 %copy-start = (bf16[3072,512]{1,0:T(8,128)(2,1)S(1)}, bf16[3072,512]{1,0:T(8,128)(2,1)}, u32[]{:S(2)}) copy-start(bf16[3072,512]{1,0:T(8,128)(2,1)} %wk_ref.1) | copy-start | bytes 9437188
  0.0 3.2 %collective-permute-start = (bf16[4,4,1536]{2,1,0:T(4,128)(2,1)}, bf16[4,4,1536]{2,1,0:T(4,128)(2,1)S(1)}, u32[]{:S(2)}, u32[]{:S(2)}) collective-permute-start(bf16[4,4,1536]{2,1,0:T(4,128)(2,1)} %hidden.1), channel_id=1, source_target_pairs={{0,1},{1,0},{2,3},{3,2},{4,5},{5,4},{6,7},{7,6},{8,9},{9,8},{10,11... | collective-permute-start | bytes 147464 | tf_op jit(solution)/shard_map/ppermute | solution.py:39
  0.5 5.1 %collective-permute-start.1 = (bf16[4,4,1536]{2,1,0:T(4,128)(2,1)}, bf16[4,4,1536]{2,1,0:T(4,128)(2,1)S(1)}, u32[]{:S(2)}, u32[]{:S(2)}) collective-permute-start(bf16[4,4,1536]{2,1,0:T(4,128)(2,1)} %hidden.1), channel_id=1, source_target_pairs={{0,2},{1,3},{2,0},{3,1},{4,6},{5,7},{6,4},{7,5},{8,10},{9,11},{10,... | collective-permute-start | bytes 147464 | tf_op jit(solution)/shard_map/ppermute | solution.py:39
  3.1 4.0 %collective-permute-start.2 = (bf16[4,4,1536]{2,1,0:T(4,128)(2,1)}, bf16[4,4,1536]{2,1,0:T(4,128)(2,1)S(1)}, u32[]{:S(2)}, u32[]{:S(2)}) collective-permute-start(bf16[4,4,1536]{2,1,0:T(4,128)(2,1)} %hidden.1), channel_id=1, source_target_pairs={{0,3},{1,2},{2,1},{3,0},{4,7},{5,6},{6,5},{7,4},{8,11},{9,10},{10,... | collective-permute-start | bytes 147464 | tf_op jit(solution)/shard_map/ppermute | solution.py:39
  3.2 2.5 %slice-start.2 = ((s8[6291456]{0:T(1024)(128)(4,1)}), s8[4194304]{0:T(1024)(128)(4,1)S(1)}, s32[]{:S(2)}) async-start(s8[6291456]{0:T(1024)(128)(4,1)} %bitcast.3), calls=%async_computation.2 | async-start | bytes 8388608
  3.2 2.9 %slice-start.3 = ((s8[6291456]{0:T(1024)(128)(4,1)}), s8[2097152]{0:T(1024)(128)(4,1)S(1)}, s32[]{:S(2)}) async-start(s8[6291456]{0:T(1024)(128)(4,1)} %bitcast.3), calls=%async_computation.3 | async-start | bytes 4194304
  4.5 2.6 %copy-start.4 = (bf16[1,512,512]{2,1,0:T(8,128)(2,1)S(1)}, bf16[1,512,512]{2,1,0:T(8,128)(2,1)}, u32[]{:S(2)}) copy-start(bf16[1,512,512]{2,1,0:T(8,128)(2,1)} %pk_ref.1) | copy-start | bytes 1572868
  4.5 2.6 %copy-start.5 = (bf16[4,64,512]{2,1,0:T(8,128)(2,1)S(1)}, bf16[4,64,512]{2,1,0:T(8,128)(2,1)}, u32[]{:S(2)}) copy-start(bf16[4,64,512]{2,1,0:T(8,128)(2,1)} %gk_ref.1) | copy-start | bytes 786436
  7.1 6.2 %slice-start = ((s8[6291456]{0:T(1024)(128)(4,1)}), s8[4194304]{0:T(1024)(128)(4,1)S(1)}, s32[]{:S(2)}) async-start(s8[6291456]{0:T(1024)(128)(4,1)} %bitcast.1), calls=%async_computation | async-start | bytes 8388608
  7.1 6.2 %slice-start.1 = ((s8[6291456]{0:T(1024)(128)(4,1)}), s8[2097152]{0:T(1024)(128)(4,1)S(1)}, s32[]{:S(2)}) async-start(s8[6291456]{0:T(1024)(128)(4,1)} %bitcast.1), calls=%async_computation.1 | async-start | bytes 4194304
  8.7 4.0 %collective-permute-start.3 = (bf16[144,128]{1,0:T(8,128)(2,1)S(1)}, bf16[144,128]{1,0:T(8,128)(2,1)S(1)}, u32[]{:S(2)}, u32[]{:S(2)}) collective-permute-start(bf16[144,128]{1,0:T(8,128)(2,1)S(1)} %get-tuple-element.39), channel_id=1, source_target_pairs={{0,2},{2,0},{4,6},{6,4},{8,10},{10,8},{12,14},{14,12},{16,18},{18,... | collective-permute-start | bytes 110600 | tf_op jit(solution)/shard_map/ppermute | solution.py:29
  13.3 1.2 %collective-permute-start.4 = (bf16[4,4,1536]{2,1,0:T(4,128)(2,1)S(1)}, bf16[4,4,1536]{2,1,0:T(4,128)(2,1)S(1)}, u32[]{:S(2)}, u32[]{:S(2)}) collective-permute-start(bf16[4,4,1536]{2,1,0:T(4,128)(2,1)S(1)} %get-tuple-element.42), channel_id=1, source_target_pairs={{0,1},{1,0},{2,3},{3,2},{4,5},{5,4},{6,7},{7,6},{8,9},{9,8},{10,11... | collective-permute-start | bytes 147464 | tf_op jit(solution)/shard_map/ppermute | solution.py:39

commit v12 on v10

--- a/solution.py
+++ b/solution.py
@@ -499,7 +499,7 @@
         name="fetch",
     )(kept_lse, in_hbm(w_out))
 
-    chunk = math.gcd(part, 512)
+    chunk = math.gcd(part, 1536)
     ctx, *sums = pl.pallas_call(
         functools.partial(project_kernel, (steps, own, tp, heads, chunk)),
         out_shape=(

time: 15.3 us -> 15.3 us (level)
  no operation moved by 1% of the time
where the time goes in v12:
time: 15.3 us; the launch traced here: 15.2 us
  Pallas kernels  7.65 us (50%)
  starting transfers between devices  4.9 us (32%)
  waiting for transfers between devices  1.16 us (8%)
  local copies, waits for them, and re-layouts  0.71 us (5%)
  other arithmetic  0.65 us (4%)
    ppermute x4, starting transfers between devices, across(): return lax.ppermute(value, ('req', 'tp'), pairs)  3.16 us
    pallas_call x1, Pallas kernels, body(): pl.pallas_call(fetch_kernel, out_shape=(jax.ShapeDtypeStruct((8, heads *...  2.05 us
    ppermute x1, starting transfers between devices, permute_by(): return lax.ppermute(value, axis, pairs)  1.74 us
    pallas_call x1, Pallas kernels, body(): pl.pallas_call(functools.partial(attend_kernel, (steps, own, tp, kv, grou...  1.55 us
    pallas_call x1, Pallas kernels, body(): pl.pallas_call(functools.partial(prepare_kernel, (steps, own, tp, group,...  1.27 us
    pallas_call x1, Pallas kernels, body(): pl.pallas_call(fresh_kernel, out_shape=(jax.ShapeDtypeStruct((rows, kv *...  1.01 us
    ppermute x4, waiting for transfers between devices, across(): return lax.ppermute(value, ('req', 'tp'), pairs)  0.93 us
    unnamed x20, local copies, waits for them, and re-layouts  0.71 us
  transfers between devices with their start and end apart: 5, of which 4 were waited for; matrix products, arithmetic and copies ran while one was open for 0% of the time, Pallas kernels for 36%

profile of v12, /device:TPU:0, one launch (start us, length us, event | category | flops | bytes accessed | tf_op | source)
XLA Modules:
  0.0 15.2 jit_solution(944490051439965194)
XLA Ops:
  0.0 0.5 %collective-permute-start = (bf16[4,4,1536]{2,1,0:T(4,128)(2,1)}, bf16[4,4,1536]{2,1,0:T(4,128)(2,1)S(1)}, u32[]{:S(2)}, u32[]{:S(2)}) collective-permute-start(bf16[4,4,1536]{2,1,0:T(4,128)(2,1)} %hidden.1), channel_id=1, source_target_pairs={{0,1},{1,0},{2,3},{3,2},{4,5},{5,4},{6,7},{7,6},{8,9},{9,8},{10,11... | collective-permute-start | bytes 147464 | tf_op jit(solution)/shard_map/ppermute | solution.py:39
  0.5 2.6 %collective-permute-start.1 = (bf16[4,4,1536]{2,1,0:T(4,128)(2,1)}, bf16[4,4,1536]{2,1,0:T(4,128)(2,1)S(1)}, u32[]{:S(2)}, u32[]{:S(2)}) collective-permute-start(bf16[4,4,1536]{2,1,0:T(4,128)(2,1)} %hidden.1), channel_id=1, source_target_pairs={{0,2},{1,3},{2,0},{3,1},{4,6},{5,7},{6,4},{7,5},{8,10},{9,11},{10,... | collective-permute-start | bytes 147464 | tf_op jit(solution)/shard_map/ppermute | solution.py:39
  3.1 0.1 collective-permute-start.2
  3.2 0.0 collective-permute-done.refs_0_
  3.2 1.3 %prepare.1 = (f32[1,3072]{1,0:T(1,128)S(1)}, bf16[16,3072]{1,0:T(8,128)(2,1)S(1)}, f32[16,128]{1,0:T(8,128)S(1)}, f32[16,128]{1,0:T(8,128)S(1)}, f32[16,128]{1,0...) custom-call(s32[8]{0:T(128)} %lengths.1, s32[4,64]{1,0:T(4,128)} %parents.1, ...), custom_call_target="tpu_custom_call" | custom-call | flops 2000000000 | bytes 1048576 | tf_op jit(solution)/shard_map/prepare/pallas_call | solution.py:411
  4.5 0.0 copy-done.4
  4.5 0.0 copy-start.3
  4.5 0.0 copy-start.5
  4.5 1.0 %fresh.1 = (bf16[16,512]{1,0:T(8,128)(2,1)S(1)}, bf16[512,896]{1,0:T(8,128)(2,1)S(1)}) custom-call(bf16[16,3072]{1,0:T(8,128)(2,1)S(1)} %get-tuple-element.25.xn_ref, f32[16,128]{1,0:T(8,128)S(1)} %get-tuple-element.26.scale_ref, f32[16,128]{1,0:T(8,128)S(1)} %get-tuple-element.27.key_cosine_ref, f32[16,128]{1,0:T(8,128)S(1)} %get-tuple-element.28.key_sine_ref, ...), custom_call_target="tpu_custom_call" | custom-call | tf_op jit(solution)/shard_map/fresh/pallas_call | solution.py:439
  5.5 0.1 collective-permute-done.1.piece
  5.7 0.4 %slice-done.3 = s8[2097152]{0:T(1024)(128)(4,1)S(1)} async-done(((s8[6291456]{0:T(1024)(128)(4,1)}), s8[2097152]{0:T(1024)(128)(4,1)S(1)}, s32[]{:S(2)}) %slice-start.3) | async-done | bytes 2097176
  6.1 0.7 %query.1 = (f32[32,1024]{1,0:T(8,128)S(1)}, f32[16,128]{1,0:T(8,128)S(1)}) custom-call(f32[1,3072]{1,0:T(1,128)S(1)} %get-tuple-element.24.gain_ref, bf16[16,3072]{1,0:T(8,128)(2,1)S(1)} %get-tuple-element.25.xn_ref, bf16[3072,1024]{1,0:T(8,128)(2,1)S(1)} %bitcast.4, bf16[4,4,1536]{2,1,0:T(4,128)(2,1)S(1)} %collective-permute-done.1.piece), custom_call_target="tpu_custom_call" | custom-call | tf_op jit(solution)/shard_map/query/pallas_call | solution.py:458
  6.7 0.4 %collective-permute-done.2.refs_0_ = bf16[4,4,1536]{2,1,0:T(4,128)(2,1)S(1)} collective-permute-done((bf16[4,4,1536]{2,1,0:T(4,128)(2,1)}, bf16[4,4,1536]{2,1,0:T(4,128)(2,1)S(1)}, u32[]{:S(2)}, u32[]{:S(2)}) %collective-permute-start.2) | collective-permute-done | bytes 49184 | tf_op jit(solution)/shard_map/ppermute | solution.py:39
  7.1 1.6 %attend.1 = (f32[128,128]{1,0:T(8,128)S(1)}, f32[8,128]{1,0:T(8,128)S(1)}, bf16[144,128]{1,0:T(8,128)(2,1)S(1)}) custom-call(f32[1,3072]{1,0:T(1,128)S(1)} %get-tuple-element.24.gain_ref, bf16[16,3072]{1,0:T(8,128)(2,1)S(1)} %get-tuple-element.25.xn_ref, f32[16,128]{1,0:T(8,128)S(1)} %get-tuple-element.26.scale_ref, ...), custom_call_target="tpu_custom_call" | custom-call | tf_op jit(solution)/shard_map/attend/pallas_call | solution.py:471
  8.7 1.7 %collective-permute-start.3 = (bf16[144,128]{1,0:T(8,128)(2,1)S(1)}, bf16[144,128]{1,0:T(8,128)(2,1)S(1)}, u32[]{:S(2)}, u32[]{:S(2)}) collective-permute-start(bf16[144,128]{1,0:T(8,128)(2,1)S(1)} %get-tuple-element.39), channel_id=1, source_target_pairs={{0,2},{2,0},{4,6},{6,4},{8,10},{10,8},{12,14},{14,12},{16,18},{18,... | collective-permute-start | bytes 110600 | tf_op jit(solution)/shard_map/ppermute | solution.py:29
  10.4 2.0 %fetch.1 = (f32[8,128]{1,0:T(8,128)S(1)}, bf16[2,1024,1536]{2,1,0:T(8,128)(2,1)S(1)}) custom-call(f32[8,128]{1,0:T(8,128)S(1)} %get-tuple-element.37.kept_lse_ref, bf16[1024,3072]{1,0:T(8,128)(2,1)} %w_out_ref.1), custom_call_target="tpu_custom_call" | custom-call | tf_op jit(solution)/shard_map/fetch/pallas_call | solution.py:489
  12.5 0.2 %collective-permute-done.3.got_ref = bf16[144,128]{1,0:T(8,128)(2,1)S(1)} collective-permute-done((bf16[144,128]{1,0:T(8,128)(2,1)S(1)}, bf16[144,128]{1,0:T(8,128)(2,1)S(1)}, u32[]{:S(2)}, u32[]{:S(2)}) %collective-permute-start.3) | collective-permute-done | bytes 36896 | tf_op jit(solution)/shard_map/ppermute | solution.py:29
  12.7 0.6 %project.1 = (bf16[16,1024]{1,0:T(8,128)(2,1)S(1)}, bf16[4,4,1536]{2,1,0:T(4,128)(2,1)S(1)}) custom-call(f32[128,128]{1,0:T(8,128)S(1)} %get-tuple-element.36.kept_ref, f32[8,128]{1,0:T(8,128)S(1)} %get-tuple-element.38.kept_lse_ref, bf16[144,128]{1,0:T(8,128)(2,1)S(1)} %collective-permute-done.3.got_ref, bf16[2,1024,1536]{2,1,0:T(8,128)(2,1)S(1)} %get-tuple-element.40.w_out_ref), custom_call_target="tpu_custom_call" | custom-call | tf_op jit(solution)/shard_map/project/pallas_call | solution.py:503
  13.3 0.0 collective-permute-start.4
  13.3 0.0 slice-done
  13.3 0.2 %slice-done.1 = s8[4194304]{0:T(1024)(128)(4,1)S(1)} async-done(((s8[6291456]{0:T(1024)(128)(4,1)}), s8[4194304]{0:T(1024)(128)(4,1)S(1)}, s32[]{:S(2)}) %slice-start.1) | async-done | bytes 4194328
  13.5 0.5 %project_own.1 = f32[4,4,1536]{2,1,0:T(4,128)S(1)} custom-call(bf16[16,1024]{1,0:T(8,128)(2,1)S(1)} %get-tuple-element.41.ctx_ref, bf16[1024,3072]{1,0:T(8,128)(2,1)S(1)} %bitcast.2), custom_call_target="tpu_custom_call" | custom-call | tf_op jit(solution)/shard_map/project_own/pallas_call | solution.py:515
  14.1 0.5 %collective-permute-done.4 = bf16[4,4,1536]{2,1,0:T(4,128)(2,1)S(1)} collective-permute-done((bf16[4,4,1536]{2,1,0:T(4,128)(2,1)S(1)}, bf16[4,4,1536]{2,1,0:T(4,128)(2,1)S(1)}, u32[]{:S(2)}, u32[]{:S(2)}) %collective-permute-start.4) | collective-permute-done | bytes 49184 | tf_op jit(solution)/shard_map/ppermute | solution.py:39
  14.5 0.6 %add_convert_fusion = bf16[4,4,1536]{2,1,0:T(4,128)(2,1)} fusion(f32[4,4,1536]{2,1,0:T(4,128)S(1)} %project_own.1, bf16[4,4,1536]{2,1,0:T(4,128)(2,1)S(1)} %collective-permute-done.4), kind=kLoop, calls=%fused_computation | loop fusion | flops 73728 | bytes 196608 | tf_op jit(solution)/shard_map/convert_element_type | solution.py:525
  (16 shorter events, 0.0 us)
Async XLA Ops:
  0.0 4.5 %copy-start.4 = (bf16[4,64,512]{2,1,0:T(8,128)(2,1)S(1)}, bf16[4,64,512]{2,1,0:T(8,128)(2,1)}, u32[]{:S(2)}) copy-start(bf16[4,64,512]{2,1,0:T(8,128)(2,1)} %gv_ref.1) | copy-start | bytes 786436
  0.0 4.5 %copy-start.2 = (bf16[1,512,512]{2,1,0:T(8,128)(2,1)S(1)}, bf16[1,512,512]{2,1,0:T(8,128)(2,1)}, u32[]{:S(2)}) copy-start(bf16[1,512,512]{2,1,0:T(8,128)(2,1)} %pv_ref.1) | copy-start | bytes 1572868
  0.0 4.5 %copy-start.1 = (bf16[3072,512]{1,0:T(8,128)(2,1)S(1)}, bf16[3072,512]{1,0:T(8,128)(2,1)}, u32[]{:S(2)}) copy-start(bf16[3072,512]{1,0:T(8,128)(2,1)} %wv_ref.1) | copy-start | bytes 9437188
  0.0 4.5 %copy-start = (bf16[3072,512]{1,0:T(8,128)(2,1)S(1)}, bf16[3072,512]{1,0:T(8,128)(2,1)}, u32[]{:S(2)}) copy-start(bf16[3072,512]{1,0:T(8,128)(2,1)} %wk_ref.1) | copy-start | bytes 9437188
  0.0 3.2 %collective-permute-start = (bf16[4,4,1536]{2,1,0:T(4,128)(2,1)}, bf16[4,4,1536]{2,1,0:T(4,128)(2,1)S(1)}, u32[]{:S(2)}, u32[]{:S(2)}) collective-permute-start(bf16[4,4,1536]{2,1,0:T(4,128)(2,1)} %hidden.1), channel_id=1, source_target_pairs={{0,1},{1,0},{2,3},{3,2},{4,5},{5,4},{6,7},{7,6},{8,9},{9,8},{10,11... | collective-permute-start | bytes 147464 | tf_op jit(solution)/shard_map/ppermute | solution.py:39
  0.5 5.1 %collective-permute-start.1 = (bf16[4,4,1536]{2,1,0:T(4,128)(2,1)}, bf16[4,4,1536]{2,1,0:T(4,128)(2,1)S(1)}, u32[]{:S(2)}, u32[]{:S(2)}) collective-permute-start(bf16[4,4,1536]{2,1,0:T(4,128)(2,1)} %hidden.1), channel_id=1, source_target_pairs={{0,2},{1,3},{2,0},{3,1},{4,6},{5,7},{6,4},{7,5},{8,10},{9,11},{10,... | collective-permute-start | bytes 147464 | tf_op jit(solution)/shard_map/ppermute | solution.py:39
  3.1 4.0 %collective-permute-start.2 = (bf16[4,4,1536]{2,1,0:T(4,128)(2,1)}, bf16[4,4,1536]{2,1,0:T(4,128)(2,1)S(1)}, u32[]{:S(2)}, u32[]{:S(2)}) collective-permute-start(bf16[4,4,1536]{2,1,0:T(4,128)(2,1)} %hidden.1), channel_id=1, source_target_pairs={{0,3},{1,2},{2,1},{3,0},{4,7},{5,6},{6,5},{7,4},{8,11},{9,10},{10,... | collective-permute-start | bytes 147464 | tf_op jit(solution)/shard_map/ppermute | solution.py:39
  3.2 2.5 %slice-start.2 = ((s8[6291456]{0:T(1024)(128)(4,1)}), s8[4194304]{0:T(1024)(128)(4,1)S(1)}, s32[]{:S(2)}) async-start(s8[6291456]{0:T(1024)(128)(4,1)} %bitcast.3), calls=%async_computation.2 | async-start | bytes 8388608
  3.2 2.9 %slice-start.3 = ((s8[6291456]{0:T(1024)(128)(4,1)}), s8[2097152]{0:T(1024)(128)(4,1)S(1)}, s32[]{:S(2)}) async-start(s8[6291456]{0:T(1024)(128)(4,1)} %bitcast.3), calls=%async_computation.3 | async-start | bytes 4194304
  4.5 2.6 %copy-start.3 = (bf16[1,512,512]{2,1,0:T(8,128)(2,1)S(1)}, bf16[1,512,512]{2,1,0:T(8,128)(2,1)}, u32[]{:S(2)}) copy-start(bf16[1,512,512]{2,1,0:T(8,128)(2,1)} %pk_ref.1) | copy-start | bytes 1572868
  4.5 2.6 %copy-start.5 = (bf16[4,64,512]{2,1,0:T(8,128)(2,1)S(1)}, bf16[4,64,512]{2,1,0:T(8,128)(2,1)}, u32[]{:S(2)}) copy-start(bf16[4,64,512]{2,1,0:T(8,128)(2,1)} %gk_ref.1) | copy-start | bytes 786436
  7.1 6.2 %slice-start = ((s8[6291456]{0:T(1024)(128)(4,1)}), s8[2097152]{0:T(1024)(128)(4,1)S(1)}, s32[]{:S(2)}) async-start(s8[6291456]{0:T(1024)(128)(4,1)} %bitcast.1), calls=%async_computation | async-start | bytes 4194304
  8.7 4.0 %collective-permute-start.3 = (bf16[144,128]{1,0:T(8,128)(2,1)S(1)}, bf16[144,128]{1,0:T(8,128)(2,1)S(1)}, u32[]{:S(2)}, u32[]{:S(2)}) collective-permute-start(bf16[144,128]{1,0:T(8,128)(2,1)S(1)} %get-tuple-element.39), channel_id=1, source_target_pairs={{0,2},{2,0},{4,6},{6,4},{8,10},{10,8},{12,14},{14,12},{16,18},{18,... | collective-permute-start | bytes 110600 | tf_op jit(solution)/shard_map/ppermute | solution.py:29
  10.4 3.1 %slice-start.1 = ((s8[6291456]{0:T(1024)(128)(4,1)}), s8[4194304]{0:T(1024)(128)(4,1)S(1)}, s32[]{:S(2)}) async-start(s8[6291456]{0:T(1024)(128)(4,1)} %bitcast.1), calls=%async_computation.1 | async-start | bytes 8388608
  13.3 1.2 %collective-permute-start.4 = (bf16[4,4,1536]{2,1,0:T(4,128)(2,1)S(1)}, bf16[4,4,1536]{2,1,0:T(4,128)(2,1)S(1)}, u32[]{:S(2)}, u32[]{:S(2)}) collective-permute-start(bf16[4,4,1536]{2,1,0:T(4,128)(2,1)S(1)} %get-tuple-element.42), channel_id=1, source_target_pairs={{0,1},{1,0},{2,3},{3,2},{4,5},{5,4},{6,7},{7,6},{8,9},{9,8},{10,11... | collective-permute-start | bytes 147464 | tf_op jit(solution)/shard_map/ppermute | solution.py:39
